TPU v7x, 128 devices: a whole 4x4x4 slice. The times are simulated.
128 devices in a mesh: owner: 64 (over y, x, z), split: 2 (over core).
Axes of the slice: x: 4, y: 4, z: 4, core: 2. Of those that a mesh axis runs over, the one named last changes fastest.
Arguments:
- embeddings: bfloat16 [65536, 1024], P(('owner', 'split')), may hold values from -6 to 6
- cluster: int32 [65536, 1], P(('owner', 'split')), may hold values from 0 to 63; in each aligned block of 512 rows (0 to 511, 512 to 1023, ...) at most 32 rows name the same one
- order: int32 [65536], P(('owner', 'split')), may hold values from 0 to 65535, each once
Outputs:
- best: float32 [65536], P(('owner', 'split'))
Inputs may be any that keep to these rules, and one draw needn't show every extreme that they name: Among the 512 rows of one device (aligned blocks of rows) no cluster id appears more than 32 times, and in some blocks one appears exactly 32 times; every cluster has rows. `order`: each number appears once.
All inputs are finite; a program needn't handle non-finite values.
Results may differ from a plain program's by a relative error of at most 0.0014.
Values may be sent and summed in bfloat16 or wider, within the bound.
No kernel may reach another device: no remote copies, remote signals or barrier semaphores. Data moves between devices by JAX's collectives and lax.ppermute only.
A program may use at most 64 MiB of HBM per device.

v0:
```python
import jax
import jax.numpy as jnp
from jax import lax
from jax.sharding import PartitionSpec as P

empty_order = 2**30


def fold_keys(queries, query_order, carry, keys, key_order):
    count = keys.shape[0]
    width = 512
    key_blocks = keys.reshape(count // width, width, keys.shape[1])
    order_blocks = key_order.reshape(count // width, width)

    def step(running, block):
        block_keys, block_order = block
        sims = lax.dot_general(
            queries, block_keys, (((1,), (1,)), ((), ())), preferred_element_type=jnp.float32
        )
        valid = block_order[None, :] < query_order[:, None]
        return (
            jnp.maximum(running, jnp.max(jnp.where(valid, sims, jnp.float32(-1.0)), axis=1)),
            None,
        )

    result, unused = lax.scan(step, carry, (key_blocks, order_blocks))
    return result


def shards(embeddings, cluster, order):
    owners = lax.axis_size("owner")
    rows = embeddings.shape[0]
    width = embeddings.shape[1]
    slots = 4 * rows // owners
    e = embeddings.astype(jnp.float32)
    unit = (e * lax.rsqrt(jnp.sum(e * e, axis=1, keepdims=True) + 1e-06)).astype(jnp.bfloat16)
    cid = cluster[:, 0]
    onehot = (cid[:, None] == jnp.arange(owners, dtype=jnp.int32)[None, :]).astype(jnp.int32)
    position = jnp.sum(jnp.cumsum(onehot, axis=0) * onehot, axis=1) - 1
    target = cid * slots + position
    packed = jnp.zeros((owners * slots, width), jnp.bfloat16).at[target].set(unit)
    packed_order = jnp.full((owners * slots,), empty_order, jnp.int32).at[target].set(order)
    packed = packed.reshape(owners, slots, width)
    packed_order = packed_order.reshape(owners, slots)
    start_best = jnp.full((owners * slots,), -1.0, jnp.float32)
    received, received_order = (
        lax.all_to_all(packed, "owner", split_axis=0, concat_axis=0, tiled=True),
        lax.all_to_all(packed_order, "owner", split_axis=0, concat_axis=0, tiled=True),
    )
    queries = received.reshape(owners * slots, width)
    query_order = received_order.reshape(owners * slots)
    best_slots = fold_keys(
        queries,
        query_order,
        start_best,
        lax.all_gather(queries, "split", axis=0, tiled=True),
        lax.all_gather(query_order, "split", axis=0, tiled=True),
    )
    returned = lax.all_to_all(
        best_slots.reshape(owners, slots), "owner", split_axis=0, concat_axis=0, tiled=True
    )
    return returned.reshape(owners * slots)[target]


def solution(mesh):
    return jax.shard_map(
        shards,
        mesh=mesh,
        in_specs=(P(("owner", "split"), None), P(("owner", "split"), None), P(("owner", "split"))),
        out_specs=P(("owner", "split")),
        check_vma=False,
    )
```

profile of v0, /device:TPU:1, one launch (start us, length us, event | category | flops | bytes accessed | tf_op | source)
XLA Modules:
  0.0 173.1 jit_solution(423956939194567585)
XLA Ops:
  6.5 0.0 all-gather.2.cloned.1.call-start
  6.5 0.7 fusion.12
  7.2 1.2 reduce-window.6
  8.4 0.2 slice_reduce_fusion
  8.7 0.8 fusion.11
  9.5 0.7 compare_select_fusion
  10.2 1.5 fusion.4
  11.7 5.9 %scatter_custom_fusion.1 = bf16[2048,1024]{1,0:T(8,128)(2,1)} fusion(s32[512]{0:T(512)S(1)} %bitcast.54, bf16[]{:T(256)} %constant.10.clone.1, bf16[512,1024]{1,0:T(8,128)(2,1)} %param.5, f32[512]{0:T(512)S(1)} %add_rsqrt_fusion), kind=kCustom, calls=%fused_computation.14 | custom fusion | flops 1572864 | bytes 5244930 | tf_op jit(solution)/shard_map/scatter | solution.py:41
  17.7 62.2 %all_to_all.26 = bf16[64,32,1024]{2,1,0:T(8,128)(2,1)} all-to-all(bf16[64,32,1024]{2,1,0:T(8,128)(2,1)} %bitcast.46), channel_id=1, replica_groups=mesh['owner'=64,'split'=2] {'owner'}, dimensions={0} | all-to-all | bytes 8388608 | tf_op jit(solution)/shard_map/all_to_all | solution.py:47
  79.9 0.0 all-gather.2.cloned.1.call-update
  79.9 2.6 %scatter_custom_fusion = s32[2048]{0:T(1024)S(1)} fusion(s32[512]{0:T(512)S(1)} %bitcast.55, s32[512]{0:T(512)} %param.7, s32[]{:T(128)} %constant.36.clone.1), kind=kCustom, calls=%fused_computation.27 | custom fusion | bytes 8704 | tf_op jit(solution)/shard_map/scatter | solution.py:42
  82.6 0.7 all_to_all.17
  83.2 5.9 %all-to-all-start = ((s32[64,1,32]{2,1,0:T(1,128)}), s32[64,1,32]{2,1,0:T(1,128)S(1)}, u32[]{:S(2)}, u32[]{:S(2)}) async-start(s32[64,1,32]{2,1,0:T(1,128)} %bitcast.5), calls=%async_computation | async-start | bytes 65536 | tf_op jit(solution)/shard_map/all_to_all | solution.py:48
  89.2 8.4 %all-to-all-done = s32[64,1,32]{2,1,0:T(1,128)S(1)} async-done(((s32[64,1,32]{2,1,0:T(1,128)}), s32[64,1,32]{2,1,0:T(1,128)S(1)}, u32[]{:S(2)}, u32[]{:S(2)}) %all-to-all-start) | async-done | bytes 8224 | tf_op jit(solution)/shard_map/all_to_all | solution.py:48
  97.6 0.0 copy-start
  97.6 0.1 lt.37
  97.6 0.6 broadcast.67
  98.2 0.7 reduce.8
  98.9 0.1 reshape.61
  99.0 5.1 %all_gather.6 = s32[4096]{0:T(1024)S(1)} all-gather(s32[2048]{0:T(1024)S(1)} %reshape.61), channel_id=1, replica_groups=mesh['owner'=64,'split'=2] {'split'}, dimensions={0}, use_global_device_ids=true | all-gather | bytes 24576 | tf_op jit(solution)/shard_map/all_gather | solution.py:57
  104.1 0.0 all-gather.2.cloned.1.call-done
  104.1 0.0 copy-done
  104.1 39.6 %while.12 = (s32[]{:T(128)}, f32[2048]{0:T(1024)S(1)}, s32[8,512]{1,0:T(8,128)S(1)}, s32[64,32]{1,0:T(8,128)}, bf16[8,512,1024]{2,1,0:T(8,128)(2,1)}, /*index=5*...) while((s32[]{:T(128)}, f32[2048]{0:T(1024)S(1)}, ...), condition=%wide.wide.region_8.9_spmd.clone, body=%wide.wide.region_6.8_spmd.clone.sunk | while | flops 2150631424 | bytes 5290603 | solution.py:26
  104.2 4.9 %fusion.24 = f32[2048]{0:T(1024)S(1)} fusion(bf16[2048,1024]{1,0:T(8,128)(2,1)} %get-tuple-element.161, s32[2048]{0:T(1024)S(1)} %get-tuple-element.162, s32[512]{0:T(512)S(1)} %bitcast.51, bf16[8,512,1024]{2,1,0:T(8,128)(2,1)} %get-tuple-element.160, s32[]{:T(128)} %get-tuple-element.147), kind=kOutput, calls=%fused_computation.4.clone.clone.1 | convolution fusion | flops 2150627328 | bytes 5261824 | tf_op jit(solution)/shard_map/while/body/eval_jaxpr/dot_general | solution.py:17
  109.1 4.9 %fusion.24 = f32[2048]{0:T(1024)S(1)} fusion(bf16[2048,1024]{1,0:T(8,128)(2,1)} %get-tuple-element.161, s32[2048]{0:T(1024)S(1)} %get-tuple-element.162, s32[512]{0:T(512)S(1)} %bitcast.51, bf16[8,512,1024]{2,1,0:T(8,128)(2,1)} %get-tuple-element.160, s32[]{:T(128)} %get-tuple-element.147), kind=kOutput, calls=%fused_computation.4.clone.clone.1 | convolution fusion | flops 2150627328 | bytes 5261824 | tf_op jit(solution)/shard_map/while/body/eval_jaxpr/dot_general | solution.py:17
  114.1 4.9 %fusion.24 = f32[2048]{0:T(1024)S(1)} fusion(bf16[2048,1024]{1,0:T(8,128)(2,1)} %get-tuple-element.161, s32[2048]{0:T(1024)S(1)} %get-tuple-element.162, s32[512]{0:T(512)S(1)} %bitcast.51, bf16[8,512,1024]{2,1,0:T(8,128)(2,1)} %get-tuple-element.160, s32[]{:T(128)} %get-tuple-element.147), kind=kOutput, calls=%fused_computation.4.clone.clone.1 | convolution fusion | flops 2150627328 | bytes 5261824 | tf_op jit(solution)/shard_map/while/body/eval_jaxpr/dot_general | solution.py:17
  119.0 4.9 %fusion.24 = f32[2048]{0:T(1024)S(1)} fusion(bf16[2048,1024]{1,0:T(8,128)(2,1)} %get-tuple-element.161, s32[2048]{0:T(1024)S(1)} %get-tuple-element.162, s32[512]{0:T(512)S(1)} %bitcast.51, bf16[8,512,1024]{2,1,0:T(8,128)(2,1)} %get-tuple-element.160, s32[]{:T(128)} %get-tuple-element.147), kind=kOutput, calls=%fused_computation.4.clone.clone.1 | convolution fusion | flops 2150627328 | bytes 5261824 | tf_op jit(solution)/shard_map/while/body/eval_jaxpr/dot_general | solution.py:17
  124.0 4.9 %fusion.24 = f32[2048]{0:T(1024)S(1)} fusion(bf16[2048,1024]{1,0:T(8,128)(2,1)} %get-tuple-element.161, s32[2048]{0:T(1024)S(1)} %get-tuple-element.162, s32[512]{0:T(512)S(1)} %bitcast.51, bf16[8,512,1024]{2,1,0:T(8,128)(2,1)} %get-tuple-element.160, s32[]{:T(128)} %get-tuple-element.147), kind=kOutput, calls=%fused_computation.4.clone.clone.1 | convolution fusion | flops 2150627328 | bytes 5261824 | tf_op jit(solution)/shard_map/while/body/eval_jaxpr/dot_general | solution.py:17
  128.9 4.9 %fusion.24 = f32[2048]{0:T(1024)S(1)} fusion(bf16[2048,1024]{1,0:T(8,128)(2,1)} %get-tuple-element.161, s32[2048]{0:T(1024)S(1)} %get-tuple-element.162, s32[512]{0:T(512)S(1)} %bitcast.51, bf16[8,512,1024]{2,1,0:T(8,128)(2,1)} %get-tuple-element.160, s32[]{:T(128)} %get-tuple-element.147), kind=kOutput, calls=%fused_computation.4.clone.clone.1 | convolution fusion | flops 2150627328 | bytes 5261824 | tf_op jit(solution)/shard_map/while/body/eval_jaxpr/dot_general | solution.py:17
  133.9 4.9 %fusion.24 = f32[2048]{0:T(1024)S(1)} fusion(bf16[2048,1024]{1,0:T(8,128)(2,1)} %get-tuple-element.161, s32[2048]{0:T(1024)S(1)} %get-tuple-element.162, s32[512]{0:T(512)S(1)} %bitcast.51, bf16[8,512,1024]{2,1,0:T(8,128)(2,1)} %get-tuple-element.160, s32[]{:T(128)} %get-tuple-element.147), kind=kOutput, calls=%fused_computation.4.clone.clone.1 | convolution fusion | flops 2150627328 | bytes 5261824 | tf_op jit(solution)/shard_map/while/body/eval_jaxpr/dot_general | solution.py:17
  138.8 4.9 %fusion.24 = f32[2048]{0:T(1024)S(1)} fusion(bf16[2048,1024]{1,0:T(8,128)(2,1)} %get-tuple-element.161, s32[2048]{0:T(1024)S(1)} %get-tuple-element.162, s32[512]{0:T(512)S(1)} %bitcast.51, bf16[8,512,1024]{2,1,0:T(8,128)(2,1)} %get-tuple-element.160, s32[]{:T(128)} %get-tuple-element.147), kind=kOutput, calls=%fused_computation.4.clone.clone.1 | convolution fusion | flops 2150627328 | bytes 5261824 | tf_op jit(solution)/shard_map/while/body/eval_jaxpr/dot_general | solution.py:17
  143.8 0.7 all_to_all.21
  144.4 7.8 %all-to-all-start.2 = ((f32[64,1,32]{2,1,0:T(1,128)}), f32[64,1,32]{2,1,0:T(1,128)S(1)}, u32[]{:S(2)}, u32[]{:S(2)}) async-start(f32[64,1,32]{2,1,0:T(1,128)} %bitcast.10), calls=%async_computation.2 | async-start | bytes 65536 | tf_op jit(solution)/shard_map/all_to_all | solution.py:59
  152.3 8.4 %all-to-all-done.2 = f32[64,1,32]{2,1,0:T(1,128)S(1)} async-done(((f32[64,1,32]{2,1,0:T(1,128)}), f32[64,1,32]{2,1,0:T(1,128)S(1)}, u32[]{:S(2)}, u32[]{:S(2)}) %all-to-all-start.2) | async-done | bytes 8224 | tf_op jit(solution)/shard_map/all_to_all | solution.py:59
  160.6 0.5 broadcast.68
  161.2 0.7 reduce.9
  161.9 0.1 reshape.66
  162.0 4.3 %gather_fusion = f32[512]{0:T(512)} fusion(f32[2048]{0:T(1024)S(1)} %reshape.66, s32[1024]{0:T(1024)S(1)} %pad_clamp_fusion), kind=kCustom, calls=%fused_computation | custom fusion | bytes 6144 | tf_op jit(solution)/shard_map/gather | solution.py:62
  (23 shorter events, 0.2 us)
Async XLA Ops:
  6.5 97.6 %all-gather.2.cloned.1.call-start = ((), (), s32[]{:S(2)}) async-start(), calls=%async_computation.3 | async-start | bytes 12582912 | tf_op jit(solution)/shard_map/all_gather | solution.py:56
  83.2 14.3 %all-to-all-start = ((s32[64,1,32]{2,1,0:T(1,128)}), s32[64,1,32]{2,1,0:T(1,128)S(1)}, u32[]{:S(2)}, u32[]{:S(2)}) async-start(s32[64,1,32]{2,1,0:T(1,128)} %bitcast.5), calls=%async_computation | async-start | bytes 65536 | tf_op jit(solution)/shard_map/all_to_all | solution.py:48
  97.6 6.6 %copy-start = (s32[64,1,32]{2,1,0:T(1,128)}, s32[64,1,32]{2,1,0:T(1,128)S(1)}, u32[]{:S(2)}) copy-start(s32[64,1,32]{2,1,0:T(1,128)S(1)} %all-to-all-done) | copy-start | bytes 24580
  144.4 16.2 %all-to-all-start.2 = ((f32[64,1,32]{2,1,0:T(1,128)}), f32[64,1,32]{2,1,0:T(1,128)S(1)}, u32[]{:S(2)}, u32[]{:S(2)}) async-start(f32[64,1,32]{2,1,0:T(1,128)} %bitcast.10), calls=%async_computation.2 | async-start | bytes 65536 | tf_op jit(solution)/shard_map/all_to_all | solution.py:59
Sparse Core Ops, SparseCore 0:
  80.1 21.7 all-gather.1
where the time goes:
time: 174 us; the launch traced here: 173 us
  blocking collectives  67.4 us (39%)
  matrix products  39.2 us (23%)
  waiting for transfers between devices  16.8 us (10%)
  starting transfers between devices  13.7 us (8%)
  between operations  13.5 us (8%)
  other arithmetic  12.4 us (7%)
  local copies, waits for them, and re-layouts  9.83 us (6%)
    all_to_all x1, blocking collectives, shards(): lax.all_to_all(packed, 'owner', split_axis=0, concat_axis=0, tiled=True)  62.2 us
    dot_general x8, matrix products, step(): lax.dot_general(queries, block_keys, (((1,), (1,)), ((), ())), preferred_...  39.2 us
    all_to_all x1, waiting for transfers between devices, shards(): lax.all_to_all(packed_order, 'owner', split_axis=0, concat_axis=0, tiled=...  8.39 us
    all_to_all x1, waiting for transfers between devices, shards(): lax.all_to_all(best_slots.reshape(owners, slots), 'owner', split_axis=0,...  8.39 us
    all_to_all x1, starting transfers between devices, shards(): lax.all_to_all(best_slots.reshape(owners, slots), 'owner', split_axis=0,...  7.79 us
    scatter x1, other arithmetic, shards(): jnp.zeros((owners * slots, width), jnp.bfloat16).at[target].set(unit)  5.94 us
    all_to_all x1, starting transfers between devices, shards(): lax.all_to_all(packed_order, 'owner', split_axis=0, concat_axis=0, tiled=...  5.92 us
    all_gather x1, blocking collectives, shards(): lax.all_gather(query_order, 'split', axis=0, tiled=True)  5.15 us
  transfers between devices with their start and end apart: 3, of which 2 were waited for; matrix products, arithmetic and copies ran while one was open for 2% of the time, Pallas kernels for 0%

commit v1 on v0

v1 whole, which is shorter than its diff:
```python
import functools
import jax
import jax.numpy as jnp
from jax import lax
from jax.experimental import pallas as pl
from jax.experimental.pallas import tpu as pltpu
from jax.sharding import PartitionSpec as P

CAP = 32
LANES = 128
EMPTY = 262144.0
TILE = 512


def pack_kernel(emb_ref, cid_ref, order_ref, out_ref, target_ref, unit_ref):
    step = pl.program_id(0)
    rows, width = emb_ref.shape

    @pl.when(step == 0)
    def _():
        chunk = 128
        for r in range(rows // chunk):
            part = pl.ds(r * chunk, chunk)
            e = emb_ref[part, :].astype(jnp.float32)
            scale = lax.rsqrt(jnp.sum(e * e, axis=1, keepdims=True) + 1e-06)
            unit_ref[part, :width] = (e * scale).astype(jnp.bfloat16)
        cid = cid_ref[...].astype(jnp.float32)
        column = jnp.transpose(jnp.broadcast_to(cid, (LANES, rows)))
        above = lax.broadcasted_iota(jnp.int32, (rows, LANES), 0)
        for j in range(rows // LANES):
            lanes = slice(j * LANES, (j + 1) * LANES)
            here = lax.broadcasted_iota(jnp.int32, (rows, LANES), 1) + j * LANES
            same = (column == cid[:, lanes]) & (above < here)
            place = jnp.sum(same.astype(jnp.float32), axis=0, keepdims=True)
            target_ref[:, lanes] = (cid[:, lanes] * CAP + place).astype(jnp.int32)
        code = order_ref[...] + 1
        high = jnp.broadcast_to((code >> 8).astype(jnp.float32), (LANES // 2, rows))
        low = jnp.broadcast_to((code & 255).astype(jnp.float32), (LANES // 2, rows))
        both = jnp.concatenate([high, low], axis=0)
        unit_ref[:, width:] = jnp.transpose(both).astype(jnp.bfloat16)

    group, cap, full = out_ref.shape
    slots = group * cap
    slot = lax.broadcasted_iota(jnp.int32, (slots, rows), 0) + step * slots
    place = (slot == target_ref[...]).astype(jnp.float32).astype(jnp.bfloat16)
    packed = jnp.dot(place, unit_ref[...], preferred_element_type=jnp.float32)
    out_ref[...] = packed.astype(jnp.bfloat16).reshape(group, cap, full)


def pack(embeddings, cid, order, owners):
    rows, width = embeddings.shape
    full = width + LANES
    group = TILE // CAP
    return pl.pallas_call(
        pack_kernel,
        grid=(owners // group,),
        out_shape=(
            jax.ShapeDtypeStruct((owners, CAP, full), jnp.bfloat16),
            jax.ShapeDtypeStruct((1, rows), jnp.int32),
        ),
        in_specs=[
            pl.BlockSpec((rows, width), lambda i: (0, 0)),
            pl.BlockSpec((1, rows), lambda i: (0, 0)),
            pl.BlockSpec((1, rows), lambda i: (0, 0)),
        ],
        out_specs=(
            pl.BlockSpec((group, CAP, full), lambda i: (i, 0, 0)),
            pl.BlockSpec((1, rows), lambda i: (0, 0)),
        ),
        scratch_shapes=[pltpu.VMEM((rows, full), jnp.bfloat16)],
        compiler_params=pltpu.CompilerParams(vmem_limit_bytes=32 * 2**20),
        name="pack_rows",
    )(embeddings, cid, order)


def read_ranks(x_ref, width, column_ref, row_ref):
    count = x_ref.shape[0]
    for t in range(count // TILE):
        part = slice(t * TILE, (t + 1) * TILE)
        two = x_ref[part, width:].astype(jnp.float32)
        other = pltpu.roll(two, LANES // 2, 1)
        lane = lax.broadcasted_iota(jnp.int32, two.shape, 1)
        code = jnp.where(lane < LANES // 2, two * 256.0 + other, two + other * 256.0)
        code = jnp.where(code == 0.0, EMPTY, code)
        if column_ref is not None:
            column_ref[part, :] = code
        if row_ref is not None:
            row_ref[:, part] = jnp.transpose(code)[:8, :]


def compare(x, y, column, row, rows_best, columns_best):
    sims = lax.dot_general(x, y, (((1,), (1,)), ((), ())), preferred_element_type=jnp.float32)
    columns = []
    for j in range(sims.shape[1] // LANES):
        lanes = slice(j * LANES, (j + 1) * LANES)
        s = sims[:, lanes]
        earlier = row[:1, lanes] < column
        rows_best = jnp.maximum(rows_best, jnp.where(earlier, s, -1.0))
        if columns_best is not None:
            later = jnp.where(earlier, -1.0, s)
            columns.append(jnp.max(later.reshape(-1, 8, LANES), axis=0))
    if columns_best is None:
        return rows_best, None
    return rows_best, jnp.maximum(columns_best, jnp.concatenate(columns, axis=1))


def own_kernel(width, x_ref, out_ref, column_ref, row_ref, rows_ref, columns_ref):
    count = x_ref.shape[0]
    read_ranks(x_ref, width, column_ref, row_ref)
    rows_ref[...] = jnp.full(rows_ref.shape, -1.0, jnp.float32)
    columns_ref[...] = jnp.full(columns_ref.shape, -1.0, jnp.float32)
    tiles = count // TILE
    for i in range(tiles):
        a = slice(i * TILE, (i + 1) * TILE)
        for j in range(i, tiles):
            b = slice(j * TILE, (j + 1) * TILE)
            best, across = compare(
                x_ref[a, :width], x_ref[b, :width], column_ref[a, :], row_ref[:, b],
                rows_ref[a, :], columns_ref[:, b] if j > i else None,
            )
            rows_ref[a, :] = best
            if across is not None:
                columns_ref[:, b] = across
    for i in range(tiles):
        a = slice(i * TILE, (i + 1) * TILE)
        best = jnp.max(jnp.transpose(rows_ref[a, :]), axis=0, keepdims=True)
        best = jnp.maximum(best, jnp.max(columns_ref[:, a], axis=0, keepdims=True))
        out_ref[:, a] = jnp.broadcast_to(best, (8, TILE))


def own_pairs(x, width):
    count, full = x.shape
    pairs = count * (count + TILE) // 2
    return pl.pallas_call(
        functools.partial(own_kernel, width),
        out_shape=jax.ShapeDtypeStruct((8, count), jnp.float32),
        in_specs=[pl.BlockSpec(memory_space=pltpu.VMEM)],
        out_specs=pl.BlockSpec(memory_space=pltpu.VMEM),
        scratch_shapes=[
            pltpu.VMEM((count, LANES), jnp.float32),
            pltpu.VMEM((8, count), jnp.float32),
            pltpu.VMEM((count, LANES), jnp.float32),
            pltpu.VMEM((8, count), jnp.float32),
        ],
        compiler_params=pltpu.CompilerParams(vmem_limit_bytes=40 * 2**20),
        cost_estimate=pl.CostEstimate(
            flops=2 * pairs * width, bytes_accessed=2 * count * full, transcendentals=0
        ),
        name="own_pairs",
    )(x)


def cross_kernel(width, core_ref, x_ref, y_ref, own_ref, out_ref, column_ref, row_ref, rows_ref, columns_ref):
    count = x_ref.shape[0]
    core = core_ref[0]
    read_ranks(x_ref, width, column_ref, None)
    read_ranks(y_ref, width, None, row_ref)
    rows_ref[...] = jnp.full(rows_ref.shape, -1.0, jnp.float32)
    columns_ref[...] = jnp.full(columns_ref.shape, -1.0, jnp.float32)
    tiles = count // TILE
    half = tiles // 2
    for t in range(tiles * half):
        i = jnp.where(core == 0, t // half, half + t % half)
        j = jnp.where(core == 0, t % half, t // half)
        a = pl.ds(pl.multiple_of(i * TILE, TILE), TILE)
        b = pl.ds(pl.multiple_of(j * TILE, TILE), TILE)
        best, across = compare(
            x_ref[a, :width], y_ref[b, :width], column_ref[a, :], row_ref[:, b],
            rows_ref[a, :], columns_ref[:, b],
        )
        rows_ref[a, :] = best
        columns_ref[:, b] = across
    parity = lax.broadcasted_iota(jnp.int32, (8, LANES), 0) % 2
    for g in range(count // LANES):
        a = slice(g * LANES, (g + 1) * LANES)
        mine = jnp.max(jnp.transpose(rows_ref[a, :]), axis=0, keepdims=True)
        mine = jnp.maximum(mine, own_ref[:1, a])
        theirs = jnp.max(columns_ref[:, a], axis=0, keepdims=True)
        out_ref[g * 8 : (g + 1) * 8, :] = jnp.where(
            parity == core, jnp.broadcast_to(mine, (8, LANES)), jnp.broadcast_to(theirs, (8, LANES))
        )


def cross_pairs(core, x, y, own, width):
    count, full = x.shape
    return pl.pallas_call(
        functools.partial(cross_kernel, width),
        out_shape=jax.ShapeDtypeStruct((count // LANES * 8, LANES), jnp.float32),
        in_specs=[pl.BlockSpec(memory_space=pltpu.SMEM)] + [pl.BlockSpec(memory_space=pltpu.VMEM)] * 3,
        out_specs=pl.BlockSpec(memory_space=pltpu.VMEM),
        scratch_shapes=[
            pltpu.VMEM((count, LANES), jnp.float32),
            pltpu.VMEM((8, count), jnp.float32),
            pltpu.VMEM((count, LANES), jnp.float32),
            pltpu.VMEM((8, count), jnp.float32),
        ],
        compiler_params=pltpu.CompilerParams(vmem_limit_bytes=40 * 2**20),
        cost_estimate=pl.CostEstimate(
            flops=count * count * width, bytes_accessed=4 * count * full, transcendentals=0
        ),
        name="cross_pairs",
    )(core, x, y, own)


def pick_kernel(lane_ref, recv_ref, target_ref, out_ref):
    pairs = recv_ref.shape[0]
    owners = pairs // 2
    best = jnp.maximum(
        recv_ref[pl.ds(0, owners, stride=2), :], recv_ref[pl.ds(1, owners, stride=2), :]
    )
    target = target_ref[...]
    rows = target.shape[1]
    cid = target >> 5
    slot = (target & (CAP - 1)) + lane_ref[0]
    chosen = lax.broadcasted_iota(jnp.int32, (owners, rows), 0) == cid
    chosen = chosen.astype(jnp.float32).astype(jnp.bfloat16)
    total = jnp.zeros((LANES, rows), jnp.float32)
    rest = best
    for _ in range(3):
        piece = rest.astype(jnp.bfloat16)
        rest = rest - piece.astype(jnp.float32)
        total += lax.dot_general(
            piece, chosen, (((0,), (0,)), ((), ())), preferred_element_type=jnp.float32
        )
    mine = lax.broadcasted_iota(jnp.int32, (LANES, rows), 0) == slot
    out_ref[...] = jnp.sum(jnp.where(mine, total, 0.0), axis=0, keepdims=True)


def pick(lane, recv, target):
    return pl.pallas_call(
        pick_kernel,
        out_shape=jax.ShapeDtypeStruct(target.shape, jnp.float32),
        in_specs=[pl.BlockSpec(memory_space=pltpu.SMEM)] + [pl.BlockSpec(memory_space=pltpu.VMEM)] * 2,
        out_specs=pl.BlockSpec(memory_space=pltpu.VMEM),
        name="pick_results",
    )(lane, recv, target)


def shards(embeddings, cluster, order):
    owners = lax.axis_size("owner")
    rows, width = embeddings.shape
    packed, target = pack(embeddings, cluster.reshape(1, rows), order.reshape(1, rows), owners)
    received = lax.all_to_all(packed, "owner", split_axis=0, concat_axis=0, tiled=True)
    mine = received.reshape(owners * CAP, width + LANES)
    theirs = lax.ppermute(mine, "split", [(0, 1), (1, 0)])
    own = own_pairs(mine, width)
    core = lax.axis_index("split").astype(jnp.int32).reshape(1)
    best = cross_pairs(core, mine, theirs, own, width)
    returned = lax.all_to_all(best, ("owner", "split"), split_axis=0, concat_axis=0, tiled=True)
    per_row = LANES // CAP
    lane = (lax.axis_index("owner") % per_row * CAP).astype(jnp.int32).reshape(1)
    return pick(lane, returned, target).reshape(rows)


def solution(mesh):
    return jax.shard_map(
        shards,
        mesh=mesh,
        in_specs=(P(("owner", "split"), None), P(("owner", "split"), None), P(("owner", "split"))),
        out_specs=P(("owner", "split")),
        check_vma=False,
    )
```

time: 174 us -> 111 us (0.64)
  matrix products: 39.2 us -> 0 us
  Pallas kernels: 0 us -> 23.4 us
  between operations: 13.5 us -> 0.05 us
  other arithmetic: 12.4 us -> 0 us
  starting transfers between devices: 13.7 us -> 6.13 us
  waiting for transfers between devices: 16.8 us -> 9.38 us
  local copies, waits for them, and re-layouts: 9.83 us -> 3.22 us
    dot_general x8 -> x0, matrix products: 39.2 us -> none  [step(): lax.dot_general(queries, block_keys, (((1,), (1,)), ((), ())), preferred_...]
    pallas_call x0 -> x4, Pallas kernels: none -> 23.4 us  [the longest x1 9.59 us: cross_pairs(): pl.pallas_call(functools.partial(cross_kernel, width), out_shape=jax.Shap...]
    all_to_all x2 -> x1, starting transfers between devices: 13.7 us -> 3.81 us  [shards(): lax.all_to_all(best, ('owner', 'split'), split_axis=0, concat_axis=0, til...]
    all_to_all x2 -> x1, waiting for transfers between devices: 16.8 us -> 9.38 us  [shards(): lax.all_to_all(best, ('owner', 'split'), split_axis=0, concat_axis=0, til...]
    all_to_all x1, blocking collectives: 62.2 us -> 68.7 us  [shards(): lax.all_to_all(packed, 'owner', split_axis=0, concat_axis=0, tiled=True)]
    scatter x1 -> x0, other arithmetic: 5.94 us -> none  [shards(): jnp.zeros((owners * slots, width), jnp.bfloat16).at[target].set(unit)]
    all_gather x1 -> x0, blocking collectives: 5.15 us -> none  [shards(): lax.all_gather(query_order, 'split', axis=0, tiled=True)]
    gather x1 -> x0, local copies, waits for them, and re-layouts: 4.27 us -> none  [shards(): return returned.reshape(owners * slots)[target]]
  transfers between devices with their start and end apart: 3 -> 2, of which waited for: 2 -> 1; matrix products, arithmetic and copies ran while one was open for 2% -> 0% of each run, Pallas kernels for 0% -> 7%
where the time goes in v1:
time: 111 us
  blocking collectives  68.7 us (62%)
  Pallas kernels  23.4 us (21%)
  waiting for transfers between devices  9.38 us (8%)
  starting transfers between devices  6.13 us (6%)
  local copies, waits for them, and re-layouts  3.22 us (3%)
    all_to_all x1, blocking collectives, shards(): lax.all_to_all(packed, 'owner', split_axis=0, concat_axis=0, tiled=True)  68.7 us
    pallas_call x1, Pallas kernels, cross_pairs(): pl.pallas_call(functools.partial(cross_kernel, width), out_shape=jax.Shap...  9.59 us
    all_to_all x1, waiting for transfers between devices, shards(): lax.all_to_all(best, ('owner', 'split'), split_axis=0, concat_axis=0, til...  9.38 us
    pallas_call x1, Pallas kernels, own_pairs(): pl.pallas_call(functools.partial(own_kernel, width), out_shape=jax.ShapeD...  8.14 us
    pallas_call x1, Pallas kernels, pack(): pl.pallas_call(pack_kernel, grid=(owners // group,), out_shape=(jax.Shape...  3.89 us
    all_to_all x1, starting transfers between devices, shards(): lax.all_to_all(best, ('owner', 'split'), split_axis=0, concat_axis=0, til...  3.81 us
    unnamed x10, local copies, waits for them, and re-layouts  3.22 us
    ppermute x1, starting transfers between devices, shards(): theirs = lax.ppermute(mine, 'split', [(0, 1), (1, 0)])  2.32 us
  transfers between devices with their start and end apart: 2, of which 1 were waited for; matrix products, arithmetic and copies ran while one was open for 0% of the time, Pallas kernels for 7%

profile of v1, /device:TPU:1, one launch (start us, length us, event | category | flops | bytes accessed | tf_op | source)
XLA Modules:
  0.0 110.9 jit_solution(5712146017763157092)
XLA Ops:
  0.0 0.0 copy-start
  0.0 1.2 %copy-done = bf16[512,1024]{1,0:T(8,128)(2,1)S(1)} copy-done((bf16[512,1024]{1,0:T(8,128)(2,1)S(1)}, bf16[512,1024]{1,0:T(8,128)(2,1)}, u32[]{:S(2)}) %copy-start) | copy-done | bytes 1048600
  1.2 0.0 copy-start.1
  1.2 0.7 copy-done.1
  1.9 0.0 copy-start.2
  1.9 0.7 copy-done.2
  2.6 3.9 %pack_rows.1 = (bf16[64,32,1152]{2,1,0:T(8,128)(2,1)S(1)}, s32[1,512]{1,0:T(1,128)S(1)}) custom-call(bf16[512,1024]{1,0:T(8,128)(2,1)S(1)} %copy-done, s32[1,512]{1,0:T(1,128)S(1)} %bitcast.10, s32[1,512]{1,0:T(1,128)S(1)} %bitcast.11), custom_call_target="tpu_custom_call" | custom-call | tf_op jit(solution)/shard_map/pack_rows/pallas_call | solution.py:54
  6.5 0.0 copy-start.3
  6.5 68.7 %all_to_all.16 = bf16[64,32,1152]{2,1,0:T(8,128)(2,1)} all-to-all(bf16[64,32,1152]{2,1,0:T(8,128)(2,1)S(1)} %get-tuple-element.7), channel_id=1, replica_groups=mesh['owner'=64,'split'=2] {'owner'}, dimensions={0} | all-to-all | bytes 9437184 | tf_op jit(solution)/shard_map/all_to_all | solution.py:243
  75.2 0.0 copy-done.3
  75.2 2.3 %collective-permute-start = (bf16[2048,1152]{1,0:T(8,128)(2,1)}, bf16[2048,1152]{1,0:T(8,128)(2,1)}, u32[]{:S(2)}, u32[]{:S(2)}) collective-permute-start(bf16[2048,1152]{1,0:T(8,128)(2,1)} %bitcast.4.x_ref), channel_id=1, source_target_pairs={{0,1},{1,0},{2,3},{3,2},{4,5},{5,4},{6,7},{7,6},{8,9},{9,8},{10,11... | collective-permute-start | bytes 14155784 | tf_op jit(solution)/shard_map/ppermute | solution.py:245
  77.5 8.1 %own_pairs.1.own_ref = f32[8,2048]{1,0:T(8,128)S(1)} custom-call(bf16[2048,1152]{1,0:T(8,128)(2,1)} %bitcast.4.x_ref), custom_call_target="tpu_custom_call" | custom-call | flops 5368709120 | bytes 4718592 | tf_op jit(solution)/shard_map/own_pairs/pallas_call | solution.py:134
  85.7 0.0 collective-permute-done.y_ref
  85.7 9.6 %cross_pairs.1 = f32[128,128]{1,0:T(8,128)} custom-call(s32[1]{0:T(128)} %bitcast.1.core_ref, bf16[2048,1152]{1,0:T(8,128)(2,1)} %bitcast.4.x_ref, bf16[2048,1152]{1,0:T(8,128)(2,1)} %collective-permute-done.y_ref, f32[8,2048]{1,0:T(8,128)S(1)} %own_pairs.1.own_ref), custom_call_target="tpu_custom_call" | custom-call | flops 4294967296 | bytes 9437184 | tf_op jit(solution)/shard_map/cross_pairs/pallas_call | solution.py:186
  95.3 3.8 %all-to-all-start.1 = ((f32[128,1,128]{2,1,0:T(1,128)}), f32[128,1,128]{2,1,0:T(1,128)S(1)}, u32[]{:S(2)}, u32[]{:S(2)}) async-start(f32[128,1,128]{2,1,0:T(1,128)} %bitcast.6), calls=%async_computation.1 | async-start | bytes 131072 | tf_op jit(solution)/shard_map/all_to_all | solution.py:249
  99.1 9.4 %all-to-all-done.1 = f32[128,1,128]{2,1,0:T(1,128)S(1)} async-done(((f32[128,1,128]{2,1,0:T(1,128)}), f32[128,1,128]{2,1,0:T(1,128)S(1)}, u32[]{:S(2)}, u32[]{:S(2)}) %all-to-all-start.1) | async-done | bytes 65568 | tf_op jit(solution)/shard_map/all_to_all | solution.py:249
  108.5 0.0 copy-start.4
  108.5 0.6 copy-done.4
  109.1 1.7 %pick_results.1 = f32[1,512]{1,0:T(1,128)} custom-call(s32[1]{0:T(128)} %bitcast.lane_ref, f32[128,128]{1,0:T(8,128)} %bitcast.12, s32[1,512]{1,0:T(1,128)} %copy-done.3), custom_call_target="tpu_custom_call" | custom-call | tf_op jit(solution)/shard_map/pick_results/pallas_call | solution.py:230
Async XLA Ops:
  0.0 1.2 %copy-start = (bf16[512,1024]{1,0:T(8,128)(2,1)S(1)}, bf16[512,1024]{1,0:T(8,128)(2,1)}, u32[]{:S(2)}) copy-start(bf16[512,1024]{1,0:T(8,128)(2,1)} %emb_ref.1) | copy-start | bytes 3145732
  1.2 0.7 copy-start.1
  1.9 0.7 copy-start.2
  6.5 68.7 %copy-start.3 = (s32[1,512]{1,0:T(1,128)}, s32[1,512]{1,0:T(1,128)S(1)}, u32[]{:S(2)}) copy-start(s32[1,512]{1,0:T(1,128)S(1)} %get-tuple-element.8.target_ref) | copy-start | bytes 6148
  75.2 10.5 %collective-permute-start = (bf16[2048,1152]{1,0:T(8,128)(2,1)}, bf16[2048,1152]{1,0:T(8,128)(2,1)}, u32[]{:S(2)}, u32[]{:S(2)}) collective-permute-start(bf16[2048,1152]{1,0:T(8,128)(2,1)} %bitcast.4.x_ref), channel_id=1, source_target_pairs={{0,1},{1,0},{2,3},{3,2},{4,5},{5,4},{6,7},{7,6},{8,9},{9,8},{10,11... | collective-permute-start | bytes 14155784 | tf_op jit(solution)/shard_map/ppermute | solution.py:245
  95.3 13.2 %all-to-all-start.1 = ((f32[128,1,128]{2,1,0:T(1,128)}), f32[128,1,128]{2,1,0:T(1,128)S(1)}, u32[]{:S(2)}, u32[]{:S(2)}) async-start(f32[128,1,128]{2,1,0:T(1,128)} %bitcast.6), calls=%async_computation.1 | async-start | bytes 131072 | tf_op jit(solution)/shard_map/all_to_all | solution.py:249
  108.5 0.6 copy-start.4

commit v2 on v0

v2 whole, which is shorter than its diff:
```python
import functools
import jax
import jax.numpy as jnp
from jax import lax
from jax.experimental import pallas as pl
from jax.experimental.pallas import tpu as pltpu
from jax.sharding import PartitionSpec as P

CAP = 32
LANES = 128
META = 16
EMPTY = 262144.0
TILE = 512
PER_TILE = TILE // CAP
PER_ROW = LANES // CAP


def pack_kernel(emb_hbm, cid_hbm, order_hbm, out_ref, target_ref, emb_ref, cid_ref, order_ref, unit_ref, sems):
    rows, width = emb_ref.shape
    owners = out_ref.shape[0]
    chunk = 128
    chunks = rows // chunk
    small = [
        pltpu.make_async_copy(cid_hbm, cid_ref, sems.at[chunks]),
        pltpu.make_async_copy(order_hbm, order_ref, sems.at[chunks + 1]),
    ]
    loads = []
    for r in range(chunks):
        part = pl.ds(r * chunk, chunk)
        loads.append(pltpu.make_async_copy(emb_hbm.at[part], emb_ref.at[part], sems.at[r]))
    for copy in small + loads:
        copy.start()
    for copy in small:
        copy.wait()
    cid = cid_ref[...].astype(jnp.float32)
    column = jnp.transpose(jnp.broadcast_to(cid, (LANES, rows)))
    above = lax.broadcasted_iota(jnp.int32, (rows, LANES), 0)
    for j in range(rows // LANES):
        lanes = slice(j * LANES, (j + 1) * LANES)
        here = lax.broadcasted_iota(jnp.int32, (rows, LANES), 1) + j * LANES
        same = (column == cid[:, lanes]) & (above < here)
        place = jnp.sum(same.astype(jnp.float32), axis=0, keepdims=True)
        target_ref[:, lanes] = (cid[:, lanes] * CAP + place).astype(jnp.int32)
    code = order_ref[...] + 1
    high = jnp.broadcast_to((code >> 8).astype(jnp.float32), (META // 2, rows))
    low = jnp.broadcast_to((code & 255).astype(jnp.float32), (META // 2, rows))
    both = jnp.concatenate([high, low, jnp.zeros((LANES - META, rows), jnp.float32)], axis=0)
    unit_ref[:, width:] = jnp.transpose(both).astype(jnp.bfloat16)
    for r in range(chunks):
        part = pl.ds(r * chunk, chunk)
        loads[r].wait()
        e = emb_ref[part, :].astype(jnp.float32)
        scale = lax.rsqrt(jnp.sum(e * e, axis=1, keepdims=True) + 1e-06)
        unit_ref[part, :width] = (e * scale).astype(jnp.bfloat16)
    target = target_ref[...]
    me = lax.axis_index("owner") % PER_ROW
    segment = lax.broadcasted_iota(jnp.int32, (META, LANES), 1) // CAP
    for step in range(owners // PER_TILE):
        block = slice(step * PER_TILE, (step + 1) * PER_TILE)
        slot = lax.broadcasted_iota(jnp.int32, (TILE, rows), 0) + step * TILE
        place = (slot == target).astype(jnp.float32).astype(jnp.bfloat16)
        packed = jnp.dot(place, unit_ref[...], preferred_element_type=jnp.float32)
        for k in range(width // LANES):
            part = packed[:, k * LANES : (k + 1) * LANES].astype(jnp.bfloat16)
            out_ref[block, k * CAP : (k + 1) * CAP, :] = part.reshape(PER_TILE, CAP, LANES)
        ranks = jnp.transpose(packed[:, width:])[:META, :]
        for t in range(PER_TILE // PER_ROW):
            tile = ranks[:, t * LANES : (t + 1) * LANES]
            for q in range(PER_ROW):
                alone = jnp.where(segment == q, tile, 0.0)
                moved = pltpu.roll(alone, (me + PER_ROW - q) % PER_ROW * CAP, 1)
                out_ref[step * PER_TILE + t * PER_ROW + q, width // LANES * CAP :, :] = moved.astype(
                    jnp.bfloat16
                )


def pack(embeddings, cid, order, owners):
    rows, width = embeddings.shape
    return pl.pallas_call(
        pack_kernel,
        out_shape=(
            jax.ShapeDtypeStruct((owners, width // LANES * CAP + META, LANES), jnp.bfloat16),
            jax.ShapeDtypeStruct((1, rows), jnp.int32),
        ),
        in_specs=[pl.BlockSpec(memory_space=pl.ANY)] * 3,
        out_specs=(pl.BlockSpec(memory_space=pltpu.VMEM),) * 2,
        scratch_shapes=[
            pltpu.VMEM((rows, width), jnp.bfloat16),
            pltpu.VMEM((1, rows), jnp.int32),
            pltpu.VMEM((1, rows), jnp.int32),
            pltpu.VMEM((rows, width + LANES), jnp.bfloat16),
            pltpu.SemaphoreType.DMA((rows // 128 + 2,)),
        ],
        compiler_params=pltpu.CompilerParams(vmem_limit_bytes=32 * 2**20),
        name="pack_rows",
    )(embeddings, cid, order)


def tile_copies(source, first, target, sems):
    copies = []
    for k in range(target.shape[2] // LANES):
        copies.append(
            pltpu.make_async_copy(
                source.at[pl.ds(first, PER_TILE), pl.ds(k * CAP, CAP), :],
                target.at[:, :, pl.ds(k * LANES, LANES)],
                sems.at[k],
            )
        )
    return copies


def rank_row(meta_ref, group):
    tiles = meta_ref[group * PER_ROW : (group + 1) * PER_ROW].astype(jnp.float32)
    both = jnp.sum(tiles, axis=0)
    code = both[: META // 2] * 256.0 + both[META // 2 :]
    return jnp.where(code == 0.0, EMPTY, code)


def as_column(row):
    return jnp.transpose(jnp.broadcast_to(row[:1], (LANES, LANES)))


def compare(x_ref, y_ref, column_ref, row_ref, rows_ref, columns_ref):
    width = x_ref.shape[2]
    y = y_ref[...].reshape(TILE, width)
    part = TILE // 2
    for h in range(2):
        some = slice(h * part, (h + 1) * part)
        x = x_ref[h * PER_TILE // 2 : (h + 1) * PER_TILE // 2].reshape(part, width)
        sims = lax.dot_general(x, y, (((1,), (1,)), ((), ())), preferred_element_type=jnp.float32)
        column = column_ref[some, :]
        best = rows_ref[some, :]
        for j in range(TILE // LANES):
            lanes = slice(j * LANES, (j + 1) * LANES)
            s = sims[:, lanes]
            earlier = row_ref[:1, lanes] < column
            best = jnp.maximum(best, jnp.where(earlier, s, -1.0))
            if columns_ref is not None:
                later = jnp.where(earlier, -1.0, s)
                across = jnp.max(later.reshape(-1, 8, LANES), axis=0)
                columns_ref[:, lanes] = jnp.maximum(columns_ref[:, lanes], across)
        rows_ref[some, :] = best


def own_kernel(x_hbm, out_ref, x_ref, meta_ref, column_ref, row_ref, rows_ref, columns_ref, sems, meta_sem):
    tiles = x_ref.shape[0]
    meta_row = x_hbm.shape[1] - META
    meta = pltpu.make_async_copy(x_hbm.at[:, pl.ds(meta_row, META), :], meta_ref, meta_sem)
    meta.start()
    loads = [tile_copies(x_hbm, t * PER_TILE, x_ref.at[t], sems.at[t]) for t in range(tiles)]
    for load in loads:
        for copy in load:
            copy.start()
    rows_ref[...] = jnp.full(rows_ref.shape, -1.0, jnp.float32)
    columns_ref[...] = jnp.full(columns_ref.shape, -1.0, jnp.float32)
    meta.wait()
    for j in range(tiles):
        b = slice(j * TILE, (j + 1) * TILE)
        for g in range(j * TILE // LANES, (j + 1) * TILE // LANES):
            lanes = slice(g * LANES, (g + 1) * LANES)
            row = rank_row(meta_ref, g)
            row_ref[:, lanes] = row
            column_ref[lanes, :] = as_column(row)
        for copy in loads[j]:
            copy.wait()
        for i in range(j + 1):
            a = slice(i * TILE, (i + 1) * TILE)
            compare(
                x_ref.at[i], x_ref.at[j], column_ref.at[a], row_ref.at[:, b],
                rows_ref.at[a], columns_ref.at[:, b] if j > i else None,
            )
    for g in range(tiles * TILE // LANES):
        a = slice(g * LANES, (g + 1) * LANES)
        best = jnp.max(jnp.transpose(rows_ref[a, :]), axis=0, keepdims=True)
        best = jnp.maximum(best, jnp.max(columns_ref[:, a], axis=0, keepdims=True))
        out_ref[:, a] = jnp.broadcast_to(best, (8, LANES))


def own_pairs(x, width):
    owners = x.shape[0]
    count = owners * CAP
    tiles = count // TILE
    return pl.pallas_call(
        own_kernel,
        out_shape=jax.ShapeDtypeStruct((8, count), jnp.float32),
        in_specs=[pl.BlockSpec(memory_space=pl.ANY)],
        out_specs=pl.BlockSpec(memory_space=pltpu.VMEM),
        scratch_shapes=[
            pltpu.VMEM((tiles, PER_TILE, CAP, width), jnp.bfloat16),
            pltpu.VMEM((owners, META, LANES), jnp.bfloat16),
            pltpu.VMEM((count, LANES), jnp.float32),
            pltpu.VMEM((8, count), jnp.float32),
            pltpu.VMEM((count, LANES), jnp.float32),
            pltpu.VMEM((8, count), jnp.float32),
            pltpu.SemaphoreType.DMA((tiles, width // LANES)),
            pltpu.SemaphoreType.DMA(()),
        ],
        compiler_params=pltpu.CompilerParams(vmem_limit_bytes=32 * 2**20),
        cost_estimate=pl.CostEstimate(
            flops=count * (count + TILE) * width, bytes_accessed=2 * count * width, transcendentals=0
        ),
        name="own_pairs",
    )(x)


def cross_kernel(x_hbm, y_hbm, own_ref, out_ref, a_ref, b_ref, a_meta, b_meta, column_ref, row_ref, rows_ref, columns_ref, a_sems, b_sems, meta_sems):
    core = lax.axis_index("split")
    tiles, halves = a_ref.shape[0], b_ref.shape[0]
    meta_row = x_hbm.shape[1] - META
    half = halves * PER_TILE

    def copies(all_hbm, some_hbm, first):
        metas = [
            pltpu.make_async_copy(all_hbm.at[:, pl.ds(meta_row, META), :], a_meta, meta_sems.at[0]),
            pltpu.make_async_copy(
                some_hbm.at[pl.ds(first, half), pl.ds(meta_row, META), :], b_meta, meta_sems.at[1]
            ),
        ]
        a = [tile_copies(all_hbm, t * PER_TILE, a_ref.at[t], a_sems.at[t]) for t in range(tiles)]
        b = [tile_copies(some_hbm, first + t * PER_TILE, b_ref.at[t], b_sems.at[t]) for t in range(halves)]
        return metas, a, b

    def start(metas, a, b):
        for copy in metas + b[0] + a[0]:
            copy.start()
        for load in b[1:] + a[1:]:
            for copy in load:
                copy.start()

    @pl.when(core == 0)
    def _():
        start(*copies(x_hbm, y_hbm, 0))

    @pl.when(core != 0)
    def _():
        start(*copies(y_hbm, x_hbm, half))

    metas, a_loads, b_loads = copies(x_hbm, y_hbm, 0)
    rows_ref[...] = jnp.full(rows_ref.shape, -1.0, jnp.float32)
    columns_ref[...] = jnp.full(columns_ref.shape, -1.0, jnp.float32)
    for copy in metas:
        copy.wait()
    for g in range(tiles * TILE // LANES):
        lanes = slice(g * LANES, (g + 1) * LANES)
        column_ref[lanes, :] = as_column(rank_row(a_meta, g))
    for g in range(halves * TILE // LANES):
        row_ref[:, g * LANES : (g + 1) * LANES] = rank_row(b_meta, g)
    for copy in b_loads[0]:
        copy.wait()
    for i in range(tiles):
        a = slice(i * TILE, (i + 1) * TILE)
        for copy in a_loads[i]:
            copy.wait()
        for j in range(halves):
            b = slice(j * TILE, (j + 1) * TILE)
            if i == 0 and j > 0:
                for copy in b_loads[j]:
                    copy.wait()
            compare(
                a_ref.at[i], b_ref.at[j], column_ref.at[a], row_ref.at[:, b],
                rows_ref.at[a], columns_ref.at[:, b],
            )
    parity = lax.broadcasted_iota(jnp.int32, (8, LANES), 0) % 2
    groups = tiles * TILE // LANES
    cut = groups - halves * TILE // LANES
    nothing = jnp.full((1, LANES), -1.0, jnp.float32)
    for g in range(groups):
        a = slice(g * LANES, (g + 1) * LANES)
        from_all = jnp.max(jnp.transpose(rows_ref[a, :]), axis=0, keepdims=True)
        low = high = nothing
        if g < groups - cut:
            low = jnp.max(columns_ref[:, a], axis=0, keepdims=True)
        if g >= cut:
            b = slice((g - cut) * LANES, (g - cut + 1) * LANES)
            high = jnp.max(columns_ref[:, b], axis=0, keepdims=True)
        mine = jnp.maximum(own_ref[:1, a], jnp.where(core == 0, from_all, high))
        theirs = jnp.where(core == 0, low, from_all)
        out_ref[g * 8 : (g + 1) * 8, :] = jnp.where(
            parity == core, jnp.broadcast_to(mine, (8, LANES)), jnp.broadcast_to(theirs, (8, LANES))
        )


def cross_pairs(x, y, own, width):
    owners = x.shape[0]
    count = owners * CAP
    tiles = count // TILE
    halves = tiles // 2
    return pl.pallas_call(
        cross_kernel,
        out_shape=jax.ShapeDtypeStruct((count // LANES * 8, LANES), jnp.float32),
        in_specs=[pl.BlockSpec(memory_space=pl.ANY)] * 2 + [pl.BlockSpec(memory_space=pltpu.VMEM)],
        out_specs=pl.BlockSpec(memory_space=pltpu.VMEM),
        scratch_shapes=[
            pltpu.VMEM((tiles, PER_TILE, CAP, width), jnp.bfloat16),
            pltpu.VMEM((halves, PER_TILE, CAP, width), jnp.bfloat16),
            pltpu.VMEM((owners, META, LANES), jnp.bfloat16),
            pltpu.VMEM((owners // 2, META, LANES), jnp.bfloat16),
            pltpu.VMEM((count, LANES), jnp.float32),
            pltpu.VMEM((8, count // 2), jnp.float32),
            pltpu.VMEM((count, LANES), jnp.float32),
            pltpu.VMEM((8, count // 2), jnp.float32),
            pltpu.SemaphoreType.DMA((tiles, width // LANES)),
            pltpu.SemaphoreType.DMA((halves, width // LANES)),
            pltpu.SemaphoreType.DMA((2,)),
        ],
        compiler_params=pltpu.CompilerParams(vmem_limit_bytes=32 * 2**20),
        cost_estimate=pl.CostEstimate(
            flops=count * count * width, bytes_accessed=3 * count * width, transcendentals=0
        ),
        name="cross_pairs",
    )(x, y, own)


def pick_kernel(recv_ref, target_ref, out_ref):
    pairs = recv_ref.shape[0]
    owners = pairs // 2
    best = jnp.maximum(
        recv_ref[pl.ds(0, owners, stride=2), :], recv_ref[pl.ds(1, owners, stride=2), :]
    )
    target = target_ref[...]
    rows = target.shape[1]
    cid = target >> 5
    slot = (target & (CAP - 1)) + lax.axis_index("owner") % PER_ROW * CAP
    chosen = lax.broadcasted_iota(jnp.int32, (owners, rows), 0) == cid
    chosen = chosen.astype(jnp.float32).astype(jnp.bfloat16)
    total = jnp.zeros((LANES, rows), jnp.float32)
    rest = best
    for _ in range(3):
        piece = rest.astype(jnp.bfloat16)
        rest = rest - piece.astype(jnp.float32)
        total += lax.dot_general(
            piece, chosen, (((0,), (0,)), ((), ())), preferred_element_type=jnp.float32
        )
    mine = lax.broadcasted_iota(jnp.int32, (LANES, rows), 0) == slot
    out_ref[...] = jnp.sum(jnp.where(mine, total, 0.0), axis=0, keepdims=True)


def pick(recv, target):
    return pl.pallas_call(
        pick_kernel,
        out_shape=jax.ShapeDtypeStruct(target.shape, jnp.float32),
        in_specs=[pl.BlockSpec(memory_space=pltpu.VMEM)] * 2,
        out_specs=pl.BlockSpec(memory_space=pltpu.VMEM),
        compiler_params=pltpu.CompilerParams(vmem_limit_bytes=8 * 2**20),
        name="pick_results",
    )(recv, target)


def shards(embeddings, cluster, order):
    owners = lax.axis_size("owner")
    rows, width = embeddings.shape
    packed, target = pack(embeddings, cluster.reshape(1, rows), order.reshape(1, rows), owners)
    mine = lax.all_to_all(packed, "owner", split_axis=0, concat_axis=0, tiled=True)
    theirs = lax.ppermute(mine, "split", [(0, 1), (1, 0)])
    own = own_pairs(mine, width)
    best = cross_pairs(mine, theirs, own, width)
    returned = lax.all_to_all(best, ("owner", "split"), split_axis=0, concat_axis=0, tiled=True)
    return pick(returned, target).reshape(rows)


def solution(mesh):
    return jax.shard_map(
        shards,
        mesh=mesh,
        in_specs=(P(("owner", "split"), None), P(("owner", "split"), None), P(("owner", "split"))),
        out_specs=P(("owner", "split")),
        check_vma=False,
    )
```

time: 174 us -> 106 us (0.61)
  matrix products: 39.2 us -> 0 us
  Pallas kernels: 0 us -> 21.7 us
  waiting for transfers between devices: 16.8 us -> 0.01 us
  between operations: 13.5 us -> 0.04 us
  other arithmetic: 12.4 us -> 0 us
  blocking collectives: 67.4 us -> 79.1 us
  starting transfers between devices: 13.7 us -> 2.22 us
  local copies, waits for them, and re-layouts: 9.83 us -> 2.59 us
    dot_general x8 -> x0, matrix products: 39.2 us -> none  [step(): lax.dot_general(queries, block_keys, (((1,), (1,)), ((), ())), preferred_...]
    pallas_call x0 -> x4, Pallas kernels: none -> 21.7 us  [the longest x1 8.74 us: cross_pairs(): pl.pallas_call(cross_kernel, out_shape=jax.ShapeDtypeStruct((count // LAN...]
    all_to_all x2 -> x0, waiting for transfers between devices: 16.8 us -> none  [the longest x1 8.39 us: shards(): lax.all_to_all(packed_order, 'owner', split_axis=0, concat_axis=0, tiled=...]
    all_to_all x2 -> x0, starting transfers between devices: 13.7 us -> none  [the longest x1 7.79 us: shards(): lax.all_to_all(best_slots.reshape(owners, slots), 'owner', split_axis=0,...]
    all_to_all x0 -> x1, blocking collectives: none -> 13.1 us  [shards(): lax.all_to_all(best, ('owner', 'split'), split_axis=0, concat_axis=0, til...]
    scatter x1 -> x0, other arithmetic: 5.94 us -> none  [shards(): jnp.zeros((owners * slots, width), jnp.bfloat16).at[target].set(unit)]
    all_gather x1 -> x0, blocking collectives: 5.15 us -> none  [shards(): lax.all_gather(query_order, 'split', axis=0, tiled=True)]
    gather x1 -> x0, local copies, waits for them, and re-layouts: 4.27 us -> none  [shards(): return returned.reshape(owners * slots)[target]]
  transfers between devices with their start and end apart: 3 -> 1, of which waited for: 2 -> 0; matrix products, arithmetic and copies ran while one was open for 2% -> 0% of each run, Pallas kernels for 0% -> 8%
where the time goes in v2:
time: 106 us
  blocking collectives  79.1 us (75%)
  Pallas kernels  21.7 us (20%)
  local copies, waits for them, and re-layouts  2.59 us (2%)
  starting transfers between devices  2.22 us (2%)
    all_to_all x1, blocking collectives, shards(): lax.all_to_all(packed, 'owner', split_axis=0, concat_axis=0, tiled=True)  66 us
    all_to_all x1, blocking collectives, shards(): lax.all_to_all(best, ('owner', 'split'), split_axis=0, concat_axis=0, til...  13.1 us
    pallas_call x1, Pallas kernels, cross_pairs(): pl.pallas_call(cross_kernel, out_shape=jax.ShapeDtypeStruct((count // LAN...  8.74 us
    pallas_call x1, Pallas kernels, own_pairs(): pl.pallas_call(own_kernel, out_shape=jax.ShapeDtypeStruct((8, count), jnp...  8.32 us
    pallas_call x1, Pallas kernels, pack(): pl.pallas_call(pack_kernel, out_shape=(jax.ShapeDtypeStruct((owners, widt...  3.8 us
    unnamed x6, local copies, waits for them, and re-layouts  2.59 us
    ppermute x1, starting transfers between devices, shards(): theirs = lax.ppermute(mine, 'split', [(0, 1), (1, 0)])  2.22 us
  transfers between devices with their start and end apart: 1, of which 0 were waited for; matrix products, arithmetic and copies ran while one was open for 0% of the time, Pallas kernels for 8%

profile of v2, /device:TPU:1, one launch (start us, length us, event | category | flops | bytes accessed | tf_op | source)
XLA Modules:
  0.0 105.7 jit_solution(10153262384610784894)
XLA Ops:
  0.0 0.0 copy-start
  0.0 1.2 %copy-done = bf16[512,1024]{1,0:T(8,128)(2,1)S(1)} copy-done((bf16[512,1024]{1,0:T(8,128)(2,1)S(1)}, bf16[512,1024]{1,0:T(8,128)(2,1)}, u32[]{:S(2)}) %copy-start) | copy-done | bytes 1048600
  1.2 0.0 copy-start.1
  1.2 0.7 copy-done.1
  1.9 0.0 copy-start.2
  1.9 0.7 copy-done.2
  2.6 3.8 %pack_rows.1 = (bf16[64,272,128]{2,1,0:T(8,128)(2,1)S(1)}, s32[1,512]{1,0:T(1,128)S(1)}) custom-call(bf16[512,1024]{1,0:T(8,128)(2,1)S(1)} %copy-done, s32[1,512]{1,0:T(1,128)S(1)} %bitcast.9, s32[1,512]{1,0:T(1,128)S(1)} %bitcast.10), custom_call_target="tpu_custom_call" | custom-call | tf_op jit(solution)/shard_map/pack_rows/pallas_call | solution.py:79
  6.4 66.0 %all_to_all.16.x_hbm = bf16[64,272,128]{2,1,0:T(8,128)(2,1)S(1)} all-to-all(bf16[64,272,128]{2,1,0:T(8,128)(2,1)S(1)} %get-tuple-element.7), channel_id=1, replica_groups=mesh['owner'=64,'split'=2] {'owner'}, dimensions={0} | all-to-all | bytes 8912896 | tf_op jit(solution)/shard_map/all_to_all | solution.py:353
  72.4 2.2 %collective-permute-start = (bf16[64,272,128]{2,1,0:T(8,128)(2,1)S(1)}, bf16[64,272,128]{2,1,0:T(8,128)(2,1)S(1)}, u32[]{:S(2)}, u32[]{:S(2)}) collective-permute-start(bf16[64,272,128]{2,1,0:T(8,128)(2,1)S(1)} %all_to_all.16.x_hbm), channel_id=1, source_target_pairs={{0,1},{1,0},{2,3},{3,2},{4,5},{5,4},{6,7},{7,6},{8,9},{9,8},{10,11... | collective-permute-start | bytes 13369352 | tf_op jit(solution)/shard_map/ppermute | solution.py:354
  74.6 8.3 %own_pairs.1.own_ref = f32[8,2048]{1,0:T(8,128)S(1)} custom-call(bf16[64,272,128]{2,1,0:T(8,128)(2,1)S(1)} %all_to_all.16.x_hbm), custom_call_target="tpu_custom_call" | custom-call | flops 5368709120 | bytes 4194304 | tf_op jit(solution)/shard_map/own_pairs/pallas_call | solution.py:183
  82.9 0.0 collective-permute-done.y_hbm
  82.9 8.7 %cross_pairs.1 = f32[128,128]{1,0:T(8,128)S(1)} custom-call(bf16[64,272,128]{2,1,0:T(8,128)(2,1)S(1)} %all_to_all.16.x_hbm, bf16[64,272,128]{2,1,0:T(8,128)(2,1)S(1)} %collective-permute-done.y_hbm, f32[8,2048]{1,0:T(8,128)S(1)} %own_pairs.1.own_ref), custom_call_target="tpu_custom_call" | custom-call | flops 4294967296 | bytes 6291456 | tf_op jit(solution)/shard_map/cross_pairs/pallas_call | solution.py:288
  91.7 13.1 %all_to_all.17 = f32[128,1,128]{2,1,0:T(1,128)S(1)} all-to-all(f32[128,1,128]{2,1,0:T(1,128)S(1)} %bitcast.8), channel_id=1, replica_groups=mesh['owner'=64,'split'=2] {'owner','split'}, dimensions={0} | all-to-all | bytes 131072 | tf_op jit(solution)/shard_map/all_to_all | solution.py:357
  104.8 0.9 pick_results.1
Async XLA Ops:
  0.0 1.2 %copy-start = (bf16[512,1024]{1,0:T(8,128)(2,1)S(1)}, bf16[512,1024]{1,0:T(8,128)(2,1)}, u32[]{:S(2)}) copy-start(bf16[512,1024]{1,0:T(8,128)(2,1)} %emb_hbm.1) | copy-start | bytes 3145732
  1.2 0.7 copy-start.1
  1.9 0.7 copy-start.2
  72.4 10.6 %collective-permute-start = (bf16[64,272,128]{2,1,0:T(8,128)(2,1)S(1)}, bf16[64,272,128]{2,1,0:T(8,128)(2,1)S(1)}, u32[]{:S(2)}, u32[]{:S(2)}) collective-permute-start(bf16[64,272,128]{2,1,0:T(8,128)(2,1)S(1)} %all_to_all.16.x_hbm), channel_id=1, source_target_pairs={{0,1},{1,0},{2,3},{3,2},{4,5},{5,4},{6,7},{7,6},{8,9},{9,8},{10,11... | collective-permute-start | bytes 13369352 | tf_op jit(solution)/shard_map/ppermute | solution.py:354

commit v3 on v2

v3 whole, which is shorter than its diff:
```python
import functools
import jax
import jax.numpy as jnp
from jax import lax
from jax.experimental import pallas as pl
from jax.experimental.pallas import tpu as pltpu
from jax.sharding import PartitionSpec as P

CAP = 32
LANES = 128
META = 16
EMPTY = 262144.0
TILE = 512
PART = 512
PER_TILE = TILE // CAP
PER_ROW = LANES // CAP


def pack_kernel(emb_hbm, cid_hbm, order_hbm, out_ref, target_ref, emb_ref, cid_ref, order_ref, unit_ref, sems):
    rows, width = emb_ref.shape
    owners = out_ref.shape[0]
    chunk = 128
    chunks = rows // chunk
    small = [
        pltpu.make_async_copy(cid_hbm, cid_ref, sems.at[chunks]),
        pltpu.make_async_copy(order_hbm, order_ref, sems.at[chunks + 1]),
    ]
    loads = []
    for r in range(chunks):
        part = pl.ds(r * chunk, chunk)
        loads.append(pltpu.make_async_copy(emb_hbm.at[part], emb_ref.at[part], sems.at[r]))
    for copy in small + loads:
        copy.start()
    for copy in small:
        copy.wait()
    cid = cid_ref[...].astype(jnp.float32)
    column = jnp.transpose(jnp.broadcast_to(cid, (LANES, rows)))
    above = lax.broadcasted_iota(jnp.int32, (rows, LANES), 0)
    for j in range(rows // LANES):
        lanes = slice(j * LANES, (j + 1) * LANES)
        here = lax.broadcasted_iota(jnp.int32, (rows, LANES), 1) + j * LANES
        same = (column == cid[:, lanes]) & (above < here)
        place = jnp.sum(same.astype(jnp.float32), axis=0, keepdims=True)
        target_ref[:, lanes] = (cid[:, lanes] * CAP + place).astype(jnp.int32)
    code = order_ref[...] + 1
    high = jnp.broadcast_to((code >> 8).astype(jnp.float32), (META // 2, rows))
    low = jnp.broadcast_to((code & 255).astype(jnp.float32), (META // 2, rows))
    both = jnp.concatenate([high, low, jnp.zeros((LANES - META, rows), jnp.float32)], axis=0)
    unit_ref[:, width:] = jnp.transpose(both).astype(jnp.bfloat16)
    for r in range(chunks):
        part = pl.ds(r * chunk, chunk)
        loads[r].wait()
        e = emb_ref[part, :].astype(jnp.float32)
        scale = lax.rsqrt(jnp.sum(e * e, axis=1, keepdims=True) + 1e-06)
        unit_ref[part, :width] = (e * scale).astype(jnp.bfloat16)
    target = target_ref[...]
    me = lax.axis_index("owner") % PER_ROW
    segment = lax.broadcasted_iota(jnp.int32, (META, LANES), 1) // CAP
    for step in range(owners // PER_TILE):
        block = slice(step * PER_TILE, (step + 1) * PER_TILE)
        slot = lax.broadcasted_iota(jnp.int32, (TILE, rows), 0) + step * TILE
        place = (slot == target).astype(jnp.float32).astype(jnp.bfloat16)
        packed = jnp.dot(place, unit_ref[...], preferred_element_type=jnp.float32)
        for k in range(width // LANES):
            part = packed[:, k * LANES : (k + 1) * LANES].astype(jnp.bfloat16)
            out_ref[block, k * CAP : (k + 1) * CAP, :] = part.reshape(PER_TILE, CAP, LANES)
        ranks = jnp.transpose(packed[:, width:])[:META, :]
        for t in range(PER_TILE // PER_ROW):
            tile = ranks[:, t * LANES : (t + 1) * LANES]
            for q in range(PER_ROW):
                alone = jnp.where(segment == q, tile, 0.0)
                moved = pltpu.roll(alone, (me + PER_ROW - q) % PER_ROW * CAP, 1)
                out_ref[step * PER_TILE + t * PER_ROW + q, width // LANES * CAP :, :] = moved.astype(
                    jnp.bfloat16
                )


def pack(embeddings, cid, order, owners):
    rows, width = embeddings.shape
    return pl.pallas_call(
        pack_kernel,
        out_shape=(
            jax.ShapeDtypeStruct((owners, width // LANES * CAP + META, LANES), jnp.bfloat16),
            jax.ShapeDtypeStruct((1, rows), jnp.int32),
        ),
        in_specs=[pl.BlockSpec(memory_space=pl.ANY)] * 3,
        out_specs=(pl.BlockSpec(memory_space=pltpu.VMEM),) * 2,
        scratch_shapes=[
            pltpu.VMEM((rows, width), jnp.bfloat16),
            pltpu.VMEM((1, rows), jnp.int32),
            pltpu.VMEM((1, rows), jnp.int32),
            pltpu.VMEM((rows, width + LANES), jnp.bfloat16),
            pltpu.SemaphoreType.DMA((rows // 128 + 2,)),
        ],
        compiler_params=pltpu.CompilerParams(vmem_limit_bytes=32 * 2**20),
        name="pack_rows",
    )(embeddings, cid, order)


def rank_row(x_ref, group):
    meta = x_ref.shape[1] - META
    tiles = x_ref[group * PER_ROW : (group + 1) * PER_ROW, meta:, :].astype(jnp.float32)
    both = jnp.sum(tiles, axis=0)
    code = both[: META // 2] * 256.0 + both[META // 2 :]
    return jnp.where(code == 0.0, EMPTY, code)


def as_column(row):
    return jnp.transpose(jnp.broadcast_to(row[:1], (LANES, LANES)))


def rows_of(x_ref, first, count):
    block = slice(first // CAP, (first + count) // CAP)
    columns = (x_ref.shape[1] - META) // CAP
    parts = [x_ref[block, k * CAP : (k + 1) * CAP, :].reshape(count, LANES) for k in range(columns)]
    return jnp.concatenate(parts, axis=1)


def compare(x, y, first, start, column_ref, row_ref, rows_ref, across):
    sims = lax.dot_general(x, y, (((1,), (1,)), ((), ())), preferred_element_type=jnp.float32)
    some = slice(first, first + x.shape[0])
    column = column_ref[some, :]
    best = rows_ref[some, :]
    for j in range(y.shape[0] // LANES):
        s = sims[:, j * LANES : (j + 1) * LANES]
        earlier = row_ref[:1, start + j * LANES : start + (j + 1) * LANES] < column
        best = jnp.maximum(best, jnp.where(earlier, s, -1.0))
        if across[j] is not None:
            later = jnp.where(earlier, -1.0, s)
            across[j] = jnp.maximum(across[j], jnp.max(later.reshape(-1, 8, LANES), axis=0))
    rows_ref[some, :] = best


def lowest():
    return jnp.full((8, LANES), -1.0, jnp.float32)


def own_kernel(x_ref, out_ref, column_ref, row_ref, rows_ref, columns_ref):
    count = x_ref.shape[0] * CAP
    rows_ref[...] = jnp.full(rows_ref.shape, -1.0, jnp.float32)
    for g in range(count // LANES):
        lanes = slice(g * LANES, (g + 1) * LANES)
        row = rank_row(x_ref, g)
        row_ref[:, lanes] = row
        column_ref[lanes, :] = as_column(row)
    per = TILE // LANES
    for start in range(0, count, TILE):
        y = rows_of(x_ref, start, TILE)
        across = [lowest() for _ in range(per)]
        for first in range(0, start, PART):
            x = rows_of(x_ref, first, PART)
            compare(x, y, first, start, column_ref, row_ref, rows_ref, across)
        half = per // 2
        x = rows_of(x_ref, start, TILE // 2)
        some = [None] * half + across[half:]
        compare(x, y, start, start, column_ref, row_ref, rows_ref, some)
        across[half:] = some[half:]
        middle = start + TILE // 2
        x = rows_of(x_ref, middle, TILE // 2)
        compare(x, x, middle, middle, column_ref, row_ref, rows_ref, [None] * half)
        for j in range(per):
            columns_ref[:, start + j * LANES : start + (j + 1) * LANES] = across[j]
    for g in range(count // LANES):
        a = slice(g * LANES, (g + 1) * LANES)
        best = jnp.max(jnp.transpose(rows_ref[a, :]), axis=0, keepdims=True)
        best = jnp.maximum(best, jnp.max(columns_ref[:, a], axis=0, keepdims=True))
        out_ref[:, a] = jnp.broadcast_to(best, (8, LANES))


def own_pairs(x, width):
    owners = x.shape[0]
    count = owners * CAP
    return pl.pallas_call(
        own_kernel,
        out_shape=jax.ShapeDtypeStruct((8, count), jnp.float32),
        in_specs=[pl.BlockSpec(memory_space=pltpu.VMEM)],
        out_specs=pl.BlockSpec(memory_space=pltpu.VMEM),
        scratch_shapes=[
            pltpu.VMEM((count, LANES), jnp.float32),
            pltpu.VMEM((8, count), jnp.float32),
            pltpu.VMEM((count, LANES), jnp.float32),
            pltpu.VMEM((8, count), jnp.float32),
        ],
        compiler_params=pltpu.CompilerParams(vmem_limit_bytes=24 * 2**20),
        cost_estimate=pl.CostEstimate(
            flops=count * (count + TILE) * width, bytes_accessed=2 * count * width, transcendentals=0
        ),
        name="own_pairs",
    )(x)


def cross_kernel(x_ref, y_ref, own_ref, out_ref, column_ref, row_ref, rows_ref, columns_ref):
    core = lax.axis_index("split")
    count = x_ref.shape[0] * CAP
    half = count // 2
    rows_ref[...] = jnp.full(rows_ref.shape, -1.0, jnp.float32)

    def pairs(all_ref, some_ref):
        for g in range(count // LANES):
            column_ref[g * LANES : (g + 1) * LANES, :] = as_column(rank_row(all_ref, g))
        for g in range(half // LANES):
            row_ref[:, g * LANES : (g + 1) * LANES] = rank_row(some_ref, g)
        for start in range(0, half, TILE):
            y = rows_of(some_ref, start, TILE)
            across = [lowest() for _ in range(TILE // LANES)]
            for first in range(0, count, PART):
                x = rows_of(all_ref, first, PART)
                compare(x, y, first, start, column_ref, row_ref, rows_ref, across)
            for j, best in enumerate(across):
                columns_ref[:, start + j * LANES : start + (j + 1) * LANES] = best

    @pl.when(core == 0)
    def _():
        pairs(x_ref, y_ref.at[: half // CAP])

    @pl.when(core != 0)
    def _():
        pairs(y_ref, x_ref.at[half // CAP :])

    parity = lax.broadcasted_iota(jnp.int32, (8, LANES), 0) % 2
    groups = count // LANES
    nothing = jnp.full((1, LANES), -1.0, jnp.float32)
    for g in range(groups):
        a = slice(g * LANES, (g + 1) * LANES)
        from_all = jnp.max(jnp.transpose(rows_ref[a, :]), axis=0, keepdims=True)
        b = slice(g % (groups // 2) * LANES, (g % (groups // 2) + 1) * LANES)
        from_half = jnp.max(columns_ref[:, b], axis=0, keepdims=True)
        low, high = (from_half, nothing) if g < groups // 2 else (nothing, from_half)
        mine = jnp.maximum(own_ref[:1, a], jnp.where(core == 0, from_all, high))
        theirs = jnp.where(core == 0, low, from_all)
        out_ref[g * 8 : (g + 1) * 8, :] = jnp.where(
            parity == core, jnp.broadcast_to(mine, (8, LANES)), jnp.broadcast_to(theirs, (8, LANES))
        )


def cross_pairs(x, y, own, width):
    owners = x.shape[0]
    count = owners * CAP
    return pl.pallas_call(
        cross_kernel,
        out_shape=jax.ShapeDtypeStruct((count // LANES * 8, LANES), jnp.float32),
        in_specs=[pl.BlockSpec(memory_space=pltpu.VMEM)] * 3,
        out_specs=pl.BlockSpec(memory_space=pltpu.VMEM),
        scratch_shapes=[
            pltpu.VMEM((count, LANES), jnp.float32),
            pltpu.VMEM((8, count // 2), jnp.float32),
            pltpu.VMEM((count, LANES), jnp.float32),
            pltpu.VMEM((8, count // 2), jnp.float32),
        ],
        compiler_params=pltpu.CompilerParams(vmem_limit_bytes=24 * 2**20),
        cost_estimate=pl.CostEstimate(
            flops=count * count * width, bytes_accessed=3 * count * width, transcendentals=0
        ),
        name="cross_pairs",
    )(x, y, own)


def pick_kernel(recv_ref, target_ref, out_ref):
    pairs = recv_ref.shape[0]
    owners = pairs // 2
    best = jnp.maximum(
        recv_ref[pl.ds(0, owners, stride=2), :], recv_ref[pl.ds(1, owners, stride=2), :]
    )
    target = target_ref[...]
    rows = target.shape[1]
    cid = target >> 5
    slot = (target & (CAP - 1)) + lax.axis_index("owner") % PER_ROW * CAP
    chosen = lax.broadcasted_iota(jnp.int32, (owners, rows), 0) == cid
    chosen = chosen.astype(jnp.float32).astype(jnp.bfloat16)
    total = jnp.zeros((LANES, rows), jnp.float32)
    rest = best
    for _ in range(3):
        piece = rest.astype(jnp.bfloat16)
        rest = rest - piece.astype(jnp.float32)
        total += lax.dot_general(
            piece, chosen, (((0,), (0,)), ((), ())), preferred_element_type=jnp.float32
        )
    mine = lax.broadcasted_iota(jnp.int32, (LANES, rows), 0) == slot
    out_ref[...] = jnp.sum(jnp.where(mine, total, 0.0), axis=0, keepdims=True)


def pick(recv, target):
    return pl.pallas_call(
        pick_kernel,
        out_shape=jax.ShapeDtypeStruct(target.shape, jnp.float32),
        in_specs=[pl.BlockSpec(memory_space=pltpu.VMEM)] * 2,
        out_specs=pl.BlockSpec(memory_space=pltpu.VMEM),
        compiler_params=pltpu.CompilerParams(vmem_limit_bytes=8 * 2**20),
        name="pick_results",
    )(recv, target)


def shards(embeddings, cluster, order):
    owners = lax.axis_size("owner")
    rows, width = embeddings.shape
    packed, target = pack(embeddings, cluster.reshape(1, rows), order.reshape(1, rows), owners)
    mine = lax.all_to_all(packed, "owner", split_axis=0, concat_axis=0, tiled=True)
    theirs = lax.ppermute(mine, "split", [(0, 1), (1, 0)])
    own = own_pairs(mine, width)
    best = cross_pairs(mine, theirs, own, width)
    returned = lax.all_to_all(best, ("owner", "split"), split_axis=0, concat_axis=0, tiled=True)
    return pick(returned, target).reshape(rows)


def solution(mesh):
    return jax.shard_map(
        shards,
        mesh=mesh,
        in_specs=(P(("owner", "split"), None), P(("owner", "split"), None), P(("owner", "split"))),
        out_specs=P(("owner", "split")),
        check_vma=False,
    )
```

time: 106 us -> 101 us (0.953)
  Pallas kernels: 21.7 us -> 15.2 us
  waiting for transfers between devices: 0.01 us -> 1.87 us
    pallas_call x1, Pallas kernels: 8.74 us -> 5.26 us  [cross_pairs(): pl.pallas_call(cross_kernel, out_shape=jax.ShapeDtypeStruct((count // LAN...]
    pallas_call x1, Pallas kernels: 8.32 us -> 5.29 us  [own_pairs(): pl.pallas_call(own_kernel, out_shape=jax.ShapeDtypeStruct((8, count), jnp...]
    ppermute x1, waiting for transfers between devices: 0.01 us -> 1.87 us  [shards(): theirs = lax.ppermute(mine, 'split', [(0, 1), (1, 0)])]
  transfers between devices with their start and end apart: 1 -> 1, of which waited for: 0 -> 1; matrix products, arithmetic and copies ran while one was open for 0% -> 0% of each run, Pallas kernels for 8% -> 5%
where the time goes in v3:
time: 101 us
  blocking collectives  79.3 us (79%)
  Pallas kernels  15.2 us (15%)
  local copies, waits for them, and re-layouts  2.59 us (3%)
  starting transfers between devices  2.22 us (2%)
  waiting for transfers between devices  1.87 us (2%)
    all_to_all x1, blocking collectives, shards(): lax.all_to_all(packed, 'owner', split_axis=0, concat_axis=0, tiled=True)  66 us
    all_to_all x1, blocking collectives, shards(): lax.all_to_all(best, ('owner', 'split'), split_axis=0, concat_axis=0, til...  13.3 us
    pallas_call x1, Pallas kernels, own_pairs(): pl.pallas_call(own_kernel, out_shape=jax.ShapeDtypeStruct((8, count), jnp...  5.29 us
    pallas_call x1, Pallas kernels, cross_pairs(): pl.pallas_call(cross_kernel, out_shape=jax.ShapeDtypeStruct((count // LAN...  5.26 us
    pallas_call x1, Pallas kernels, pack(): pl.pallas_call(pack_kernel, out_shape=(jax.ShapeDtypeStruct((owners, widt...  3.8 us
    unnamed x6, local copies, waits for them, and re-layouts  2.59 us
    ppermute x1, starting transfers between devices, shards(): theirs = lax.ppermute(mine, 'split', [(0, 1), (1, 0)])  2.22 us
  transfers between devices with their start and end apart: 1, of which 1 were waited for; matrix products, arithmetic and copies ran while one was open for 0% of the time, Pallas kernels for 5%

profile of v3, /device:TPU:1, one launch (start us, length us, event | category | flops | bytes accessed | tf_op | source)
XLA Modules:
  0.0 101.2 jit_solution(3328857483437305718)
XLA Ops:
  0.0 0.0 copy-start
  0.0 1.2 %copy-done = bf16[512,1024]{1,0:T(8,128)(2,1)S(1)} copy-done((bf16[512,1024]{1,0:T(8,128)(2,1)S(1)}, bf16[512,1024]{1,0:T(8,128)(2,1)}, u32[]{:S(2)}) %copy-start) | copy-done | bytes 1048600
  1.2 0.0 copy-start.1
  1.2 0.7 copy-done.1
  1.9 0.0 copy-start.2
  1.9 0.7 copy-done.2
  2.6 3.8 %pack_rows.1 = (bf16[64,272,128]{2,1,0:T(8,128)(2,1)S(1)}, s32[1,512]{1,0:T(1,128)S(1)}) custom-call(bf16[512,1024]{1,0:T(8,128)(2,1)S(1)} %copy-done, s32[1,512]{1,0:T(1,128)S(1)} %bitcast.9, s32[1,512]{1,0:T(1,128)S(1)} %bitcast.10), custom_call_target="tpu_custom_call" | custom-call | tf_op jit(solution)/shard_map/pack_rows/pallas_call | solution.py:80
  6.4 66.0 %all_to_all.16.x_ref = bf16[64,272,128]{2,1,0:T(8,128)(2,1)S(1)} all-to-all(bf16[64,272,128]{2,1,0:T(8,128)(2,1)S(1)} %get-tuple-element.7), channel_id=1, replica_groups=mesh['owner'=64,'split'=2] {'owner'}, dimensions={0} | all-to-all | bytes 8912896 | tf_op jit(solution)/shard_map/all_to_all | solution.py:297
  72.4 2.2 %collective-permute-start = (bf16[64,272,128]{2,1,0:T(8,128)(2,1)S(1)}, bf16[64,272,128]{2,1,0:T(8,128)(2,1)S(1)}, u32[]{:S(2)}, u32[]{:S(2)}) collective-permute-start(bf16[64,272,128]{2,1,0:T(8,128)(2,1)S(1)} %all_to_all.16.x_ref), channel_id=1, source_target_pairs={{0,1},{1,0},{2,3},{3,2},{4,5},{5,4},{6,7},{7,6},{8,9},{9,8},{10,11... | collective-permute-start | bytes 13369352 | tf_op jit(solution)/shard_map/ppermute | solution.py:298
  74.6 5.3 %own_pairs.1.own_ref = f32[8,2048]{1,0:T(8,128)S(1)} custom-call(bf16[64,272,128]{2,1,0:T(8,128)(2,1)S(1)} %all_to_all.16.x_ref), custom_call_target="tpu_custom_call" | custom-call | flops 5368709120 | bytes 4194304 | tf_op jit(solution)/shard_map/own_pairs/pallas_call | solution.py:173
  79.9 1.9 %collective-permute-done.y_ref = bf16[64,272,128]{2,1,0:T(8,128)(2,1)S(1)} collective-permute-done((bf16[64,272,128]{2,1,0:T(8,128)(2,1)S(1)}, bf16[64,272,128]{2,1,0:T(8,128)(2,1)S(1)}, u32[]{:S(2)}, u32[]{:S(2)}) %collective-permute-start) | collective-permute-done | bytes 4456480 | tf_op jit(solution)/shard_map/ppermute | solution.py:298
  81.8 5.3 %cross_pairs.1 = f32[128,128]{1,0:T(8,128)S(1)} custom-call(bf16[64,272,128]{2,1,0:T(8,128)(2,1)S(1)} %all_to_all.16.x_ref, bf16[64,272,128]{2,1,0:T(8,128)(2,1)S(1)} %collective-permute-done.y_ref, f32[8,2048]{1,0:T(8,128)S(1)} %own_pairs.1.own_ref), custom_call_target="tpu_custom_call" | custom-call | flops 4294967296 | bytes 6291456 | tf_op jit(solution)/shard_map/cross_pairs/pallas_call | solution.py:239
  87.0 13.3 %all_to_all.17 = f32[128,1,128]{2,1,0:T(1,128)S(1)} all-to-all(f32[128,1,128]{2,1,0:T(1,128)S(1)} %bitcast.8), channel_id=1, replica_groups=mesh['owner'=64,'split'=2] {'owner','split'}, dimensions={0} | all-to-all | bytes 131072 | tf_op jit(solution)/shard_map/all_to_all | solution.py:301
  100.4 0.9 pick_results.1
Async XLA Ops:
  0.0 1.2 %copy-start = (bf16[512,1024]{1,0:T(8,128)(2,1)S(1)}, bf16[512,1024]{1,0:T(8,128)(2,1)}, u32[]{:S(2)}) copy-start(bf16[512,1024]{1,0:T(8,128)(2,1)} %emb_hbm.1) | copy-start | bytes 3145732
  1.2 0.7 copy-start.1
  1.9 0.7 copy-start.2
  72.4 9.4 %collective-permute-start = (bf16[64,272,128]{2,1,0:T(8,128)(2,1)S(1)}, bf16[64,272,128]{2,1,0:T(8,128)(2,1)S(1)}, u32[]{:S(2)}, u32[]{:S(2)}) collective-permute-start(bf16[64,272,128]{2,1,0:T(8,128)(2,1)S(1)} %all_to_all.16.x_ref), channel_id=1, source_target_pairs={{0,1},{1,0},{2,3},{3,2},{4,5},{5,4},{6,7},{7,6},{8,9},{9,8},{10,11... | collective-permute-start | bytes 13369352 | tf_op jit(solution)/shard_map/ppermute | solution.py:298

commit v4 on v3

--- a/solution.py
+++ b/solution.py
@@ -8,7 +8,7 @@
 
 CAP = 32
 LANES = 128
-META = 16
+META = 8
 EMPTY = 262144.0
 TILE = 512
 PART = 512
@@ -16,40 +16,31 @@
 PER_ROW = LANES // CAP
 
 
-def pack_kernel(emb_hbm, cid_hbm, order_hbm, out_ref, target_ref, emb_ref, cid_ref, order_ref, unit_ref, sems):
+def pack_kernel(emb_ref, code_ref, out_ref, target_ref, unit_ref):
     rows, width = emb_ref.shape
     owners = out_ref.shape[0]
-    chunk = 128
-    chunks = rows // chunk
-    small = [
-        pltpu.make_async_copy(cid_hbm, cid_ref, sems.at[chunks]),
-        pltpu.make_async_copy(order_hbm, order_ref, sems.at[chunks + 1]),
-    ]
-    loads = []
-    for r in range(chunks):
-        part = pl.ds(r * chunk, chunk)
-        loads.append(pltpu.make_async_copy(emb_hbm.at[part], emb_ref.at[part], sems.at[r]))
-    for copy in small + loads:
-        copy.start()
-    for copy in small:
-        copy.wait()
-    cid = cid_ref[...].astype(jnp.float32)
+    code = code_ref[...]
+    cid = (code >> 16).astype(jnp.float32)
     column = jnp.transpose(jnp.broadcast_to(cid, (LANES, rows)))
-    above = lax.broadcasted_iota(jnp.int32, (rows, LANES), 0)
+    above = lax.broadcasted_iota(jnp.int32, (LANES, LANES), 0)
+    here = lax.broadcasted_iota(jnp.int32, (LANES, LANES), 1)
     for j in range(rows // LANES):
         lanes = slice(j * LANES, (j + 1) * LANES)
-        here = lax.broadcasted_iota(jnp.int32, (rows, LANES), 1) + j * LANES
-        same = (column == cid[:, lanes]) & (above < here)
-        place = jnp.sum(same.astype(jnp.float32), axis=0, keepdims=True)
+        place = jnp.zeros((1, LANES), jnp.float32)
+        for i in range(j + 1):
+            same = column[i * LANES : (i + 1) * LANES] == cid[:, lanes]
+            if i == j:
+                same = same & (above < here)
+            place += jnp.sum(jnp.where(same, 1.0, 0.0), axis=0, keepdims=True)
         target_ref[:, lanes] = (cid[:, lanes] * CAP + place).astype(jnp.int32)
-    code = order_ref[...] + 1
-    high = jnp.broadcast_to((code >> 8).astype(jnp.float32), (META // 2, rows))
-    low = jnp.broadcast_to((code & 255).astype(jnp.float32), (META // 2, rows))
+    rank = (code & 65535) + 1
+    high = jnp.broadcast_to((rank >> 8).astype(jnp.float32), (META // 2, rows))
+    low = jnp.broadcast_to((rank & 255).astype(jnp.float32), (META // 2, rows))
     both = jnp.concatenate([high, low, jnp.zeros((LANES - META, rows), jnp.float32)], axis=0)
     unit_ref[:, width:] = jnp.transpose(both).astype(jnp.bfloat16)
-    for r in range(chunks):
-        part = pl.ds(r * chunk, chunk)
-        loads[r].wait()
+    chunk = 128
+    for r in range(rows // chunk):
+        part = slice(r * chunk, (r + 1) * chunk)
         e = emb_ref[part, :].astype(jnp.float32)
         scale = lax.rsqrt(jnp.sum(e * e, axis=1, keepdims=True) + 1e-06)
         unit_ref[part, :width] = (e * scale).astype(jnp.bfloat16)
@@ -58,8 +49,8 @@
     segment = lax.broadcasted_iota(jnp.int32, (META, LANES), 1) // CAP
     for step in range(owners // PER_TILE):
         block = slice(step * PER_TILE, (step + 1) * PER_TILE)
-        slot = lax.broadcasted_iota(jnp.int32, (TILE, rows), 0) + step * TILE
-        place = (slot == target).astype(jnp.float32).astype(jnp.bfloat16)
+        slot = lax.broadcasted_iota(jnp.int32, (TILE, rows), 0)
+        place = jnp.where(slot == target - step * TILE, 1.0, 0.0).astype(jnp.bfloat16)
         packed = jnp.dot(place, unit_ref[...], preferred_element_type=jnp.float32)
         for k in range(width // LANES):
             part = packed[:, k * LANES : (k + 1) * LANES].astype(jnp.bfloat16)
@@ -75,7 +66,7 @@
                 )
 
 
-def pack(embeddings, cid, order, owners):
+def pack(embeddings, code, owners):
     rows, width = embeddings.shape
     return pl.pallas_call(
         pack_kernel,
@@ -83,26 +74,20 @@
             jax.ShapeDtypeStruct((owners, width // LANES * CAP + META, LANES), jnp.bfloat16),
             jax.ShapeDtypeStruct((1, rows), jnp.int32),
         ),
-        in_specs=[pl.BlockSpec(memory_space=pl.ANY)] * 3,
+        in_specs=[pl.BlockSpec(memory_space=pltpu.VMEM)] * 2,
         out_specs=(pl.BlockSpec(memory_space=pltpu.VMEM),) * 2,
-        scratch_shapes=[
-            pltpu.VMEM((rows, width), jnp.bfloat16),
-            pltpu.VMEM((1, rows), jnp.int32),
-            pltpu.VMEM((1, rows), jnp.int32),
-            pltpu.VMEM((rows, width + LANES), jnp.bfloat16),
-            pltpu.SemaphoreType.DMA((rows // 128 + 2,)),
-        ],
-        compiler_params=pltpu.CompilerParams(vmem_limit_bytes=32 * 2**20),
+        scratch_shapes=[pltpu.VMEM((rows, width + LANES), jnp.bfloat16)],
+        compiler_params=pltpu.CompilerParams(vmem_limit_bytes=24 * 2**20),
         name="pack_rows",
-    )(embeddings, cid, order)
+    )(embeddings, code)
 
 
 def rank_row(x_ref, group):
     meta = x_ref.shape[1] - META
     tiles = x_ref[group * PER_ROW : (group + 1) * PER_ROW, meta:, :].astype(jnp.float32)
     both = jnp.sum(tiles, axis=0)
-    code = both[: META // 2] * 256.0 + both[META // 2 :]
-    return jnp.where(code == 0.0, EMPTY, code)
+    code = both[:1] * 256.0 + both[META // 2 : META // 2 + 1]
+    return jnp.broadcast_to(jnp.where(code == 0.0, EMPTY, code), (8, LANES))
 
 
 def as_column(row):
@@ -293,7 +278,9 @@
 def shards(embeddings, cluster, order):
     owners = lax.axis_size("owner")
     rows, width = embeddings.shape
-    packed, target = pack(embeddings, cluster.reshape(1, rows), order.reshape(1, rows), owners)
+    cid, rank = lax.optimization_barrier((cluster.reshape(1, rows), order.reshape(1, rows)))
+    code = cid * 65536 + rank
+    packed, target = pack(embeddings, code, owners)
     mine = lax.all_to_all(packed, "owner", split_axis=0, concat_axis=0, tiled=True)
     theirs = lax.ppermute(mine, "split", [(0, 1), (1, 0)])
     own = own_pairs(mine, width)

time: 101 us -> 98.8 us (0.978)
  local copies, waits for them, and re-layouts: 2.59 us -> 1.22 us
    unnamed x6 -> x2, local copies, waits for them, and re-layouts: 2.59 us -> 1.22 us
    all_to_all x1, blocking collectives: 66 us -> 64.9 us  [shards(): lax.all_to_all(packed, 'owner', split_axis=0, concat_axis=0, tiled=True)]
where the time goes in v4:
time: 98.8 us; the launch traced here: 98.6 us
  blocking collectives  78.3 us (79%)
  Pallas kernels  14.8 us (15%)
  starting transfers between devices  1.91 us (2%)
  waiting for transfers between devices  1.67 us (2%)
  local copies, waits for them, and re-layouts  1.22 us (1%)
    all_to_all x1, blocking collectives, shards(): lax.all_to_all(packed, 'owner', split_axis=0, concat_axis=0, tiled=True)  64.9 us
    all_to_all x1, blocking collectives, shards(): lax.all_to_all(best, ('owner', 'split'), split_axis=0, concat_axis=0, til...  13.3 us
    pallas_call x1, Pallas kernels, own_pairs(): pl.pallas_call(own_kernel, out_shape=jax.ShapeDtypeStruct((8, count), jnp...  5.3 us
    pallas_call x1, Pallas kernels, cross_pairs(): pl.pallas_call(cross_kernel, out_shape=jax.ShapeDtypeStruct((count // LAN...  5.26 us
    pallas_call x1, Pallas kernels, pack(): pl.pallas_call(pack_kernel, out_shape=(jax.ShapeDtypeStruct((owners, widt...  3.35 us
  transfers between devices with their start and end apart: 1, of which 1 were waited for; matrix products, arithmetic and copies ran while one was open for 0% of the time, Pallas kernels for 5%

profile of v4, /device:TPU:1, one launch (start us, length us, event | category | flops | bytes accessed | tf_op | source)
XLA Modules:
  0.0 98.6 jit_solution(7939019042289372189)
XLA Ops:
  0.0 0.7 multiply_add_fusion.code_ref
  0.7 0.0 copy-start
  0.7 1.2 %copy-done = bf16[512,1024]{1,0:T(8,128)(2,1)S(1)} copy-done((bf16[512,1024]{1,0:T(8,128)(2,1)S(1)}, bf16[512,1024]{1,0:T(8,128)(2,1)}, u32[]{:S(2)}) %copy-start) | copy-done | bytes 1048600
  1.9 3.3 %pack_rows.1 = (bf16[64,264,128]{2,1,0:T(8,128)(2,1)S(1)}, s32[1,512]{1,0:T(1,128)S(1)}) custom-call(bf16[512,1024]{1,0:T(8,128)(2,1)S(1)} %copy-done, s32[1,512]{1,0:T(1,128)S(1)} %multiply_add_fusion.code_ref), custom_call_target="tpu_custom_call" | custom-call | tf_op jit(solution)/shard_map/pack_rows/pallas_call | solution.py:71
  5.3 64.9 %all_to_all.16.x_ref = bf16[64,264,128]{2,1,0:T(8,128)(2,1)S(1)} all-to-all(bf16[64,264,128]{2,1,0:T(8,128)(2,1)S(1)} %get-tuple-element.11), channel_id=1, replica_groups=mesh['owner'=64,'split'=2] {'owner'}, dimensions={0} | all-to-all | bytes 8650752 | tf_op jit(solution)/shard_map/all_to_all | solution.py:284
  70.2 1.9 %collective-permute-start = (bf16[64,264,128]{2,1,0:T(8,128)(2,1)S(1)}, bf16[64,264,128]{2,1,0:T(8,128)(2,1)S(1)}, u32[]{:S(2)}, u32[]{:S(2)}) collective-permute-start(bf16[64,264,128]{2,1,0:T(8,128)(2,1)S(1)} %all_to_all.16.x_ref), channel_id=1, source_target_pairs={{0,1},{1,0},{2,3},{3,2},{4,5},{5,4},{6,7},{7,6},{8,9},{9,8},{10,11... | collective-permute-start | bytes 12976136 | tf_op jit(solution)/shard_map/ppermute | solution.py:285
  72.1 5.3 %own_pairs.1.own_ref = f32[8,2048]{1,0:T(8,128)S(1)} custom-call(bf16[64,264,128]{2,1,0:T(8,128)(2,1)S(1)} %all_to_all.16.x_ref), custom_call_target="tpu_custom_call" | custom-call | flops 5368709120 | bytes 4194304 | tf_op jit(solution)/shard_map/own_pairs/pallas_call | solution.py:158
  77.4 1.7 %collective-permute-done.y_ref = bf16[64,264,128]{2,1,0:T(8,128)(2,1)S(1)} collective-permute-done((bf16[64,264,128]{2,1,0:T(8,128)(2,1)S(1)}, bf16[64,264,128]{2,1,0:T(8,128)(2,1)S(1)}, u32[]{:S(2)}, u32[]{:S(2)}) %collective-permute-start) | collective-permute-done | bytes 4325408 | tf_op jit(solution)/shard_map/ppermute | solution.py:285
  79.1 5.3 %cross_pairs.1 = f32[128,128]{1,0:T(8,128)S(1)} custom-call(bf16[64,264,128]{2,1,0:T(8,128)(2,1)S(1)} %all_to_all.16.x_ref, bf16[64,264,128]{2,1,0:T(8,128)(2,1)S(1)} %collective-permute-done.y_ref, f32[8,2048]{1,0:T(8,128)S(1)} %own_pairs.1.own_ref), custom_call_target="tpu_custom_call" | custom-call | flops 4294967296 | bytes 6291456 | tf_op jit(solution)/shard_map/cross_pairs/pallas_call | solution.py:224
  84.4 13.3 %all_to_all.17 = f32[128,1,128]{2,1,0:T(1,128)S(1)} all-to-all(f32[128,1,128]{2,1,0:T(1,128)S(1)} %bitcast.8), channel_id=1, replica_groups=mesh['owner'=64,'split'=2] {'owner','split'}, dimensions={0} | all-to-all | bytes 131072 | tf_op jit(solution)/shard_map/all_to_all | solution.py:288
  97.7 0.9 pick_results.1
Async XLA Ops:
  0.7 1.2 %copy-start = (bf16[512,1024]{1,0:T(8,128)(2,1)S(1)}, bf16[512,1024]{1,0:T(8,128)(2,1)}, u32[]{:S(2)}) copy-start(bf16[512,1024]{1,0:T(8,128)(2,1)} %emb_ref.1) | copy-start | bytes 3145732
  70.2 8.9 %collective-permute-start = (bf16[64,264,128]{2,1,0:T(8,128)(2,1)S(1)}, bf16[64,264,128]{2,1,0:T(8,128)(2,1)S(1)}, u32[]{:S(2)}, u32[]{:S(2)}) collective-permute-start(bf16[64,264,128]{2,1,0:T(8,128)(2,1)S(1)} %all_to_all.16.x_ref), channel_id=1, source_target_pairs={{0,1},{1,0},{2,3},{3,2},{4,5},{5,4},{6,7},{7,6},{8,9},{9,8},{10,11... | collective-permute-start | bytes 12976136 | tf_op jit(solution)/shard_map/ppermute | solution.py:285

commit v5 on v4

--- a/solution.py
+++ b/solution.py
@@ -174,43 +174,70 @@
     )(x)
 
 
-def cross_kernel(x_ref, y_ref, own_ref, out_ref, column_ref, row_ref, rows_ref, columns_ref):
+def cross(all_ref, some_ref, column_ref, row_ref, rows_ref, columns_ref):
+    count = all_ref.shape[0] * CAP
+    rows_ref[...] = jnp.full(rows_ref.shape, -1.0, jnp.float32)
+    for g in range(count // LANES):
+        lanes = slice(g * LANES, (g + 1) * LANES)
+        column_ref[lanes, :] = as_column(rank_row(all_ref, g))
+        row_ref[:, lanes] = rank_row(some_ref, g)
+    for start in range(0, count, TILE):
+        y = rows_of(some_ref, start, TILE)
+        lanes = [slice(start + j * LANES, start + (j + 1) * LANES) for j in range(TILE // LANES)]
+        across = [columns_ref[:, part] for part in lanes]
+        for first in range(0, count, PART):
+            x = rows_of(all_ref, first, PART)
+            compare(x, y, first, start, column_ref, row_ref, rows_ref, across)
+        for part, best in zip(lanes, across):
+            columns_ref[:, part] = best
+
+
+def first_kernel(x_ref, y_ref, rows_out, columns_out, column_ref, row_ref, rows_ref):
     core = lax.axis_index("split")
-    count = x_ref.shape[0] * CAP
-    half = count // 2
-    rows_ref[...] = jnp.full(rows_ref.shape, -1.0, jnp.float32)
-
-    def pairs(all_ref, some_ref):
-        for g in range(count // LANES):
-            column_ref[g * LANES : (g + 1) * LANES, :] = as_column(rank_row(all_ref, g))
-        for g in range(half // LANES):
-            row_ref[:, g * LANES : (g + 1) * LANES] = rank_row(some_ref, g)
-        for start in range(0, half, TILE):
-            y = rows_of(some_ref, start, TILE)
-            across = [lowest() for _ in range(TILE // LANES)]
-            for first in range(0, count, PART):
-                x = rows_of(all_ref, first, PART)
-                compare(x, y, first, start, column_ref, row_ref, rows_ref, across)
-            for j, best in enumerate(across):
-                columns_ref[:, start + j * LANES : start + (j + 1) * LANES] = best
+    half = y_ref.shape[0]
+    columns_out[...] = jnp.full(columns_out.shape, -1.0, jnp.float32)
 
     @pl.when(core == 0)
     def _():
-        pairs(x_ref, y_ref.at[: half // CAP])
+        cross(x_ref.at[:half], y_ref, column_ref, row_ref, rows_ref, columns_out)
 
     @pl.when(core != 0)
     def _():
-        pairs(y_ref, x_ref.at[half // CAP :])
+        cross(y_ref, x_ref.at[half:], column_ref, row_ref, rows_ref, columns_out)
+
+    for g in range(half * CAP // LANES):
+        a = slice(g * LANES, (g + 1) * LANES)
+        best = jnp.max(jnp.transpose(rows_ref[a, :]), axis=0, keepdims=True)
+        rows_out[:, a] = jnp.broadcast_to(best, (8, LANES))
+
+
+def second_kernel(
+    x_ref, y_ref, z_ref, own_ref, first_ref, columns_in, out_ref, column_ref, row_ref, rows_ref, columns_ref
+):
+    core = lax.axis_index("split")
+    half = y_ref.shape[0]
+    columns_ref[...] = columns_in[...]
+
+    @pl.when(core == 0)
+    def _():
+        cross(x_ref.at[half:], y_ref, column_ref, row_ref, rows_ref, columns_ref)
+
+    @pl.when(core != 0)
+    def _():
+        cross(z_ref, x_ref.at[half:], column_ref, row_ref, rows_ref, columns_ref)
 
     parity = lax.broadcasted_iota(jnp.int32, (8, LANES), 0) % 2
-    groups = count // LANES
+    groups = half * CAP // LANES
     nothing = jnp.full((1, LANES), -1.0, jnp.float32)
-    for g in range(groups):
+    for g in range(2 * groups):
         a = slice(g * LANES, (g + 1) * LANES)
-        from_all = jnp.max(jnp.transpose(rows_ref[a, :]), axis=0, keepdims=True)
-        b = slice(g % (groups // 2) * LANES, (g % (groups // 2) + 1) * LANES)
+        b = slice(g % groups * LANES, (g % groups + 1) * LANES)
+        if g < groups:
+            from_all = first_ref[:1, b]
+        else:
+            from_all = jnp.max(jnp.transpose(rows_ref[b, :]), axis=0, keepdims=True)
         from_half = jnp.max(columns_ref[:, b], axis=0, keepdims=True)
-        low, high = (from_half, nothing) if g < groups // 2 else (nothing, from_half)
+        low, high = (from_half, nothing) if g < groups else (nothing, from_half)
         mine = jnp.maximum(own_ref[:1, a], jnp.where(core == 0, from_all, high))
         theirs = jnp.where(core == 0, low, from_all)
         out_ref[g * 8 : (g + 1) * 8, :] = jnp.where(
@@ -218,26 +245,36 @@
         )
 
 
-def cross_pairs(x, y, own, width):
-    owners = x.shape[0]
-    count = owners * CAP
+def cross_pairs(x, y, z, own, width):
+    half = y.shape[0] * CAP
+    cost = pl.CostEstimate(flops=2 * half * half * width, bytes_accessed=4 * half * width, transcendentals=0)
+    vmem = pl.BlockSpec(memory_space=pltpu.VMEM)
+    scratch = [
+        pltpu.VMEM((half, LANES), jnp.float32),
+        pltpu.VMEM((8, half), jnp.float32),
+        pltpu.VMEM((half, LANES), jnp.float32),
+    ]
+    params = pltpu.CompilerParams(vmem_limit_bytes=24 * 2**20)
+    first, columns = pl.pallas_call(
+        first_kernel,
+        out_shape=(jax.ShapeDtypeStruct((8, half), jnp.float32),) * 2,
+        in_specs=[vmem] * 2,
+        out_specs=(vmem,) * 2,
+        scratch_shapes=scratch,
+        compiler_params=params,
+        cost_estimate=cost,
+        name="cross_first",
+    )(x, y)
     return pl.pallas_call(
-        cross_kernel,
-        out_shape=jax.ShapeDtypeStruct((count // LANES * 8, LANES), jnp.float32),
-        in_specs=[pl.BlockSpec(memory_space=pltpu.VMEM)] * 3,
-        out_specs=pl.BlockSpec(memory_space=pltpu.VMEM),
-        scratch_shapes=[
-            pltpu.VMEM((count, LANES), jnp.float32),
-            pltpu.VMEM((8, count // 2), jnp.float32),
-            pltpu.VMEM((count, LANES), jnp.float32),
-            pltpu.VMEM((8, count // 2), jnp.float32),
-        ],
-        compiler_params=pltpu.CompilerParams(vmem_limit_bytes=24 * 2**20),
-        cost_estimate=pl.CostEstimate(
-            flops=count * count * width, bytes_accessed=3 * count * width, transcendentals=0
-        ),
-        name="cross_pairs",
-    )(x, y, own)
+        second_kernel,
+        out_shape=jax.ShapeDtypeStruct((2 * half // LANES * 8, LANES), jnp.float32),
+        in_specs=[vmem] * 6,
+        out_specs=vmem,
+        scratch_shapes=scratch + [pltpu.VMEM((8, half), jnp.float32)],
+        compiler_params=params,
+        cost_estimate=cost,
+        name="cross_second",
+    )(x, y, z, own, first, columns)
 
 
 def pick_kernel(recv_ref, target_ref, out_ref):
@@ -282,9 +319,12 @@
     code = cid * 65536 + rank
     packed, target = pack(embeddings, code, owners)
     mine = lax.all_to_all(packed, "owner", split_axis=0, concat_axis=0, tiled=True)
-    theirs = lax.ppermute(mine, "split", [(0, 1), (1, 0)])
+    swap = [(0, 1), (1, 0)]
+    half = owners // 2
+    first = lax.ppermute(mine[:half], "split", swap)
+    second = lax.ppermute(mine[half:], "split", swap)
     own = own_pairs(mine, width)
-    best = cross_pairs(mine, theirs, own, width)
+    best = cross_pairs(mine, first, second, own, width)
     returned = lax.all_to_all(best, ("owner", "split"), split_axis=0, concat_axis=0, tiled=True)
     return pick(returned, target).reshape(rows)
 

time: 98.8 us -> 98 us (level)
  waiting for transfers between devices: 1.67 us -> 0.01 us
    ppermute x1 -> x2, waiting for transfers between devices: 1.67 us -> 0.01 us  [the longest x1 0.01 us: shards(): first = lax.ppermute(mine[:half], 'split', swap)]
    pallas_call x1 -> x2, Pallas kernels: 5.26 us -> 5.53 us  [the longest x1 2.85 us: cross_pairs(): pl.pallas_call(first_kernel, out_shape=(jax.ShapeDtypeStruct((8, half), j...]
    ppermute x1 -> x2, starting transfers between devices: 1.91 us -> 2.09 us  [the longest x1 1.99 us: shards(): first = lax.ppermute(mine[:half], 'split', swap)]
  transfers between devices with their start and end apart: 1 -> 2, of which waited for: 1 -> 0; matrix products, arithmetic and copies ran while one was open for 0% -> 0% of each run, Pallas kernels for 5% -> 8%
where the time goes in v5:
time: 98 us; the launch traced here: 97.8 us
  blocking collectives  78.4 us (80%)
  Pallas kernels  15 us (15%)
  starting transfers between devices  2.09 us (2%)
  local copies, waits for them, and re-layouts  1.52 us (2%)
    all_to_all x1, blocking collectives, shards(): lax.all_to_all(packed, 'owner', split_axis=0, concat_axis=0, tiled=True)  64.9 us
    all_to_all x1, blocking collectives, shards(): lax.all_to_all(best, ('owner', 'split'), split_axis=0, concat_axis=0, til...  13.4 us
    pallas_call x1, Pallas kernels, own_pairs(): pl.pallas_call(own_kernel, out_shape=jax.ShapeDtypeStruct((8, count), jnp...  5.28 us
    pallas_call x1, Pallas kernels, pack(): pl.pallas_call(pack_kernel, out_shape=(jax.ShapeDtypeStruct((owners, widt...  3.35 us
    pallas_call x1, Pallas kernels, cross_pairs(): pl.pallas_call(first_kernel, out_shape=(jax.ShapeDtypeStruct((8, half), j...  2.85 us
    pallas_call x1, Pallas kernels, cross_pairs(): pl.pallas_call(second_kernel, out_shape=jax.ShapeDtypeStruct((2 * half //...  2.68 us
    ppermute x1, starting transfers between devices, shards(): first = lax.ppermute(mine[:half], 'split', swap)  1.99 us
  transfers between devices with their start and end apart: 2, of which 0 were waited for; matrix products, arithmetic and copies ran while one was open for 0% of the time, Pallas kernels for 8%

profile of v5, /device:TPU:1, one launch (start us, length us, event | category | flops | bytes accessed | tf_op | source)
XLA Modules:
  0.0 97.8 jit_solution(5159995594641914301)
XLA Ops:
  0.0 0.7 multiply_add_fusion.code_ref
  0.7 0.0 copy-start
  0.7 1.2 %copy-done = bf16[512,1024]{1,0:T(8,128)(2,1)S(1)} copy-done((bf16[512,1024]{1,0:T(8,128)(2,1)S(1)}, bf16[512,1024]{1,0:T(8,128)(2,1)}, u32[]{:S(2)}) %copy-start) | copy-done | bytes 1048600
  1.9 3.3 %pack_rows.1 = (bf16[64,264,128]{2,1,0:T(8,128)(2,1)S(1)}, s32[1,512]{1,0:T(1,128)S(1)}) custom-call(bf16[512,1024]{1,0:T(8,128)(2,1)S(1)} %copy-done, s32[1,512]{1,0:T(1,128)S(1)} %multiply_add_fusion.code_ref), custom_call_target="tpu_custom_call" | custom-call | tf_op jit(solution)/shard_map/pack_rows/pallas_call | solution.py:71
  5.3 64.9 %all_to_all.16.x_ref = bf16[64,264,128]{2,1,0:T(8,128)(2,1)S(1)} all-to-all(bf16[64,264,128]{2,1,0:T(8,128)(2,1)S(1)} %get-tuple-element.13), channel_id=1, replica_groups=mesh['owner'=64,'split'=2] {'owner'}, dimensions={0} | all-to-all | bytes 8650752 | tf_op jit(solution)/shard_map/all_to_all | solution.py:321
  70.2 0.3 fusion
  70.5 2.0 %collective-permute-start = (bf16[32,264,128]{2,1,0:T(8,128)(2,1)S(1)}, bf16[32,264,128]{2,1,0:T(8,128)(2,1)S(1)}, u32[]{:S(2)}, u32[]{:S(2)}) collective-permute-start(bf16[32,264,128]{2,1,0:T(8,128)(2,1)S(1)} %get-tuple-element.18), channel_id=1, source_target_pairs={{0,1},{1,0},{2,3},{3,2},{4,5},{5,4},{6,7},{7,6},{8,9},{9,8},{10,11... | collective-permute-start | bytes 6488072 | tf_op jit(solution)/shard_map/ppermute | solution.py:324
  72.5 0.1 collective-permute-start.1
  72.6 5.3 %own_pairs.1.own_ref = f32[8,2048]{1,0:T(8,128)S(1)} custom-call(bf16[64,264,128]{2,1,0:T(8,128)(2,1)S(1)} %all_to_all.16.x_ref), custom_call_target="tpu_custom_call" | custom-call | flops 5368709120 | bytes 4194304 | tf_op jit(solution)/shard_map/own_pairs/pallas_call | solution.py:158
  77.9 0.0 collective-permute-done.y_ref
  77.9 2.9 %cross_first.1 = (f32[8,1024]{1,0:T(8,128)S(1)}, f32[8,1024]{1,0:T(8,128)S(1)}) custom-call(bf16[64,264,128]{2,1,0:T(8,128)(2,1)S(1)} %all_to_all.16.x_ref, bf16[32,264,128]{2,1,0:T(8,128)(2,1)S(1)} %collective-permute-done.y_ref), custom_call_target="tpu_custom_call" | custom-call | flops 2147483648 | bytes 4194304 | tf_op jit(solution)/shard_map/cross_first/pallas_call | solution.py:258
  80.8 0.0 collective-permute-done.1.z_ref
  80.8 2.7 %cross_second.1 = f32[128,128]{1,0:T(8,128)S(1)} custom-call(bf16[64,264,128]{2,1,0:T(8,128)(2,1)S(1)} %all_to_all.16.x_ref, bf16[32,264,128]{2,1,0:T(8,128)(2,1)S(1)} %collective-permute-done.y_ref, bf16[32,264,128]{2,1,0:T(8,128)(2,1)S(1)} %collective-permute-done.1.z_ref, f32[8,2048]{1,0:T(8,128)S(1)} %own_pairs.1.own_ref, ...), custom_call_target="tpu_custom_call" | custom-call | flops 2147483648 | bytes 4194304 | tf_op jit(solution)/shard_map/cross_second/pallas_call | solution.py:268
  83.5 13.4 %all_to_all.17 = f32[128,1,128]{2,1,0:T(1,128)S(1)} all-to-all(f32[128,1,128]{2,1,0:T(1,128)S(1)} %bitcast.7), channel_id=1, replica_groups=mesh['owner'=64,'split'=2] {'owner','split'}, dimensions={0} | all-to-all | bytes 131072 | tf_op jit(solution)/shard_map/all_to_all | solution.py:328
  96.9 0.9 pick_results.1
Async XLA Ops:
  0.7 1.2 %copy-start = (bf16[512,1024]{1,0:T(8,128)(2,1)S(1)}, bf16[512,1024]{1,0:T(8,128)(2,1)}, u32[]{:S(2)}) copy-start(bf16[512,1024]{1,0:T(8,128)(2,1)} %emb_ref.1) | copy-start | bytes 3145732
  70.5 7.4 %collective-permute-start = (bf16[32,264,128]{2,1,0:T(8,128)(2,1)S(1)}, bf16[32,264,128]{2,1,0:T(8,128)(2,1)S(1)}, u32[]{:S(2)}, u32[]{:S(2)}) collective-permute-start(bf16[32,264,128]{2,1,0:T(8,128)(2,1)S(1)} %get-tuple-element.18), channel_id=1, source_target_pairs={{0,1},{1,0},{2,3},{3,2},{4,5},{5,4},{6,7},{7,6},{8,9},{9,8},{10,11... | collective-permute-start | bytes 6488072 | tf_op jit(solution)/shard_map/ppermute | solution.py:324
  72.5 8.3 %collective-permute-start.1 = (bf16[32,264,128]{2,1,0:T(8,128)(2,1)S(1)}, bf16[32,264,128]{2,1,0:T(8,128)(2,1)S(1)}, u32[]{:S(2)}, u32[]{:S(2)}) collective-permute-start(bf16[32,264,128]{2,1,0:T(8,128)(2,1)S(1)} %get-tuple-element.17), channel_id=1, source_target_pairs={{0,1},{1,0},{2,3},{3,2},{4,5},{5,4},{6,7},{7,6},{8,9},{9,8},{10,11... | collective-permute-start | bytes 6488072 | tf_op jit(solution)/shard_map/ppermute | solution.py:325

commit v6 on v5

--- a/solution.py
+++ b/solution.py
@@ -16,23 +16,37 @@
 PER_ROW = LANES // CAP
 
 
-def pack_kernel(emb_ref, code_ref, out_ref, target_ref, unit_ref):
+def pack_kernel(emb_ref, code_ref, out_ref, target_ref, unit_ref, sorted_ref, counts_ref, counts_smem, sem):
     rows, width = emb_ref.shape
     owners = out_ref.shape[0]
+    columns = width // LANES
     code = code_ref[...]
     cid = (code >> 16).astype(jnp.float32)
     column = jnp.transpose(jnp.broadcast_to(cid, (LANES, rows)))
     above = lax.broadcasted_iota(jnp.int32, (LANES, LANES), 0)
     here = lax.broadcasted_iota(jnp.int32, (LANES, LANES), 1)
+    before = jnp.sum(jnp.where(column < here[:1].astype(jnp.float32), 1.0, 0.0), axis=0, keepdims=True)
+    number = jnp.sum(jnp.where(column == here[:1].astype(jnp.float32), 1.0, 0.0), axis=0, keepdims=True)
+    counts_ref[...] = jnp.zeros(counts_ref.shape, jnp.int32)
+    counts_ref[0:1, :] = before.astype(jnp.int32)
+    counts_ref[1:2, :] = number.astype(jnp.int32)
+    copy = pltpu.make_async_copy(counts_ref, counts_smem, sem)
+    copy.start()
+    goals = []
     for j in range(rows // LANES):
         lanes = slice(j * LANES, (j + 1) * LANES)
         place = jnp.zeros((1, LANES), jnp.float32)
-        for i in range(j + 1):
-            same = column[i * LANES : (i + 1) * LANES] == cid[:, lanes]
-            if i == j:
-                same = same & (above < here)
-            place += jnp.sum(jnp.where(same, 1.0, 0.0), axis=0, keepdims=True)
+        lower = jnp.zeros((1, LANES), jnp.float32)
+        for i in range(rows // LANES):
+            other = column[i * LANES : (i + 1) * LANES]
+            lower += jnp.sum(jnp.where(other < cid[:, lanes], 1.0, 0.0), axis=0, keepdims=True)
+            if i <= j:
+                same = other == cid[:, lanes]
+                if i == j:
+                    same = same & (above < here)
+                place += jnp.sum(jnp.where(same, 1.0, 0.0), axis=0, keepdims=True)
         target_ref[:, lanes] = (cid[:, lanes] * CAP + place).astype(jnp.int32)
+        goals.append((lower + place).astype(jnp.int32))
     rank = (code & 65535) + 1
     high = jnp.broadcast_to((rank >> 8).astype(jnp.float32), (META // 2, rows))
     low = jnp.broadcast_to((rank & 255).astype(jnp.float32), (META // 2, rows))
@@ -44,26 +58,29 @@
         e = emb_ref[part, :].astype(jnp.float32)
         scale = lax.rsqrt(jnp.sum(e * e, axis=1, keepdims=True) + 1e-06)
         unit_ref[part, :width] = (e * scale).astype(jnp.bfloat16)
-    target = target_ref[...]
+    slot = lax.broadcasted_iota(jnp.int32, (rows, rows), 0)
+    place = jnp.where(slot == jnp.concatenate(goals, axis=1), 1.0, 0.0).astype(jnp.bfloat16)
+    ordered = jnp.dot(place, unit_ref[...], preferred_element_type=jnp.float32)
+    for k in range(columns + 1):
+        sorted_ref[k, :rows, :] = ordered[:, k * LANES : (k + 1) * LANES]
+        sorted_ref[k, rows:, :] = jnp.zeros((CAP, LANES), jnp.float32)
+    copy.wait()
     me = lax.axis_index("owner") % PER_ROW
     segment = lax.broadcasted_iota(jnp.int32, (META, LANES), 1) // CAP
-    for step in range(owners // PER_TILE):
-        block = slice(step * PER_TILE, (step + 1) * PER_TILE)
-        slot = lax.broadcasted_iota(jnp.int32, (TILE, rows), 0)
-        place = jnp.where(slot == target - step * TILE, 1.0, 0.0).astype(jnp.bfloat16)
-        packed = jnp.dot(place, unit_ref[...], preferred_element_type=jnp.float32)
-        for k in range(width // LANES):
-            part = packed[:, k * LANES : (k + 1) * LANES].astype(jnp.bfloat16)
-            out_ref[block, k * CAP : (k + 1) * CAP, :] = part.reshape(PER_TILE, CAP, LANES)
-        ranks = jnp.transpose(packed[:, width:])[:META, :]
-        for t in range(PER_TILE // PER_ROW):
-            tile = ranks[:, t * LANES : (t + 1) * LANES]
-            for q in range(PER_ROW):
-                alone = jnp.where(segment == q, tile, 0.0)
-                moved = pltpu.roll(alone, (me + PER_ROW - q) % PER_ROW * CAP, 1)
-                out_ref[step * PER_TILE + t * PER_ROW + q, width // LANES * CAP :, :] = moved.astype(
-                    jnp.bfloat16
-                )
+    line = lax.broadcasted_iota(jnp.int32, (CAP, LANES), 0)
+    for group in range(owners // PER_ROW):
+        ranks = []
+        for q in range(PER_ROW):
+            c = group * PER_ROW + q
+            some = pl.ds(counts_smem[0, c], CAP)
+            for k in range(columns):
+                out_ref[c, k * CAP : (k + 1) * CAP, :] = sorted_ref[k, some, :].astype(jnp.bfloat16)
+            ranks.append(jnp.where(line < counts_smem[1, c], sorted_ref[columns, some, :], 0.0))
+        tile = jnp.transpose(jnp.concatenate(ranks, axis=0))[:META, :]
+        for q in range(PER_ROW):
+            alone = jnp.where(segment == q, tile, 0.0)
+            moved = pltpu.roll(alone, (me + PER_ROW - q) % PER_ROW * CAP, 1)
+            out_ref[group * PER_ROW + q, columns * CAP :, :] = moved.astype(jnp.bfloat16)
 
 
 def pack(embeddings, code, owners):
@@ -76,7 +93,13 @@
         ),
         in_specs=[pl.BlockSpec(memory_space=pltpu.VMEM)] * 2,
         out_specs=(pl.BlockSpec(memory_space=pltpu.VMEM),) * 2,
-        scratch_shapes=[pltpu.VMEM((rows, width + LANES), jnp.bfloat16)],
+        scratch_shapes=[
+            pltpu.VMEM((rows, width + LANES), jnp.bfloat16),
+            pltpu.VMEM((width // LANES + 1, rows + CAP, LANES), jnp.float32),
+            pltpu.VMEM((8, LANES), jnp.int32),
+            pltpu.SMEM((8, LANES), jnp.int32),
+            pltpu.SemaphoreType.DMA(()),
+        ],
         compiler_params=pltpu.CompilerParams(vmem_limit_bytes=24 * 2**20),
         name="pack_rows",
     )(embeddings, code)

time: 98 us -> 96.8 us (0.988)
  Pallas kernels: 15 us -> 13.8 us
    pallas_call x1, Pallas kernels: 3.35 us -> 2.1 us  [pack(): pl.pallas_call(pack_kernel, out_shape=(jax.ShapeDtypeStruct((owners, widt...]
where the time goes in v6:
time: 96.8 us; the launch traced here: 96.6 us
  blocking collectives  78.4 us (81%)
  Pallas kernels  13.8 us (14%)
  starting transfers between devices  2.08 us (2%)
  local copies, waits for them, and re-layouts  1.52 us (2%)
    all_to_all x1, blocking collectives, shards(): lax.all_to_all(packed, 'owner', split_axis=0, concat_axis=0, tiled=True)  64.9 us
    all_to_all x1, blocking collectives, shards(): lax.all_to_all(best, ('owner', 'split'), split_axis=0, concat_axis=0, til...  13.5 us
    pallas_call x1, Pallas kernels, own_pairs(): pl.pallas_call(own_kernel, out_shape=jax.ShapeDtypeStruct((8, count), jnp...  5.28 us
    pallas_call x1, Pallas kernels, cross_pairs(): pl.pallas_call(second_kernel, out_shape=jax.ShapeDtypeStruct((2 * half //...  2.86 us
    pallas_call x1, Pallas kernels, cross_pairs(): pl.pallas_call(first_kernel, out_shape=(jax.ShapeDtypeStruct((8, half), j...  2.67 us
    pallas_call x1, Pallas kernels, pack(): pl.pallas_call(pack_kernel, out_shape=(jax.ShapeDtypeStruct((owners, widt...  2.1 us
    ppermute x1, starting transfers between devices, shards(): first = lax.ppermute(mine[:half], 'split', swap)  1.99 us
  transfers between devices with their start and end apart: 2, of which 0 were waited for; matrix products, arithmetic and copies ran while one was open for 0% of the time, Pallas kernels for 8%

profile of v6, /device:TPU:1, one launch (start us, length us, event | category | flops | bytes accessed | tf_op | source)
XLA Modules:
  0.0 96.6 jit_solution(2380015167098680347)
XLA Ops:
  0.0 0.7 multiply_add_fusion.code_ref
  0.7 0.0 copy-start
  0.7 1.2 %copy-done = bf16[512,1024]{1,0:T(8,128)(2,1)S(1)} copy-done((bf16[512,1024]{1,0:T(8,128)(2,1)S(1)}, bf16[512,1024]{1,0:T(8,128)(2,1)}, u32[]{:S(2)}) %copy-start) | copy-done | bytes 1048600
  1.9 2.1 %pack_rows.1 = (bf16[64,264,128]{2,1,0:T(8,128)(2,1)S(1)}, s32[1,512]{1,0:T(1,128)S(1)}) custom-call(bf16[512,1024]{1,0:T(8,128)(2,1)S(1)} %copy-done, s32[1,512]{1,0:T(1,128)S(1)} %multiply_add_fusion.code_ref), custom_call_target="tpu_custom_call" | custom-call | tf_op jit(solution)/shard_map/pack_rows/pallas_call | solution.py:88
  4.0 64.9 %all_to_all.16.x_ref = bf16[64,264,128]{2,1,0:T(8,128)(2,1)S(1)} all-to-all(bf16[64,264,128]{2,1,0:T(8,128)(2,1)S(1)} %get-tuple-element.13), channel_id=1, replica_groups=mesh['owner'=64,'split'=2] {'owner'}, dimensions={0} | all-to-all | bytes 8650752 | tf_op jit(solution)/shard_map/all_to_all | solution.py:344
  69.0 0.3 fusion
  69.3 2.0 %collective-permute-start = (bf16[32,264,128]{2,1,0:T(8,128)(2,1)S(1)}, bf16[32,264,128]{2,1,0:T(8,128)(2,1)S(1)}, u32[]{:S(2)}, u32[]{:S(2)}) collective-permute-start(bf16[32,264,128]{2,1,0:T(8,128)(2,1)S(1)} %get-tuple-element.18), channel_id=1, source_target_pairs={{0,1},{1,0},{2,3},{3,2},{4,5},{5,4},{6,7},{7,6},{8,9},{9,8},{10,11... | collective-permute-start | bytes 6488072 | tf_op jit(solution)/shard_map/ppermute | solution.py:347
  71.3 0.1 collective-permute-start.1
  71.4 5.3 %own_pairs.1.own_ref = f32[8,2048]{1,0:T(8,128)S(1)} custom-call(bf16[64,264,128]{2,1,0:T(8,128)(2,1)S(1)} %all_to_all.16.x_ref), custom_call_target="tpu_custom_call" | custom-call | flops 5368709120 | bytes 4194304 | tf_op jit(solution)/shard_map/own_pairs/pallas_call | solution.py:181
  76.7 0.0 collective-permute-done.y_ref
  76.7 2.7 %cross_first.1 = (f32[8,1024]{1,0:T(8,128)S(1)}, f32[8,1024]{1,0:T(8,128)S(1)}) custom-call(bf16[64,264,128]{2,1,0:T(8,128)(2,1)S(1)} %all_to_all.16.x_ref, bf16[32,264,128]{2,1,0:T(8,128)(2,1)S(1)} %collective-permute-done.y_ref), custom_call_target="tpu_custom_call" | custom-call | flops 2147483648 | bytes 4194304 | tf_op jit(solution)/shard_map/cross_first/pallas_call | solution.py:281
  79.3 0.0 collective-permute-done.1.z_ref
  79.4 2.9 %cross_second.1 = f32[128,128]{1,0:T(8,128)S(1)} custom-call(bf16[64,264,128]{2,1,0:T(8,128)(2,1)S(1)} %all_to_all.16.x_ref, bf16[32,264,128]{2,1,0:T(8,128)(2,1)S(1)} %collective-permute-done.y_ref, bf16[32,264,128]{2,1,0:T(8,128)(2,1)S(1)} %collective-permute-done.1.z_ref, f32[8,2048]{1,0:T(8,128)S(1)} %own_pairs.1.own_ref, ...), custom_call_target="tpu_custom_call" | custom-call | flops 2147483648 | bytes 4194304 | tf_op jit(solution)/shard_map/cross_second/pallas_call | solution.py:291
  82.2 13.5 %all_to_all.17 = f32[128,1,128]{2,1,0:T(1,128)S(1)} all-to-all(f32[128,1,128]{2,1,0:T(1,128)S(1)} %bitcast.7), channel_id=1, replica_groups=mesh['owner'=64,'split'=2] {'owner','split'}, dimensions={0} | all-to-all | bytes 131072 | tf_op jit(solution)/shard_map/all_to_all | solution.py:351
  95.7 0.9 pick_results.1
Async XLA Ops:
  0.7 1.2 %copy-start = (bf16[512,1024]{1,0:T(8,128)(2,1)S(1)}, bf16[512,1024]{1,0:T(8,128)(2,1)}, u32[]{:S(2)}) copy-start(bf16[512,1024]{1,0:T(8,128)(2,1)} %emb_ref.1) | copy-start | bytes 3145732
  69.3 7.4 %collective-permute-start = (bf16[32,264,128]{2,1,0:T(8,128)(2,1)S(1)}, bf16[32,264,128]{2,1,0:T(8,128)(2,1)S(1)}, u32[]{:S(2)}, u32[]{:S(2)}) collective-permute-start(bf16[32,264,128]{2,1,0:T(8,128)(2,1)S(1)} %get-tuple-element.18), channel_id=1, source_target_pairs={{0,1},{1,0},{2,3},{3,2},{4,5},{5,4},{6,7},{7,6},{8,9},{9,8},{10,11... | collective-permute-start | bytes 6488072 | tf_op jit(solution)/shard_map/ppermute | solution.py:347
  71.3 8.1 %collective-permute-start.1 = (bf16[32,264,128]{2,1,0:T(8,128)(2,1)S(1)}, bf16[32,264,128]{2,1,0:T(8,128)(2,1)S(1)}, u32[]{:S(2)}, u32[]{:S(2)}) collective-permute-start(bf16[32,264,128]{2,1,0:T(8,128)(2,1)S(1)} %get-tuple-element.17), channel_id=1, source_target_pairs={{0,1},{1,0},{2,3},{3,2},{4,5},{5,4},{6,7},{7,6},{8,9},{9,8},{10,11... | collective-permute-start | bytes 6488072 | tf_op jit(solution)/shard_map/ppermute | solution.py:348

commit v7 on v6

--- a/solution.py
+++ b/solution.py
@@ -8,7 +8,7 @@
 
 CAP = 32
 LANES = 128
-META = 8
+META = 16
 EMPTY = 262144.0
 TILE = 512
 PART = 512

time: 96.8 us -> 98.1 us (1.013)
    all_to_all x1, blocking collectives: 64.9 us -> 66 us  [shards(): lax.all_to_all(packed, 'owner', split_axis=0, concat_axis=0, tiled=True)]
where the time goes in v7:
time: 98.1 us; the launch traced here: 97.8 us
  blocking collectives  79.3 us (81%)
  Pallas kernels  13.8 us (14%)
  starting transfers between devices  2.41 us (2%)
  local copies, waits for them, and re-layouts  1.51 us (2%)
    all_to_all x1, blocking collectives, shards(): lax.all_to_all(packed, 'owner', split_axis=0, concat_axis=0, tiled=True)  66 us
    all_to_all x1, blocking collectives, shards(): lax.all_to_all(best, ('owner', 'split'), split_axis=0, concat_axis=0, til...  13.4 us
    pallas_call x1, Pallas kernels, own_pairs(): pl.pallas_call(own_kernel, out_shape=jax.ShapeDtypeStruct((8, count), jnp...  5.29 us
    pallas_call x1, Pallas kernels, cross_pairs(): pl.pallas_call(second_kernel, out_shape=jax.ShapeDtypeStruct((2 * half //...  2.86 us
    pallas_call x1, Pallas kernels, cross_pairs(): pl.pallas_call(first_kernel, out_shape=(jax.ShapeDtypeStruct((8, half), j...  2.67 us
    ppermute x1, starting transfers between devices, shards(): first = lax.ppermute(mine[:half], 'split', swap)  2.32 us
    pallas_call x1, Pallas kernels, pack(): pl.pallas_call(pack_kernel, out_shape=(jax.ShapeDtypeStruct((owners, widt...  2.09 us
  transfers between devices with their start and end apart: 2, of which 0 were waited for; matrix products, arithmetic and copies ran while one was open for 0% of the time, Pallas kernels for 8%

profile of v7, /device:TPU:1, one launch (start us, length us, event | category | flops | bytes accessed | tf_op | source)
XLA Modules:
  0.0 97.8 jit_solution(12099320701716834129)
XLA Ops:
  0.0 0.7 multiply_add_fusion.code_ref
  0.7 0.0 copy-start
  0.7 1.2 %copy-done = bf16[512,1024]{1,0:T(8,128)(2,1)S(1)} copy-done((bf16[512,1024]{1,0:T(8,128)(2,1)S(1)}, bf16[512,1024]{1,0:T(8,128)(2,1)}, u32[]{:S(2)}) %copy-start) | copy-done | bytes 1048600
  1.9 2.1 %pack_rows.1 = (bf16[64,272,128]{2,1,0:T(8,128)(2,1)S(1)}, s32[1,512]{1,0:T(1,128)S(1)}) custom-call(bf16[512,1024]{1,0:T(8,128)(2,1)S(1)} %copy-done, s32[1,512]{1,0:T(1,128)S(1)} %multiply_add_fusion.code_ref), custom_call_target="tpu_custom_call" | custom-call | tf_op jit(solution)/shard_map/pack_rows/pallas_call | solution.py:88
  4.0 66.0 %all_to_all.16.x_ref = bf16[64,272,128]{2,1,0:T(8,128)(2,1)S(1)} all-to-all(bf16[64,272,128]{2,1,0:T(8,128)(2,1)S(1)} %get-tuple-element.13), channel_id=1, replica_groups=mesh['owner'=64,'split'=2] {'owner'}, dimensions={0} | all-to-all | bytes 8912896 | tf_op jit(solution)/shard_map/all_to_all | solution.py:344
  70.0 0.3 fusion
  70.3 2.3 %collective-permute-start = (bf16[32,272,128]{2,1,0:T(8,128)(2,1)S(1)}, bf16[32,272,128]{2,1,0:T(8,128)(2,1)S(1)}, u32[]{:S(2)}, u32[]{:S(2)}) collective-permute-start(bf16[32,272,128]{2,1,0:T(8,128)(2,1)S(1)} %get-tuple-element.18), channel_id=1, source_target_pairs={{0,1},{1,0},{2,3},{3,2},{4,5},{5,4},{6,7},{7,6},{8,9},{9,8},{10,11... | collective-permute-start | bytes 6684680 | tf_op jit(solution)/shard_map/ppermute | solution.py:347
  72.6 0.1 collective-permute-start.1
  72.7 5.3 %own_pairs.1.own_ref = f32[8,2048]{1,0:T(8,128)S(1)} custom-call(bf16[64,272,128]{2,1,0:T(8,128)(2,1)S(1)} %all_to_all.16.x_ref), custom_call_target="tpu_custom_call" | custom-call | flops 5368709120 | bytes 4194304 | tf_op jit(solution)/shard_map/own_pairs/pallas_call | solution.py:181
  78.0 0.0 collective-permute-done.y_ref
  78.0 2.7 %cross_first.1 = (f32[8,1024]{1,0:T(8,128)S(1)}, f32[8,1024]{1,0:T(8,128)S(1)}) custom-call(bf16[64,272,128]{2,1,0:T(8,128)(2,1)S(1)} %all_to_all.16.x_ref, bf16[32,272,128]{2,1,0:T(8,128)(2,1)S(1)} %collective-permute-done.y_ref), custom_call_target="tpu_custom_call" | custom-call | flops 2147483648 | bytes 4194304 | tf_op jit(solution)/shard_map/cross_first/pallas_call | solution.py:281
  80.7 0.0 collective-permute-done.1.z_ref
  80.7 2.9 %cross_second.1 = f32[128,128]{1,0:T(8,128)S(1)} custom-call(bf16[64,272,128]{2,1,0:T(8,128)(2,1)S(1)} %all_to_all.16.x_ref, bf16[32,272,128]{2,1,0:T(8,128)(2,1)S(1)} %collective-permute-done.y_ref, bf16[32,272,128]{2,1,0:T(8,128)(2,1)S(1)} %collective-permute-done.1.z_ref, f32[8,2048]{1,0:T(8,128)S(1)} %own_pairs.1.own_ref, ...), custom_call_target="tpu_custom_call" | custom-call | flops 2147483648 | bytes 4194304 | tf_op jit(solution)/shard_map/cross_second/pallas_call | solution.py:291
  83.6 13.4 %all_to_all.17 = f32[128,1,128]{2,1,0:T(1,128)S(1)} all-to-all(f32[128,1,128]{2,1,0:T(1,128)S(1)} %bitcast.7), channel_id=1, replica_groups=mesh['owner'=64,'split'=2] {'owner','split'}, dimensions={0} | all-to-all | bytes 131072 | tf_op jit(solution)/shard_map/all_to_all | solution.py:351
  96.9 0.9 pick_results.1
Async XLA Ops:
  0.7 1.2 %copy-start = (bf16[512,1024]{1,0:T(8,128)(2,1)S(1)}, bf16[512,1024]{1,0:T(8,128)(2,1)}, u32[]{:S(2)}) copy-start(bf16[512,1024]{1,0:T(8,128)(2,1)} %emb_ref.1) | copy-start | bytes 3145732
  70.3 7.7 %collective-permute-start = (bf16[32,272,128]{2,1,0:T(8,128)(2,1)S(1)}, bf16[32,272,128]{2,1,0:T(8,128)(2,1)S(1)}, u32[]{:S(2)}, u32[]{:S(2)}) collective-permute-start(bf16[32,272,128]{2,1,0:T(8,128)(2,1)S(1)} %get-tuple-element.18), channel_id=1, source_target_pairs={{0,1},{1,0},{2,3},{3,2},{4,5},{5,4},{6,7},{7,6},{8,9},{9,8},{10,11... | collective-permute-start | bytes 6684680 | tf_op jit(solution)/shard_map/ppermute | solution.py:347
  72.6 8.1 %collective-permute-start.1 = (bf16[32,272,128]{2,1,0:T(8,128)(2,1)S(1)}, bf16[32,272,128]{2,1,0:T(8,128)(2,1)S(1)}, u32[]{:S(2)}, u32[]{:S(2)}) collective-permute-start(bf16[32,272,128]{2,1,0:T(8,128)(2,1)S(1)} %get-tuple-element.17), channel_id=1, source_target_pairs={{0,1},{1,0},{2,3},{3,2},{4,5},{5,4},{6,7},{7,6},{8,9},{9,8},{10,11... | collective-permute-start | bytes 6684680 | tf_op jit(solution)/shard_map/ppermute | solution.py:348

commit v8 on v6

--- a/solution.py
+++ b/solution.py
@@ -143,7 +143,7 @@
     return jnp.full((8, LANES), -1.0, jnp.float32)
 
 
-def own_kernel(x_ref, out_ref, column_ref, row_ref, rows_ref, columns_ref):
+def own_kernel(x_ref, rows_ref, columns_ref, column_ref, row_ref):
     count = x_ref.shape[0] * CAP
     rows_ref[...] = jnp.full(rows_ref.shape, -1.0, jnp.float32)
     for g in range(count // LANES):
@@ -168,136 +168,144 @@
         compare(x, x, middle, middle, column_ref, row_ref, rows_ref, [None] * half)
         for j in range(per):
             columns_ref[:, start + j * LANES : start + (j + 1) * LANES] = across[j]
-    for g in range(count // LANES):
+
+
+def cross(x_ref, y_ref, column_ref, row_ref, rows_ref, columns_ref):
+    count = y_ref.shape[0] * CAP
+    for start in range(0, count, TILE):
+        y = rows_of(y_ref, start, TILE)
+        lanes = [slice(start + j * LANES, start + (j + 1) * LANES) for j in range(TILE // LANES)]
+        across = [columns_ref[:, part] for part in lanes]
+        for first in range(0, count, PART):
+            x = rows_of(x_ref, first, PART)
+            compare(x, y, first, start, column_ref, row_ref, rows_ref, across)
+        for part, best in zip(lanes, across):
+            columns_ref[:, part] = best
+
+
+def along_lanes(rows_ref, first):
+    return jnp.max(jnp.transpose(rows_ref[first : first + LANES, :]), axis=0, keepdims=True)
+
+
+def first_kernel(x_ref, y_ref, own_rows, own_columns, column_ref, rows_ref, columns_ref, low_ref, row_ref):
+    core = lax.axis_index("split")
+    blocks = y_ref.shape[0]
+    half = blocks * CAP
+    for g in range(half // LANES):
+        row_ref[:, g * LANES : (g + 1) * LANES] = rank_row(y_ref, g)
+    columns_ref[...] = jnp.full(columns_ref.shape, -1.0, jnp.float32)
+
+    def side(first):
+        rows_ref[...] = own_rows[first : first + half, :]
+        x = x_ref.at[first // CAP : first // CAP + blocks]
+        cross(x, y_ref, column_ref.at[first : first + half], row_ref, rows_ref, columns_ref)
+
+    @pl.when(core == 0)
+    def _():
+        side(0)
+        for g in range(0, half, LANES):
+            low_ref[:, g : g + LANES] = jnp.broadcast_to(along_lanes(rows_ref, g), (8, LANES))
+        rows_ref[...] = own_rows[half:, :]
+
+    @pl.when(core != 0)
+    def _():
+        side(half)
+        for g in range(0, half, LANES):
+            low_ref[:, g : g + LANES] = jnp.broadcast_to(along_lanes(own_rows, g), (8, LANES))
+
+    low_ref[...] = jnp.maximum(
+        low_ref[...], jnp.max(own_columns[:, :half], axis=0, keepdims=True)
+    )
+
+
+def second_kernel(
+    x_ref, y_ref, z_ref, low_ref, rows_in, columns_in, own_columns, column_ref, out_ref, row_ref, rows_ref, columns_ref
+):
+    core = lax.axis_index("split")
+    blocks = y_ref.shape[0]
+    half = blocks * CAP
+    rows_ref[...] = rows_in[...]
+
+    def side(other_ref):
+        for g in range(half // LANES):
+            row_ref[:, g * LANES : (g + 1) * LANES] = rank_row(other_ref, g)
+        x = x_ref.at[blocks:]
+        cross(x, other_ref, column_ref.at[half:], row_ref, rows_ref, columns_ref)
+
+    @pl.when(core == 0)
+    def _():
+        columns_ref[...] = columns_in[...]
+        side(y_ref)
+
+    @pl.when(core != 0)
+    def _():
+        columns_ref[...] = jnp.full(columns_ref.shape, -1.0, jnp.float32)
+        side(z_ref)
+
+    parity = lax.broadcasted_iota(jnp.int32, (8, LANES), 0) % 2
+    groups = half // LANES
+    for g in range(2 * groups):
         a = slice(g * LANES, (g + 1) * LANES)
-        best = jnp.max(jnp.transpose(rows_ref[a, :]), axis=0, keepdims=True)
-        best = jnp.maximum(best, jnp.max(columns_ref[:, a], axis=0, keepdims=True))
-        out_ref[:, a] = jnp.broadcast_to(best, (8, LANES))
-
-
-def own_pairs(x, width):
-    owners = x.shape[0]
-    count = owners * CAP
-    return pl.pallas_call(
+        b = slice(g % groups * LANES, (g % groups + 1) * LANES)
+        now = jnp.max(columns_ref[:, b], axis=0, keepdims=True)
+        if g < groups:
+            mine = low_ref[:1, b]
+            theirs = jnp.where(core == 0, now, jnp.max(columns_in[:, b], axis=0, keepdims=True))
+        else:
+            mine = jnp.max(own_columns[:, a], axis=0, keepdims=True)
+            mine = jnp.maximum(mine, along_lanes(rows_ref, g % groups * LANES))
+            theirs = jnp.where(core == 0, jnp.full((1, LANES), -1.0, jnp.float32), now)
+        out_ref[g * 8 : (g + 1) * 8, :] = jnp.where(
+            parity == core, jnp.broadcast_to(mine, (8, LANES)), jnp.broadcast_to(theirs, (8, LANES))
+        )
+
+
+def all_pairs(x, y, z, width):
+    count = x.shape[0] * CAP
+    half = count // 2
+    cost = pl.CostEstimate(flops=2 * half * half * width, bytes_accessed=4 * half * width, transcendentals=0)
+    vmem = pl.BlockSpec(memory_space=pltpu.VMEM)
+    params = pltpu.CompilerParams(vmem_limit_bytes=20 * 2**20)
+
+    def array(*dims):
+        return jax.ShapeDtypeStruct(dims, jnp.float32)
+
+    own_rows, own_columns, column = pl.pallas_call(
         own_kernel,
-        out_shape=jax.ShapeDtypeStruct((8, count), jnp.float32),
-        in_specs=[pl.BlockSpec(memory_space=pltpu.VMEM)],
-        out_specs=pl.BlockSpec(memory_space=pltpu.VMEM),
-        scratch_shapes=[
-            pltpu.VMEM((count, LANES), jnp.float32),
-            pltpu.VMEM((8, count), jnp.float32),
-            pltpu.VMEM((count, LANES), jnp.float32),
-            pltpu.VMEM((8, count), jnp.float32),
-        ],
-        compiler_params=pltpu.CompilerParams(vmem_limit_bytes=24 * 2**20),
+        out_shape=(array(count, LANES), array(8, count), array(count, LANES)),
+        in_specs=[vmem],
+        out_specs=(vmem,) * 3,
+        scratch_shapes=[pltpu.VMEM((8, count), jnp.float32)],
+        compiler_params=params,
         cost_estimate=pl.CostEstimate(
             flops=count * (count + TILE) * width, bytes_accessed=2 * count * width, transcendentals=0
         ),
         name="own_pairs",
     )(x)
-
-
-def cross(all_ref, some_ref, column_ref, row_ref, rows_ref, columns_ref):
-    count = all_ref.shape[0] * CAP
-    rows_ref[...] = jnp.full(rows_ref.shape, -1.0, jnp.float32)
-    for g in range(count // LANES):
-        lanes = slice(g * LANES, (g + 1) * LANES)
-        column_ref[lanes, :] = as_column(rank_row(all_ref, g))
-        row_ref[:, lanes] = rank_row(some_ref, g)
-    for start in range(0, count, TILE):
-        y = rows_of(some_ref, start, TILE)
-        lanes = [slice(start + j * LANES, start + (j + 1) * LANES) for j in range(TILE // LANES)]
-        across = [columns_ref[:, part] for part in lanes]
-        for first in range(0, count, PART):
-            x = rows_of(all_ref, first, PART)
-            compare(x, y, first, start, column_ref, row_ref, rows_ref, across)
-        for part, best in zip(lanes, across):
-            columns_ref[:, part] = best
-
-
-def first_kernel(x_ref, y_ref, rows_out, columns_out, column_ref, row_ref, rows_ref):
-    core = lax.axis_index("split")
-    half = y_ref.shape[0]
-    columns_out[...] = jnp.full(columns_out.shape, -1.0, jnp.float32)
-
-    @pl.when(core == 0)
-    def _():
-        cross(x_ref.at[:half], y_ref, column_ref, row_ref, rows_ref, columns_out)
-
-    @pl.when(core != 0)
-    def _():
-        cross(y_ref, x_ref.at[half:], column_ref, row_ref, rows_ref, columns_out)
-
-    for g in range(half * CAP // LANES):
-        a = slice(g * LANES, (g + 1) * LANES)
-        best = jnp.max(jnp.transpose(rows_ref[a, :]), axis=0, keepdims=True)
-        rows_out[:, a] = jnp.broadcast_to(best, (8, LANES))
-
-
-def second_kernel(
-    x_ref, y_ref, z_ref, own_ref, first_ref, columns_in, out_ref, column_ref, row_ref, rows_ref, columns_ref
-):
-    core = lax.axis_index("split")
-    half = y_ref.shape[0]
-    columns_ref[...] = columns_in[...]
-
-    @pl.when(core == 0)
-    def _():
-        cross(x_ref.at[half:], y_ref, column_ref, row_ref, rows_ref, columns_ref)
-
-    @pl.when(core != 0)
-    def _():
-        cross(z_ref, x_ref.at[half:], column_ref, row_ref, rows_ref, columns_ref)
-
-    parity = lax.broadcasted_iota(jnp.int32, (8, LANES), 0) % 2
-    groups = half * CAP // LANES
-    nothing = jnp.full((1, LANES), -1.0, jnp.float32)
-    for g in range(2 * groups):
-        a = slice(g * LANES, (g + 1) * LANES)
-        b = slice(g % groups * LANES, (g % groups + 1) * LANES)
-        if g < groups:
-            from_all = first_ref[:1, b]
-        else:
-            from_all = jnp.max(jnp.transpose(rows_ref[b, :]), axis=0, keepdims=True)
-        from_half = jnp.max(columns_ref[:, b], axis=0, keepdims=True)
-        low, high = (from_half, nothing) if g < groups else (nothing, from_half)
-        mine = jnp.maximum(own_ref[:1, a], jnp.where(core == 0, from_all, high))
-        theirs = jnp.where(core == 0, low, from_all)
-        out_ref[g * 8 : (g + 1) * 8, :] = jnp.where(
-            parity == core, jnp.broadcast_to(mine, (8, LANES)), jnp.broadcast_to(theirs, (8, LANES))
-        )
-
-
-def cross_pairs(x, y, z, own, width):
-    half = y.shape[0] * CAP
-    cost = pl.CostEstimate(flops=2 * half * half * width, bytes_accessed=4 * half * width, transcendentals=0)
-    vmem = pl.BlockSpec(memory_space=pltpu.VMEM)
-    scratch = [
-        pltpu.VMEM((half, LANES), jnp.float32),
-        pltpu.VMEM((8, half), jnp.float32),
-        pltpu.VMEM((half, LANES), jnp.float32),
-    ]
-    params = pltpu.CompilerParams(vmem_limit_bytes=24 * 2**20)
-    first, columns = pl.pallas_call(
+    rows, columns, low = pl.pallas_call(
         first_kernel,
-        out_shape=(jax.ShapeDtypeStruct((8, half), jnp.float32),) * 2,
-        in_specs=[vmem] * 2,
-        out_specs=(vmem,) * 2,
-        scratch_shapes=scratch,
+        out_shape=(array(half, LANES), array(8, half), array(8, half)),
+        in_specs=[vmem] * 5,
+        out_specs=(vmem,) * 3,
+        scratch_shapes=[pltpu.VMEM((8, half), jnp.float32)],
         compiler_params=params,
         cost_estimate=cost,
         name="cross_first",
-    )(x, y)
+    )(x, y, own_rows, own_columns, column)
     return pl.pallas_call(
         second_kernel,
-        out_shape=jax.ShapeDtypeStruct((2 * half // LANES * 8, LANES), jnp.float32),
-        in_specs=[vmem] * 6,
+        out_shape=array(count // LANES * 8, LANES),
+        in_specs=[vmem] * 8,
         out_specs=vmem,
-        scratch_shapes=scratch + [pltpu.VMEM((8, half), jnp.float32)],
+        scratch_shapes=[
+            pltpu.VMEM((8, half), jnp.float32),
+            pltpu.VMEM((half, LANES), jnp.float32),
+            pltpu.VMEM((8, half), jnp.float32),
+        ],
         compiler_params=params,
         cost_estimate=cost,
         name="cross_second",
-    )(x, y, z, own, first, columns)
+    )(x, y, z, low, rows, columns, own_columns, column)
 
 
 def pick_kernel(recv_ref, target_ref, out_ref):
@@ -346,8 +354,7 @@
     half = owners // 2
     first = lax.ppermute(mine[:half], "split", swap)
     second = lax.ppermute(mine[half:], "split", swap)
-    own = own_pairs(mine, width)
-    best = cross_pairs(mine, first, second, own, width)
+    best = all_pairs(mine, first, second, width)
     returned = lax.all_to_all(best, ("owner", "split"), split_axis=0, concat_axis=0, tiled=True)
     return pick(returned, target).reshape(rows)
 

time: 96.8 us -> 96.7 us (level)
  no operation moved by 1% of the time
where the time goes in v8:
time: 96.7 us; the launch traced here: 96.5 us
  blocking collectives  78.5 us (81%)
  Pallas kernels  13.7 us (14%)
  starting transfers between devices  2.08 us (2%)
  local copies, waits for them, and re-layouts  1.52 us (2%)
    all_to_all x1, blocking collectives, shards(): lax.all_to_all(packed, 'owner', split_axis=0, concat_axis=0, tiled=True)  64.9 us
    all_to_all x1, blocking collectives, shards(): lax.all_to_all(best, ('owner', 'split'), split_axis=0, concat_axis=0, til...  13.5 us
    pallas_call x1, Pallas kernels, all_pairs(): pl.pallas_call(own_kernel, out_shape=(array(count, LANES), array(8, count...  5.25 us
    pallas_call x1, Pallas kernels, all_pairs(): pl.pallas_call(second_kernel, out_shape=array(count // LANES * 8, LANES),...  2.91 us
    pallas_call x1, Pallas kernels, all_pairs(): pl.pallas_call(first_kernel, out_shape=(array(half, LANES), array(8, half...  2.51 us
    pallas_call x1, Pallas kernels, pack(): pl.pallas_call(pack_kernel, out_shape=(jax.ShapeDtypeStruct((owners, widt...  2.11 us
    ppermute x1, starting transfers between devices, shards(): first = lax.ppermute(mine[:half], 'split', swap)  1.99 us
  transfers between devices with their start and end apart: 2, of which 0 were waited for; matrix products, arithmetic and copies ran while one was open for 0% of the time, Pallas kernels for 8%

profile of v8, /device:TPU:1, one launch (start us, length us, event | category | flops | bytes accessed | tf_op | source)
XLA Modules:
  0.0 96.5 jit_solution(14107358391523154846)
XLA Ops:
  0.0 0.7 multiply_add_fusion.code_ref
  0.7 0.0 copy-start
  0.7 1.2 %copy-done = bf16[512,1024]{1,0:T(8,128)(2,1)S(1)} copy-done((bf16[512,1024]{1,0:T(8,128)(2,1)S(1)}, bf16[512,1024]{1,0:T(8,128)(2,1)}, u32[]{:S(2)}) %copy-start) | copy-done | bytes 1048600
  1.9 2.1 %pack_rows.1 = (bf16[64,264,128]{2,1,0:T(8,128)(2,1)S(1)}, s32[1,512]{1,0:T(1,128)S(1)}) custom-call(bf16[512,1024]{1,0:T(8,128)(2,1)S(1)} %copy-done, s32[1,512]{1,0:T(1,128)S(1)} %multiply_add_fusion.code_ref), custom_call_target="tpu_custom_call" | custom-call | tf_op jit(solution)/shard_map/pack_rows/pallas_call | solution.py:88
  4.0 64.9 %all_to_all.16.x_ref = bf16[64,264,128]{2,1,0:T(8,128)(2,1)S(1)} all-to-all(bf16[64,264,128]{2,1,0:T(8,128)(2,1)S(1)} %get-tuple-element.17), channel_id=1, replica_groups=mesh['owner'=64,'split'=2] {'owner'}, dimensions={0} | all-to-all | bytes 8650752 | tf_op jit(solution)/shard_map/all_to_all | solution.py:352
  69.0 0.3 fusion
  69.3 2.0 %collective-permute-start = (bf16[32,264,128]{2,1,0:T(8,128)(2,1)S(1)}, bf16[32,264,128]{2,1,0:T(8,128)(2,1)S(1)}, u32[]{:S(2)}, u32[]{:S(2)}) collective-permute-start(bf16[32,264,128]{2,1,0:T(8,128)(2,1)S(1)} %get-tuple-element.26), channel_id=1, source_target_pairs={{0,1},{1,0},{2,3},{3,2},{4,5},{5,4},{6,7},{7,6},{8,9},{9,8},{10,11... | collective-permute-start | bytes 6488072 | tf_op jit(solution)/shard_map/ppermute | solution.py:355
  71.3 0.1 collective-permute-start.1
  71.4 5.2 %own_pairs.1 = (f32[2048,128]{1,0:T(8,128)S(1)}, f32[8,2048]{1,0:T(8,128)S(1)}, f32[2048,128]{1,0:T(8,128)S(1)}) custom-call(bf16[64,264,128]{2,1,0:T(8,128)(2,1)S(1)} %all_to_all.16.x_ref), custom_call_target="tpu_custom_call" | custom-call | flops 5368709120 | bytes 4194304 | tf_op jit(solution)/shard_map/own_pairs/pallas_call | solution.py:273
  76.6 0.0 collective-permute-done.y_ref
  76.6 2.5 %cross_first.1 = (f32[1024,128]{1,0:T(8,128)S(1)}, f32[8,1024]{1,0:T(8,128)S(1)}, f32[8,1024]{1,0:T(8,128)S(1)}) custom-call(bf16[64,264,128]{2,1,0:T(8,128)(2,1)S(1)} %all_to_all.16.x_ref, bf16[32,264,128]{2,1,0:T(8,128)(2,1)S(1)} %collective-permute-done.y_ref, f32[2048,128]{1,0:T(8,128)S(1)} %get-tuple-element.18.own_rows, ...), custom_call_target="tpu_custom_call" | custom-call | flops 2147483648 | bytes 4194304 | tf_op jit(solution)/shard_map/cross_first/pallas_call | solution.py:285
  79.1 0.0 collective-permute-done.1.z_ref
  79.2 2.9 %cross_second.1 = f32[128,128]{1,0:T(8,128)S(1)} custom-call(bf16[64,264,128]{2,1,0:T(8,128)(2,1)S(1)} %all_to_all.16.x_ref, bf16[32,264,128]{2,1,0:T(8,128)(2,1)S(1)} %collective-permute-done.y_ref, bf16[32,264,128]{2,1,0:T(8,128)(2,1)S(1)} %collective-permute-done.1.z_ref, f32[8,1024]{1,0:T(8,128)S(1)} %get-tuple-element.21.low_ref, ...), custom_call_target="tpu_custom_call" | custom-call | flops 2147483648 | bytes 4194304 | tf_op jit(solution)/shard_map/cross_second/pallas_call | solution.py:295
  82.1 13.5 %all_to_all.17 = f32[128,1,128]{2,1,0:T(1,128)S(1)} all-to-all(f32[128,1,128]{2,1,0:T(1,128)S(1)} %bitcast.7), channel_id=1, replica_groups=mesh['owner'=64,'split'=2] {'owner','split'}, dimensions={0} | all-to-all | bytes 131072 | tf_op jit(solution)/shard_map/all_to_all | solution.py:358
  95.6 0.9 pick_results.1
Async XLA Ops:
  0.7 1.2 %copy-start = (bf16[512,1024]{1,0:T(8,128)(2,1)S(1)}, bf16[512,1024]{1,0:T(8,128)(2,1)}, u32[]{:S(2)}) copy-start(bf16[512,1024]{1,0:T(8,128)(2,1)} %emb_ref.1) | copy-start | bytes 3145732
  69.3 7.3 %collective-permute-start = (bf16[32,264,128]{2,1,0:T(8,128)(2,1)S(1)}, bf16[32,264,128]{2,1,0:T(8,128)(2,1)S(1)}, u32[]{:S(2)}, u32[]{:S(2)}) collective-permute-start(bf16[32,264,128]{2,1,0:T(8,128)(2,1)S(1)} %get-tuple-element.26), channel_id=1, source_target_pairs={{0,1},{1,0},{2,3},{3,2},{4,5},{5,4},{6,7},{7,6},{8,9},{9,8},{10,11... | collective-permute-start | bytes 6488072 | tf_op jit(solution)/shard_map/ppermute | solution.py:355
  71.3 7.9 %collective-permute-start.1 = (bf16[32,264,128]{2,1,0:T(8,128)(2,1)S(1)}, bf16[32,264,128]{2,1,0:T(8,128)(2,1)S(1)}, u32[]{:S(2)}, u32[]{:S(2)}) collective-permute-start(bf16[32,264,128]{2,1,0:T(8,128)(2,1)S(1)} %get-tuple-element.25), channel_id=1, source_target_pairs={{0,1},{1,0},{2,3},{3,2},{4,5},{5,4},{6,7},{7,6},{8,9},{9,8},{10,11... | collective-permute-start | bytes 6488072 | tf_op jit(solution)/shard_map/ppermute | solution.py:356

commit v9 on v8

--- a/solution.py
+++ b/solution.py
@@ -319,15 +319,15 @@
     cid = target >> 5
     slot = (target & (CAP - 1)) + lax.axis_index("owner") % PER_ROW * CAP
     chosen = lax.broadcasted_iota(jnp.int32, (owners, rows), 0) == cid
-    chosen = chosen.astype(jnp.float32).astype(jnp.bfloat16)
-    total = jnp.zeros((LANES, rows), jnp.float32)
-    rest = best
+    chosen = jnp.where(chosen, 1.0, 0.0).astype(jnp.bfloat16)
+    pieces, rest = [], best
     for _ in range(3):
-        piece = rest.astype(jnp.bfloat16)
-        rest = rest - piece.astype(jnp.float32)
-        total += lax.dot_general(
-            piece, chosen, (((0,), (0,)), ((), ())), preferred_element_type=jnp.float32
-        )
+        pieces.append(rest.astype(jnp.bfloat16))
+        rest = rest - pieces[-1].astype(jnp.float32)
+    total = lax.dot_general(
+        jnp.concatenate(pieces, axis=0), jnp.concatenate([chosen] * 3, axis=0),
+        (((0,), (0,)), ((), ())), preferred_element_type=jnp.float32,
+    )
     mine = lax.broadcasted_iota(jnp.int32, (LANES, rows), 0) == slot
     out_ref[...] = jnp.sum(jnp.where(mine, total, 0.0), axis=0, keepdims=True)
 

time: 96.7 us -> 96.6 us (level)
  no operation moved by 1% of the time
where the time goes in v9:
time: 96.6 us; the launch traced here: 96.4 us
  blocking collectives  78.4 us (81%)
  Pallas kernels  13.6 us (14%)
  starting transfers between devices  2.09 us (2%)
  local copies, waits for them, and re-layouts  1.52 us (2%)
    all_to_all x1, blocking collectives, shards(): lax.all_to_all(packed, 'owner', split_axis=0, concat_axis=0, tiled=True)  64.9 us
    all_to_all x1, blocking collectives, shards(): lax.all_to_all(best, ('owner', 'split'), split_axis=0, concat_axis=0, til...  13.5 us
    pallas_call x1, Pallas kernels, all_pairs(): pl.pallas_call(own_kernel, out_shape=(array(count, LANES), array(8, count...  5.25 us
    pallas_call x1, Pallas kernels, all_pairs(): pl.pallas_call(second_kernel, out_shape=array(count // LANES * 8, LANES),...  2.92 us
    pallas_call x1, Pallas kernels, all_pairs(): pl.pallas_call(first_kernel, out_shape=(array(half, LANES), array(8, half...  2.51 us
    pallas_call x1, Pallas kernels, pack(): pl.pallas_call(pack_kernel, out_shape=(jax.ShapeDtypeStruct((owners, widt...  2.1 us
    ppermute x1, starting transfers between devices, shards(): first = lax.ppermute(mine[:half], 'split', swap)  2 us
  transfers between devices with their start and end apart: 2, of which 0 were waited for; matrix products, arithmetic and copies ran while one was open for 0% of the time, Pallas kernels for 8%

profile of v9, /device:TPU:1, one launch (start us, length us, event | category | flops | bytes accessed | tf_op | source)
XLA Modules:
  0.0 96.4 jit_solution(10563085163251782132)
XLA Ops:
  0.0 0.7 multiply_add_fusion.code_ref
  0.7 0.0 copy-start
  0.7 1.2 %copy-done = bf16[512,1024]{1,0:T(8,128)(2,1)S(1)} copy-done((bf16[512,1024]{1,0:T(8,128)(2,1)S(1)}, bf16[512,1024]{1,0:T(8,128)(2,1)}, u32[]{:S(2)}) %copy-start) | copy-done | bytes 1048600
  1.9 2.1 %pack_rows.1 = (bf16[64,264,128]{2,1,0:T(8,128)(2,1)S(1)}, s32[1,512]{1,0:T(1,128)S(1)}) custom-call(bf16[512,1024]{1,0:T(8,128)(2,1)S(1)} %copy-done, s32[1,512]{1,0:T(1,128)S(1)} %multiply_add_fusion.code_ref), custom_call_target="tpu_custom_call" | custom-call | tf_op jit(solution)/shard_map/pack_rows/pallas_call | solution.py:88
  4.0 64.9 %all_to_all.16.x_ref = bf16[64,264,128]{2,1,0:T(8,128)(2,1)S(1)} all-to-all(bf16[64,264,128]{2,1,0:T(8,128)(2,1)S(1)} %get-tuple-element.17), channel_id=1, replica_groups=mesh['owner'=64,'split'=2] {'owner'}, dimensions={0} | all-to-all | bytes 8650752 | tf_op jit(solution)/shard_map/all_to_all | solution.py:352
  69.0 0.3 fusion
  69.3 2.0 %collective-permute-start = (bf16[32,264,128]{2,1,0:T(8,128)(2,1)S(1)}, bf16[32,264,128]{2,1,0:T(8,128)(2,1)S(1)}, u32[]{:S(2)}, u32[]{:S(2)}) collective-permute-start(bf16[32,264,128]{2,1,0:T(8,128)(2,1)S(1)} %get-tuple-element.26), channel_id=1, source_target_pairs={{0,1},{1,0},{2,3},{3,2},{4,5},{5,4},{6,7},{7,6},{8,9},{9,8},{10,11... | collective-permute-start | bytes 6488072 | tf_op jit(solution)/shard_map/ppermute | solution.py:355
  71.3 0.1 collective-permute-start.1
  71.4 5.2 %own_pairs.1 = (f32[2048,128]{1,0:T(8,128)S(1)}, f32[8,2048]{1,0:T(8,128)S(1)}, f32[2048,128]{1,0:T(8,128)S(1)}) custom-call(bf16[64,264,128]{2,1,0:T(8,128)(2,1)S(1)} %all_to_all.16.x_ref), custom_call_target="tpu_custom_call" | custom-call | flops 5368709120 | bytes 4194304 | tf_op jit(solution)/shard_map/own_pairs/pallas_call | solution.py:273
  76.6 0.0 collective-permute-done.y_ref
  76.6 2.5 %cross_first.1 = (f32[1024,128]{1,0:T(8,128)S(1)}, f32[8,1024]{1,0:T(8,128)S(1)}, f32[8,1024]{1,0:T(8,128)S(1)}) custom-call(bf16[64,264,128]{2,1,0:T(8,128)(2,1)S(1)} %all_to_all.16.x_ref, bf16[32,264,128]{2,1,0:T(8,128)(2,1)S(1)} %collective-permute-done.y_ref, f32[2048,128]{1,0:T(8,128)S(1)} %get-tuple-element.18.own_rows, ...), custom_call_target="tpu_custom_call" | custom-call | flops 2147483648 | bytes 4194304 | tf_op jit(solution)/shard_map/cross_first/pallas_call | solution.py:285
  79.1 0.0 collective-permute-done.1.z_ref
  79.2 2.9 %cross_second.1 = f32[128,128]{1,0:T(8,128)S(1)} custom-call(bf16[64,264,128]{2,1,0:T(8,128)(2,1)S(1)} %all_to_all.16.x_ref, bf16[32,264,128]{2,1,0:T(8,128)(2,1)S(1)} %collective-permute-done.y_ref, bf16[32,264,128]{2,1,0:T(8,128)(2,1)S(1)} %collective-permute-done.1.z_ref, f32[8,1024]{1,0:T(8,128)S(1)} %get-tuple-element.21.low_ref, ...), custom_call_target="tpu_custom_call" | custom-call | flops 2147483648 | bytes 4194304 | tf_op jit(solution)/shard_map/cross_second/pallas_call | solution.py:295
  82.1 13.5 %all_to_all.17 = f32[128,1,128]{2,1,0:T(1,128)S(1)} all-to-all(f32[128,1,128]{2,1,0:T(1,128)S(1)} %bitcast.7), channel_id=1, replica_groups=mesh['owner'=64,'split'=2] {'owner','split'}, dimensions={0} | all-to-all | bytes 131072 | tf_op jit(solution)/shard_map/all_to_all | solution.py:358
  95.6 0.8 pick_results.1
Async XLA Ops:
  0.7 1.2 %copy-start = (bf16[512,1024]{1,0:T(8,128)(2,1)S(1)}, bf16[512,1024]{1,0:T(8,128)(2,1)}, u32[]{:S(2)}) copy-start(bf16[512,1024]{1,0:T(8,128)(2,1)} %emb_ref.1) | copy-start | bytes 3145732
  69.3 7.4 %collective-permute-start = (bf16[32,264,128]{2,1,0:T(8,128)(2,1)S(1)}, bf16[32,264,128]{2,1,0:T(8,128)(2,1)S(1)}, u32[]{:S(2)}, u32[]{:S(2)}) collective-permute-start(bf16[32,264,128]{2,1,0:T(8,128)(2,1)S(1)} %get-tuple-element.26), channel_id=1, source_target_pairs={{0,1},{1,0},{2,3},{3,2},{4,5},{5,4},{6,7},{7,6},{8,9},{9,8},{10,11... | collective-permute-start | bytes 6488072 | tf_op jit(solution)/shard_map/ppermute | solution.py:355
  71.3 7.9 %collective-permute-start.1 = (bf16[32,264,128]{2,1,0:T(8,128)(2,1)S(1)}, bf16[32,264,128]{2,1,0:T(8,128)(2,1)S(1)}, u32[]{:S(2)}, u32[]{:S(2)}) collective-permute-start(bf16[32,264,128]{2,1,0:T(8,128)(2,1)S(1)} %get-tuple-element.25), channel_id=1, source_target_pairs={{0,1},{1,0},{2,3},{3,2},{4,5},{5,4},{6,7},{7,6},{8,9},{9,8},{10,11... | collective-permute-start | bytes 6488072 | tf_op jit(solution)/shard_map/ppermute | solution.py:356

commit v10 on v8

--- a/solution.py
+++ b/solution.py
@@ -47,40 +47,40 @@
                 place += jnp.sum(jnp.where(same, 1.0, 0.0), axis=0, keepdims=True)
         target_ref[:, lanes] = (cid[:, lanes] * CAP + place).astype(jnp.int32)
         goals.append((lower + place).astype(jnp.int32))
-    rank = (code & 65535) + 1
-    high = jnp.broadcast_to((rank >> 8).astype(jnp.float32), (META // 2, rows))
-    low = jnp.broadcast_to((rank & 255).astype(jnp.float32), (META // 2, rows))
-    both = jnp.concatenate([high, low, jnp.zeros((LANES - META, rows), jnp.float32)], axis=0)
-    unit_ref[:, width:] = jnp.transpose(both).astype(jnp.bfloat16)
+    rank = ((code & 65535) + 1).astype(jnp.float32)
+    goal = jnp.concatenate(goals, axis=1)
+    goal_column = jnp.transpose(jnp.broadcast_to(goal.astype(jnp.float32), (LANES, rows)))
+    rank_column = jnp.transpose(jnp.broadcast_to(rank, (LANES, rows)))
+    held = []
+    for j in range(rows // LANES):
+        spot = (here[:1] + j * LANES).astype(jnp.float32)
+        held.append(jnp.sum(jnp.where(goal_column == spot, rank_column, 0.0), axis=0, keepdims=True))
+    held = jnp.concatenate(held, axis=1).astype(jnp.int32)
+    high = jnp.broadcast_to((held >> 8).astype(jnp.float32), (META // 2, rows))
+    low = jnp.broadcast_to((held & 255).astype(jnp.float32), (META // 2, rows))
+    ranks = jnp.concatenate([high, low], axis=0)
     chunk = 128
     for r in range(rows // chunk):
         part = slice(r * chunk, (r + 1) * chunk)
         e = emb_ref[part, :].astype(jnp.float32)
         scale = lax.rsqrt(jnp.sum(e * e, axis=1, keepdims=True) + 1e-06)
-        unit_ref[part, :width] = (e * scale).astype(jnp.bfloat16)
+        unit_ref[part, :] = (e * scale).astype(jnp.bfloat16)
     slot = lax.broadcasted_iota(jnp.int32, (rows, rows), 0)
-    place = jnp.where(slot == jnp.concatenate(goals, axis=1), 1.0, 0.0).astype(jnp.bfloat16)
+    place = jnp.where(slot == goal, 1.0, 0.0).astype(jnp.bfloat16)
     ordered = jnp.dot(place, unit_ref[...], preferred_element_type=jnp.float32)
-    for k in range(columns + 1):
+    for k in range(columns):
         sorted_ref[k, :rows, :] = ordered[:, k * LANES : (k + 1) * LANES]
         sorted_ref[k, rows:, :] = jnp.zeros((CAP, LANES), jnp.float32)
     copy.wait()
-    me = lax.axis_index("owner") % PER_ROW
-    segment = lax.broadcasted_iota(jnp.int32, (META, LANES), 1) // CAP
-    line = lax.broadcasted_iota(jnp.int32, (CAP, LANES), 0)
-    for group in range(owners // PER_ROW):
-        ranks = []
-        for q in range(PER_ROW):
-            c = group * PER_ROW + q
-            some = pl.ds(counts_smem[0, c], CAP)
-            for k in range(columns):
-                out_ref[c, k * CAP : (k + 1) * CAP, :] = sorted_ref[k, some, :].astype(jnp.bfloat16)
-            ranks.append(jnp.where(line < counts_smem[1, c], sorted_ref[columns, some, :], 0.0))
-        tile = jnp.transpose(jnp.concatenate(ranks, axis=0))[:META, :]
-        for q in range(PER_ROW):
-            alone = jnp.where(segment == q, tile, 0.0)
-            moved = pltpu.roll(alone, (me + PER_ROW - q) % PER_ROW * CAP, 1)
-            out_ref[group * PER_ROW + q, columns * CAP :, :] = moved.astype(jnp.bfloat16)
+    first = lax.axis_index("owner") % PER_ROW * CAP
+    lane = lax.broadcasted_iota(jnp.int32, (META, LANES), 1) - first
+    for c in range(owners):
+        start, count = counts_smem[0, c], counts_smem[1, c]
+        for k in range(columns):
+            out_ref[c, k * CAP : (k + 1) * CAP, :] = sorted_ref[k, pl.ds(start, CAP), :].astype(jnp.bfloat16)
+        moved = pltpu.roll(ranks, (first + rows - start) & (rows - 1), 1)[:, :LANES]
+        tile = jnp.where((lane >= 0) & (lane < count), moved, 0.0)
+        out_ref[c, columns * CAP :, :] = tile.astype(jnp.bfloat16)
 
 
 def pack(embeddings, code, owners):
@@ -94,8 +94,8 @@
         in_specs=[pl.BlockSpec(memory_space=pltpu.VMEM)] * 2,
         out_specs=(pl.BlockSpec(memory_space=pltpu.VMEM),) * 2,
         scratch_shapes=[
-            pltpu.VMEM((rows, width + LANES), jnp.bfloat16),
-            pltpu.VMEM((width // LANES + 1, rows + CAP, LANES), jnp.float32),
+            pltpu.VMEM((rows, width), jnp.bfloat16),
+            pltpu.VMEM((width // LANES, rows + CAP, LANES), jnp.float32),
             pltpu.VMEM((8, LANES), jnp.int32),
             pltpu.SMEM((8, LANES), jnp.int32),
             pltpu.SemaphoreType.DMA(()),

time: 96.7 us -> 96.7 us (level)
  no operation moved by 1% of the time
where the time goes in v10:
time: 96.7 us; the launch traced here: 96.4 us
  blocking collectives  78.5 us (81%)
  Pallas kernels  13.6 us (14%)
  starting transfers between devices  2.08 us (2%)
  local copies, waits for them, and re-layouts  1.52 us (2%)
    all_to_all x1, blocking collectives, shards(): lax.all_to_all(packed, 'owner', split_axis=0, concat_axis=0, tiled=True)  64.9 us
    all_to_all x1, blocking collectives, shards(): lax.all_to_all(best, ('owner', 'split'), split_axis=0, concat_axis=0, til...  13.5 us
    pallas_call x1, Pallas kernels, all_pairs(): pl.pallas_call(own_kernel, out_shape=(array(count, LANES), array(8, count...  5.24 us
    pallas_call x1, Pallas kernels, all_pairs(): pl.pallas_call(second_kernel, out_shape=array(count // LANES * 8, LANES),...  2.92 us
    pallas_call x1, Pallas kernels, all_pairs(): pl.pallas_call(first_kernel, out_shape=(array(half, LANES), array(8, half...  2.51 us
    pallas_call x1, Pallas kernels, pack(): pl.pallas_call(pack_kernel, out_shape=(jax.ShapeDtypeStruct((owners, widt...  2.04 us
    ppermute x1, starting transfers between devices, shards(): first = lax.ppermute(mine[:half], 'split', swap)  1.99 us
  transfers between devices with their start and end apart: 2, of which 0 were waited for; matrix products, arithmetic and copies ran while one was open for 0% of the time, Pallas kernels for 8%

profile of v10, /device:TPU:1, one launch (start us, length us, event | category | flops | bytes accessed | tf_op | source)
XLA Modules:
  0.0 96.4 jit_solution(16045524437801503404)
XLA Ops:
  0.0 0.7 multiply_add_fusion.code_ref
  0.7 0.0 copy-start
  0.7 1.2 %copy-done = bf16[512,1024]{1,0:T(8,128)(2,1)S(1)} copy-done((bf16[512,1024]{1,0:T(8,128)(2,1)S(1)}, bf16[512,1024]{1,0:T(8,128)(2,1)}, u32[]{:S(2)}) %copy-start) | copy-done | bytes 1048600
  1.9 2.0 %pack_rows.1 = (bf16[64,264,128]{2,1,0:T(8,128)(2,1)S(1)}, s32[1,512]{1,0:T(1,128)S(1)}) custom-call(bf16[512,1024]{1,0:T(8,128)(2,1)S(1)} %copy-done, s32[1,512]{1,0:T(1,128)S(1)} %multiply_add_fusion.code_ref), custom_call_target="tpu_custom_call" | custom-call | tf_op jit(solution)/shard_map/pack_rows/pallas_call | solution.py:88
  4.0 64.9 %all_to_all.16.x_ref = bf16[64,264,128]{2,1,0:T(8,128)(2,1)S(1)} all-to-all(bf16[64,264,128]{2,1,0:T(8,128)(2,1)S(1)} %get-tuple-element.17), channel_id=1, replica_groups=mesh['owner'=64,'split'=2] {'owner'}, dimensions={0} | all-to-all | bytes 8650752 | tf_op jit(solution)/shard_map/all_to_all | solution.py:352
  68.9 0.3 fusion
  69.2 2.0 %collective-permute-start = (bf16[32,264,128]{2,1,0:T(8,128)(2,1)S(1)}, bf16[32,264,128]{2,1,0:T(8,128)(2,1)S(1)}, u32[]{:S(2)}, u32[]{:S(2)}) collective-permute-start(bf16[32,264,128]{2,1,0:T(8,128)(2,1)S(1)} %get-tuple-element.26), channel_id=1, source_target_pairs={{0,1},{1,0},{2,3},{3,2},{4,5},{5,4},{6,7},{7,6},{8,9},{9,8},{10,11... | collective-permute-start | bytes 6488072 | tf_op jit(solution)/shard_map/ppermute | solution.py:355
  71.2 0.1 collective-permute-start.1
  71.3 5.2 %own_pairs.1 = (f32[2048,128]{1,0:T(8,128)S(1)}, f32[8,2048]{1,0:T(8,128)S(1)}, f32[2048,128]{1,0:T(8,128)S(1)}) custom-call(bf16[64,264,128]{2,1,0:T(8,128)(2,1)S(1)} %all_to_all.16.x_ref), custom_call_target="tpu_custom_call" | custom-call | flops 5368709120 | bytes 4194304 | tf_op jit(solution)/shard_map/own_pairs/pallas_call | solution.py:273
  76.5 0.0 collective-permute-done.y_ref
  76.6 2.5 %cross_first.1 = (f32[1024,128]{1,0:T(8,128)S(1)}, f32[8,1024]{1,0:T(8,128)S(1)}, f32[8,1024]{1,0:T(8,128)S(1)}) custom-call(bf16[64,264,128]{2,1,0:T(8,128)(2,1)S(1)} %all_to_all.16.x_ref, bf16[32,264,128]{2,1,0:T(8,128)(2,1)S(1)} %collective-permute-done.y_ref, f32[2048,128]{1,0:T(8,128)S(1)} %get-tuple-element.18.own_rows, ...), custom_call_target="tpu_custom_call" | custom-call | flops 2147483648 | bytes 4194304 | tf_op jit(solution)/shard_map/cross_first/pallas_call | solution.py:285
  79.1 0.0 collective-permute-done.1.z_ref
  79.1 2.9 %cross_second.1 = f32[128,128]{1,0:T(8,128)S(1)} custom-call(bf16[64,264,128]{2,1,0:T(8,128)(2,1)S(1)} %all_to_all.16.x_ref, bf16[32,264,128]{2,1,0:T(8,128)(2,1)S(1)} %collective-permute-done.y_ref, bf16[32,264,128]{2,1,0:T(8,128)(2,1)S(1)} %collective-permute-done.1.z_ref, f32[8,1024]{1,0:T(8,128)S(1)} %get-tuple-element.21.low_ref, ...), custom_call_target="tpu_custom_call" | custom-call | flops 2147483648 | bytes 4194304 | tf_op jit(solution)/shard_map/cross_second/pallas_call | solution.py:295
  82.0 13.5 %all_to_all.17 = f32[128,1,128]{2,1,0:T(1,128)S(1)} all-to-all(f32[128,1,128]{2,1,0:T(1,128)S(1)} %bitcast.7), channel_id=1, replica_groups=mesh['owner'=64,'split'=2] {'owner','split'}, dimensions={0} | all-to-all | bytes 131072 | tf_op jit(solution)/shard_map/all_to_all | solution.py:358
  95.6 0.9 pick_results.1
Async XLA Ops:
  0.7 1.2 %copy-start = (bf16[512,1024]{1,0:T(8,128)(2,1)S(1)}, bf16[512,1024]{1,0:T(8,128)(2,1)}, u32[]{:S(2)}) copy-start(bf16[512,1024]{1,0:T(8,128)(2,1)} %emb_ref.1) | copy-start | bytes 3145732
  69.2 7.3 %collective-permute-start = (bf16[32,264,128]{2,1,0:T(8,128)(2,1)S(1)}, bf16[32,264,128]{2,1,0:T(8,128)(2,1)S(1)}, u32[]{:S(2)}, u32[]{:S(2)}) collective-permute-start(bf16[32,264,128]{2,1,0:T(8,128)(2,1)S(1)} %get-tuple-element.26), channel_id=1, source_target_pairs={{0,1},{1,0},{2,3},{3,2},{4,5},{5,4},{6,7},{7,6},{8,9},{9,8},{10,11... | collective-permute-start | bytes 6488072 | tf_op jit(solution)/shard_map/ppermute | solution.py:355
  71.2 7.9 %collective-permute-start.1 = (bf16[32,264,128]{2,1,0:T(8,128)(2,1)S(1)}, bf16[32,264,128]{2,1,0:T(8,128)(2,1)S(1)}, u32[]{:S(2)}, u32[]{:S(2)}) collective-permute-start(bf16[32,264,128]{2,1,0:T(8,128)(2,1)S(1)} %get-tuple-element.25), channel_id=1, source_target_pairs={{0,1},{1,0},{2,3},{3,2},{4,5},{5,4},{6,7},{7,6},{8,9},{9,8},{10,11... | collective-permute-start | bytes 6488072 | tf_op jit(solution)/shard_map/ppermute | solution.py:356

commit v11 on v6

--- a/solution.py
+++ b/solution.py
@@ -47,40 +47,40 @@
                 place += jnp.sum(jnp.where(same, 1.0, 0.0), axis=0, keepdims=True)
         target_ref[:, lanes] = (cid[:, lanes] * CAP + place).astype(jnp.int32)
         goals.append((lower + place).astype(jnp.int32))
-    rank = (code & 65535) + 1
-    high = jnp.broadcast_to((rank >> 8).astype(jnp.float32), (META // 2, rows))
-    low = jnp.broadcast_to((rank & 255).astype(jnp.float32), (META // 2, rows))
-    both = jnp.concatenate([high, low, jnp.zeros((LANES - META, rows), jnp.float32)], axis=0)
-    unit_ref[:, width:] = jnp.transpose(both).astype(jnp.bfloat16)
+    rank = ((code & 65535) + 1).astype(jnp.float32)
+    goal = jnp.concatenate(goals, axis=1)
+    goal_column = jnp.transpose(jnp.broadcast_to(goal.astype(jnp.float32), (LANES, rows)))
+    rank_column = jnp.transpose(jnp.broadcast_to(rank, (LANES, rows)))
+    held = []
+    for j in range(rows // LANES):
+        spot = (here[:1] + j * LANES).astype(jnp.float32)
+        held.append(jnp.sum(jnp.where(goal_column == spot, rank_column, 0.0), axis=0, keepdims=True))
+    held = jnp.concatenate(held, axis=1).astype(jnp.int32)
+    high = jnp.broadcast_to((held >> 8).astype(jnp.float32), (META // 2, rows))
+    low = jnp.broadcast_to((held & 255).astype(jnp.float32), (META // 2, rows))
+    ranks = jnp.concatenate([high, low], axis=0)
     chunk = 128
     for r in range(rows // chunk):
         part = slice(r * chunk, (r + 1) * chunk)
         e = emb_ref[part, :].astype(jnp.float32)
         scale = lax.rsqrt(jnp.sum(e * e, axis=1, keepdims=True) + 1e-06)
-        unit_ref[part, :width] = (e * scale).astype(jnp.bfloat16)
+        unit_ref[part, :] = (e * scale).astype(jnp.bfloat16)
     slot = lax.broadcasted_iota(jnp.int32, (rows, rows), 0)
-    place = jnp.where(slot == jnp.concatenate(goals, axis=1), 1.0, 0.0).astype(jnp.bfloat16)
+    place = jnp.where(slot == goal, 1.0, 0.0).astype(jnp.bfloat16)
     ordered = jnp.dot(place, unit_ref[...], preferred_element_type=jnp.float32)
-    for k in range(columns + 1):
+    for k in range(columns):
         sorted_ref[k, :rows, :] = ordered[:, k * LANES : (k + 1) * LANES]
         sorted_ref[k, rows:, :] = jnp.zeros((CAP, LANES), jnp.float32)
     copy.wait()
-    me = lax.axis_index("owner") % PER_ROW
-    segment = lax.broadcasted_iota(jnp.int32, (META, LANES), 1) // CAP
-    line = lax.broadcasted_iota(jnp.int32, (CAP, LANES), 0)
-    for group in range(owners // PER_ROW):
-        ranks = []
-        for q in range(PER_ROW):
-            c = group * PER_ROW + q
-            some = pl.ds(counts_smem[0, c], CAP)
-            for k in range(columns):
-                out_ref[c, k * CAP : (k + 1) * CAP, :] = sorted_ref[k, some, :].astype(jnp.bfloat16)
-            ranks.append(jnp.where(line < counts_smem[1, c], sorted_ref[columns, some, :], 0.0))
-        tile = jnp.transpose(jnp.concatenate(ranks, axis=0))[:META, :]
-        for q in range(PER_ROW):
-            alone = jnp.where(segment == q, tile, 0.0)
-            moved = pltpu.roll(alone, (me + PER_ROW - q) % PER_ROW * CAP, 1)
-            out_ref[group * PER_ROW + q, columns * CAP :, :] = moved.astype(jnp.bfloat16)
+    first = lax.axis_index("owner") % PER_ROW * CAP
+    lane = lax.broadcasted_iota(jnp.int32, (META, LANES), 1) - first
+    for c in range(owners):
+        start, count = counts_smem[0, c], counts_smem[1, c]
+        for k in range(columns):
+            out_ref[c, k * CAP : (k + 1) * CAP, :] = sorted_ref[k, pl.ds(start, CAP), :].astype(jnp.bfloat16)
+        moved = pltpu.roll(ranks, (first + rows - start) & (rows - 1), 1)[:, :LANES]
+        tile = jnp.where((lane >= 0) & (lane < count), moved, 0.0)
+        out_ref[c, columns * CAP :, :] = tile.astype(jnp.bfloat16)
 
 
 def pack(embeddings, code, owners):
@@ -94,8 +94,8 @@
         in_specs=[pl.BlockSpec(memory_space=pltpu.VMEM)] * 2,
         out_specs=(pl.BlockSpec(memory_space=pltpu.VMEM),) * 2,
         scratch_shapes=[
-            pltpu.VMEM((rows, width + LANES), jnp.bfloat16),
-            pltpu.VMEM((width // LANES + 1, rows + CAP, LANES), jnp.float32),
+            pltpu.VMEM((rows, width), jnp.bfloat16),
+            pltpu.VMEM((width // LANES, rows + CAP, LANES), jnp.float32),
             pltpu.VMEM((8, LANES), jnp.int32),
             pltpu.SMEM((8, LANES), jnp.int32),
             pltpu.SemaphoreType.DMA(()),

time: 96.8 us -> 96.7 us (level)
  no operation moved by 1% of the time
where the time goes in v11:
time: 96.7 us; the launch traced here: 96.5 us
  blocking collectives  78.4 us (81%)
  Pallas kernels  13.8 us (14%)
  starting transfers between devices  2.08 us (2%)
  local copies, waits for them, and re-layouts  1.52 us (2%)
    all_to_all x1, blocking collectives, shards(): lax.all_to_all(packed, 'owner', split_axis=0, concat_axis=0, tiled=True)  64.9 us
    all_to_all x1, blocking collectives, shards(): lax.all_to_all(best, ('owner', 'split'), split_axis=0, concat_axis=0, til...  13.5 us
    pallas_call x1, Pallas kernels, own_pairs(): pl.pallas_call(own_kernel, out_shape=jax.ShapeDtypeStruct((8, count), jnp...  5.3 us
    pallas_call x1, Pallas kernels, cross_pairs(): pl.pallas_call(second_kernel, out_shape=jax.ShapeDtypeStruct((2 * half //...  2.86 us
    pallas_call x1, Pallas kernels, cross_pairs(): pl.pallas_call(first_kernel, out_shape=(jax.ShapeDtypeStruct((8, half), j...  2.67 us
    pallas_call x1, Pallas kernels, pack(): pl.pallas_call(pack_kernel, out_shape=(jax.ShapeDtypeStruct((owners, widt...  2.04 us
    ppermute x1, starting transfers between devices, shards(): first = lax.ppermute(mine[:half], 'split', swap)  1.99 us
  transfers between devices with their start and end apart: 2, of which 0 were waited for; matrix products, arithmetic and copies ran while one was open for 0% of the time, Pallas kernels for 8%

profile of v11, /device:TPU:1, one launch (start us, length us, event | category | flops | bytes accessed | tf_op | source)
XLA Modules:
  0.0 96.5 jit_solution(2792019963223505120)
XLA Ops:
  0.0 0.7 multiply_add_fusion.code_ref
  0.7 0.0 copy-start
  0.7 1.2 %copy-done = bf16[512,1024]{1,0:T(8,128)(2,1)S(1)} copy-done((bf16[512,1024]{1,0:T(8,128)(2,1)S(1)}, bf16[512,1024]{1,0:T(8,128)(2,1)}, u32[]{:S(2)}) %copy-start) | copy-done | bytes 1048600
  1.9 2.0 %pack_rows.1 = (bf16[64,264,128]{2,1,0:T(8,128)(2,1)S(1)}, s32[1,512]{1,0:T(1,128)S(1)}) custom-call(bf16[512,1024]{1,0:T(8,128)(2,1)S(1)} %copy-done, s32[1,512]{1,0:T(1,128)S(1)} %multiply_add_fusion.code_ref), custom_call_target="tpu_custom_call" | custom-call | tf_op jit(solution)/shard_map/pack_rows/pallas_call | solution.py:88
  4.0 64.9 %all_to_all.16.x_ref = bf16[64,264,128]{2,1,0:T(8,128)(2,1)S(1)} all-to-all(bf16[64,264,128]{2,1,0:T(8,128)(2,1)S(1)} %get-tuple-element.13), channel_id=1, replica_groups=mesh['owner'=64,'split'=2] {'owner'}, dimensions={0} | all-to-all | bytes 8650752 | tf_op jit(solution)/shard_map/all_to_all | solution.py:344
  68.9 0.3 fusion
  69.2 2.0 %collective-permute-start = (bf16[32,264,128]{2,1,0:T(8,128)(2,1)S(1)}, bf16[32,264,128]{2,1,0:T(8,128)(2,1)S(1)}, u32[]{:S(2)}, u32[]{:S(2)}) collective-permute-start(bf16[32,264,128]{2,1,0:T(8,128)(2,1)S(1)} %get-tuple-element.18), channel_id=1, source_target_pairs={{0,1},{1,0},{2,3},{3,2},{4,5},{5,4},{6,7},{7,6},{8,9},{9,8},{10,11... | collective-permute-start | bytes 6488072 | tf_op jit(solution)/shard_map/ppermute | solution.py:347
  71.2 0.1 collective-permute-start.1
  71.3 5.3 %own_pairs.1.own_ref = f32[8,2048]{1,0:T(8,128)S(1)} custom-call(bf16[64,264,128]{2,1,0:T(8,128)(2,1)S(1)} %all_to_all.16.x_ref), custom_call_target="tpu_custom_call" | custom-call | flops 5368709120 | bytes 4194304 | tf_op jit(solution)/shard_map/own_pairs/pallas_call | solution.py:181
  76.6 0.0 collective-permute-done.y_ref
  76.6 2.7 %cross_first.1 = (f32[8,1024]{1,0:T(8,128)S(1)}, f32[8,1024]{1,0:T(8,128)S(1)}) custom-call(bf16[64,264,128]{2,1,0:T(8,128)(2,1)S(1)} %all_to_all.16.x_ref, bf16[32,264,128]{2,1,0:T(8,128)(2,1)S(1)} %collective-permute-done.y_ref), custom_call_target="tpu_custom_call" | custom-call | flops 2147483648 | bytes 4194304 | tf_op jit(solution)/shard_map/cross_first/pallas_call | solution.py:281
  79.3 0.0 collective-permute-done.1.z_ref
  79.3 2.9 %cross_second.1 = f32[128,128]{1,0:T(8,128)S(1)} custom-call(bf16[64,264,128]{2,1,0:T(8,128)(2,1)S(1)} %all_to_all.16.x_ref, bf16[32,264,128]{2,1,0:T(8,128)(2,1)S(1)} %collective-permute-done.y_ref, bf16[32,264,128]{2,1,0:T(8,128)(2,1)S(1)} %collective-permute-done.1.z_ref, f32[8,2048]{1,0:T(8,128)S(1)} %own_pairs.1.own_ref, ...), custom_call_target="tpu_custom_call" | custom-call | flops 2147483648 | bytes 4194304 | tf_op jit(solution)/shard_map/cross_second/pallas_call | solution.py:291
  82.2 13.5 %all_to_all.17 = f32[128,1,128]{2,1,0:T(1,128)S(1)} all-to-all(f32[128,1,128]{2,1,0:T(1,128)S(1)} %bitcast.7), channel_id=1, replica_groups=mesh['owner'=64,'split'=2] {'owner','split'}, dimensions={0} | all-to-all | bytes 131072 | tf_op jit(solution)/shard_map/all_to_all | solution.py:351
  95.6 0.9 pick_results.1
Async XLA Ops:
  0.7 1.2 %copy-start = (bf16[512,1024]{1,0:T(8,128)(2,1)S(1)}, bf16[512,1024]{1,0:T(8,128)(2,1)}, u32[]{:S(2)}) copy-start(bf16[512,1024]{1,0:T(8,128)(2,1)} %emb_ref.1) | copy-start | bytes 3145732
  69.2 7.4 %collective-permute-start = (bf16[32,264,128]{2,1,0:T(8,128)(2,1)S(1)}, bf16[32,264,128]{2,1,0:T(8,128)(2,1)S(1)}, u32[]{:S(2)}, u32[]{:S(2)}) collective-permute-start(bf16[32,264,128]{2,1,0:T(8,128)(2,1)S(1)} %get-tuple-element.18), channel_id=1, source_target_pairs={{0,1},{1,0},{2,3},{3,2},{4,5},{5,4},{6,7},{7,6},{8,9},{9,8},{10,11... | collective-permute-start | bytes 6488072 | tf_op jit(solution)/shard_map/ppermute | solution.py:347
  71.2 8.1 %collective-permute-start.1 = (bf16[32,264,128]{2,1,0:T(8,128)(2,1)S(1)}, bf16[32,264,128]{2,1,0:T(8,128)(2,1)S(1)}, u32[]{:S(2)}, u32[]{:S(2)}) collective-permute-start(bf16[32,264,128]{2,1,0:T(8,128)(2,1)S(1)} %get-tuple-element.17), channel_id=1, source_target_pairs={{0,1},{1,0},{2,3},{3,2},{4,5},{5,4},{6,7},{7,6},{8,9},{9,8},{10,11... | collective-permute-start | bytes 6488072 | tf_op jit(solution)/shard_map/ppermute | solution.py:348
